TPU v7x, 256 devices: a whole 4x4x8 slice. The times are simulated.
256 devices in a mesh: seq: 32 (over z_hi, x, y), fsdp: 8 (over z_lo, core).
Axes of the slice: x: 4, y: 4, z: 8 (z_hi: 2, z_lo: 4; z = z_hi * 4 + z_lo), core: 2. Of those that a mesh axis runs over, the one named last changes fastest.
Arguments:
- latent: bfloat16 [8, 8192, 3584], P('fsdp', 'seq')
- targets: bfloat16 [8, 48, 96, 1536], P('fsdp', None, 'seq')
- index_map: int32 [8, 64, 128], P('fsdp'), may hold values from 0 to 4607, as said below
- proj_in: bfloat16 [3584, 1024], P(('seq', 'fsdp')), may hold values from -0.09375 to 0.09375
- proj_out: bfloat16 [1024, 1536], P(('seq', 'fsdp')), may hold values from -0.1875 to 0.1875
Outputs:
- grad_latent: bfloat16 [8, 8192, 3584], P('fsdp', 'seq')
- grad_in: float32 [3584, 1024], P(('seq', 'fsdp'))
- grad_out: float32 [1024, 1536], P(('seq', 'fsdp'))
Inputs may be any that keep to these rules, and one draw needn't show every extreme that they name: index_map[b, i, j] = r_b(i) * 96 + c_b(j), one row function and one column function an image; c_b maps the latent columns k * 4 to (k + 1) * 4 - 1 into the target columns k * 3 to (k + 1) * 3 - 1 for every band k.
All inputs are finite; a program needn't handle non-finite values.
Results may differ from a plain program's by a relative error of at most 0.007.
Values may be sent and summed in bfloat16 or wider, within the bound.
No kernel may reach another device: no remote copies, remote signals or barrier semaphores. Data moves between devices by JAX's collectives and lax.ppermute only.
A program may use at most 128 MiB of HBM per device.

v0:
```python
import jax
import jax.numpy as jnp
from jax import lax
from jax.sharding import PartitionSpec as P

loss_scale = 256.0
eps_norm = 1e-06


def silu_slope(pre):
    sig = jax.nn.sigmoid(pre)
    return sig * (1.0 + pre * (1.0 - sig))


def per_device(latent, targets, index_map, proj_in, proj_out):
    seq_count = lax.axis_size("seq")
    fsdp_count = lax.axis_size("fsdp")
    seq_place = lax.axis_index("seq")
    maps = index_map[0]
    height, width = maps.shape
    slab = targets[0]
    tgt_rows, tgt_cols, depth = slab.shape
    tgt_width = tgt_cols * seq_count
    band = width // seq_count
    local = lax.dynamic_slice_in_dim(maps, seq_place * band, band, 1)
    picks = local // tgt_width * tgt_cols + local % tgt_width - seq_place * tgt_cols
    flat_slab = slab.reshape(tgt_rows * tgt_cols, depth)
    sent = jnp.take(flat_slab, picks.reshape(-1), axis=0).reshape(height, band, depth)
    goal = lax.all_to_all(sent, "seq", split_axis=0, concat_axis=1, tiled=True)
    goal = goal.reshape(-1, depth).astype(jnp.float32)
    whole_in, whole_out = (
        lax.all_gather(proj_in, ("seq", "fsdp"), axis=0, tiled=True),
        lax.all_gather(proj_out, ("seq", "fsdp"), axis=0, tiled=True),
    )
    block = latent[0]
    pre = jnp.dot(block, whole_in, preferred_element_type=jnp.float32)
    hidden = jax.nn.silu(pre).astype(jnp.bfloat16)
    pred = jnp.dot(hidden, whole_out, preferred_element_type=jnp.float32)
    norm_pred = jnp.sqrt(jnp.sum(pred * pred, axis=1, keepdims=True) + eps_norm)
    norm_goal = jnp.sqrt(jnp.sum(goal * goal, axis=1, keepdims=True) + eps_norm)
    cosv = jnp.sum(pred * goal, axis=1, keepdims=True) / (norm_pred * norm_goal)
    grad_pred = (
        -loss_scale * (goal / (norm_pred * norm_goal) - cosv * pred / (norm_pred * norm_pred))
    ).astype(jnp.bfloat16)
    part_out = lax.dot_general(
        hidden, grad_pred, (((0,), (0,)), ((), ())), preferred_element_type=jnp.float32
    )
    grad_hidden = lax.dot_general(
        grad_pred, whole_out, (((1,), (1,)), ((), ())), preferred_element_type=jnp.float32
    )
    grad_pre = (grad_hidden * silu_slope(pre)).astype(jnp.bfloat16)
    part_in = lax.dot_general(
        block, grad_pre, (((0,), (0,)), ((), ())), preferred_element_type=jnp.float32
    )
    grad_block = lax.dot_general(
        grad_pre, whole_in, (((1,), (1,)), ((), ())), preferred_element_type=jnp.float32
    )
    grad_latent = grad_block.astype(jnp.bfloat16)[None]
    rounded_in = part_in.astype(jnp.bfloat16)
    rounded_out = part_out.astype(jnp.bfloat16)
    in_rows = part_in.shape[0] // (seq_count * fsdp_count)
    out_rows = part_out.shape[0] // (seq_count * fsdp_count)
    sectioned_in = rounded_in.astype(jnp.float32).reshape(
        seq_count, fsdp_count, in_rows, part_in.shape[1]
    )
    sectioned_out = rounded_out.astype(jnp.float32).reshape(
        seq_count, fsdp_count, out_rows, part_out.shape[1]
    )
    image_in, image_out = (
        lax.psum_scatter(sectioned_in, "fsdp", scatter_dimension=1, tiled=True),
        lax.psum_scatter(sectioned_out, "fsdp", scatter_dimension=1, tiled=True),
    )
    final_in, final_out = (
        lax.psum_scatter(image_in, "seq", scatter_dimension=0, tiled=True),
        lax.psum_scatter(image_out, "seq", scatter_dimension=0, tiled=True),
    )
    grad_in = final_in.reshape(in_rows, part_in.shape[1])
    grad_out = final_out.reshape(out_rows, part_out.shape[1])
    return (grad_latent, grad_in, grad_out)


def solution(mesh):
    placed = (
        P("fsdp", "seq", None),
        P("fsdp", None, "seq", None),
        P("fsdp", None, None),
        P(("seq", "fsdp"), None),
        P(("seq", "fsdp"), None),
    )
    return jax.shard_map(
        per_device,
        mesh=mesh,
        in_specs=placed,
        out_specs=(P("fsdp", "seq", None), P(("seq", "fsdp"), None), P(("seq", "fsdp"), None)),
        check_vma=False,
    )
```

profile of v0, /device:TPU:1, one launch (start us, length us, event | category | flops | bytes accessed | tf_op | source)
XLA Modules:
  0.0 1554.3 jit_solution(15536569637738160352)
XLA Ops:
  7.2 0.0 copy-start
  7.2 0.0 all-gather.7.cloned.1.call-start
  7.2 0.7 all-gather.7.cloned.1.call-update
  7.9 0.0 all-gather.5.cloned.1.call-start
  8.0 0.7 all-gather.5.cloned.1.call-update
  8.7 0.0 reduce-scatter.6.cloned.1.call-start
  8.7 0.9 compare_and_fusion
  9.6 0.1 ne.74
  9.7 0.1 div.54
  9.8 0.1 rem.41
  9.9 1.4 copy.24
  11.3 0.4 reshape_squeeze.3
  11.8 1.3 gather_fusion
  13.0 0.2 gather.7
  13.2 0.4 broadcast_select_fusion
  13.6 31.3 %all_to_all.4 = bf16[64,4,1536]{2,1,0:T(4,128)(2,1)S(1)} all-to-all(bf16[64,4,1536]{2,1,0:T(4,128)(2,1)S(1)} %broadcast_select_fusion), channel_id=1, replica_groups=mesh['seq'=32,'fsdp'=8] {'seq'}, dimensions={0} | all-to-all | bytes 1572864 | tf_op jit(solution)/shard_map/all_to_all | solution.py:29
  44.9 0.5 multiply_reduce_fusion.1
  45.4 0.1 sqrt.30
  45.6 0.1 convert_element_type.55
  45.7 0.1 copy.25
  45.8 1.7 reshape.177
  47.5 382.3 %all-gather.7.cloned.1.call-done = bf16[256,4,1536]{2,1,0:T(4,128)(2,1)} async-done(((bf16[1,4,1536]{2,1,0:T(4,128)(2,1)}), bf16[256,4,1536]{2,1,0:T(4,128)(2,1)}) %all-gather.7.cloned.1.call-update) | async-done | bytes 3145744 | tf_op jit(solution)/shard_map/all_gather | solution.py:33
  429.8 5.9 reshape.198
  435.7 421.3 %all-gather.5.cloned.1.call-done = bf16[256,14,1024]{2,1,0:T(8,128)(2,1)} async-done(((bf16[1,14,1024]{2,1,0:T(8,128)(2,1)}), bf16[256,14,1024]{2,1,0:T(8,128)(2,1)}) %all-gather.5.cloned.1.call-update) | async-done | bytes 7340048 | tf_op jit(solution)/shard_map/all_gather | solution.py:32
  857.0 11.3 reshape.196
  868.3 0.0 copy-done
  868.3 0.0 copy-start.2
  868.3 0.0 copy-start.3
  868.3 5.3 fusion.3
  873.6 0.0 copy-done.2
  873.6 0.0 copy-done.3
  873.6 0.0 copy-start.8
  873.6 1.2 multiply_reduce_fusion
  874.8 0.0 copy-done.8
  874.8 1.1 copy-done.7
  875.9 4.0 fusion.1
  880.0 7.6 reshape.183
  887.6 9.0 copy.29
  896.6 0.0 reduce-scatter.6.cloned.1.call-update
  896.6 0.3 reduce-scatter.4.cloned.1.call-start
  896.9 3.8 fusion.5
  900.7 0.0 copy-start.4
  900.7 0.8 copy-done.4
  901.5 7.6 convert_bitcast_fusion
  909.0 15.4 copy.27
  924.4 16.2 %reshape.181 = f32[32,8,14,1024]{3,2,1,0:T(8,128)} reshape(f32[3584,1024]{1,0:T(8,128)} %copy.27) | data formatting | bytes 29360128 | tf_op jit(solution)/shard_map/reshape | solution.py:63
  940.6 20.0 %copy.28 = f32[32,8,14,1024]{3,0,2,1:T(8,128)} copy(f32[32,8,14,1024]{3,2,1,0:T(8,128)} %reshape.181) | data formatting | bytes 29360128 | tf_op jit(solution)/shard_map/reshape | solution.py:63
  960.5 0.0 reduce-scatter.4.cloned.1.call-update
  960.6 0.0 copy-start.6
  960.6 0.0 copy-start.5
  960.6 0.3 all-reduce.5.cloned.1.call-start
  960.9 6.7 reduce-scatter.6.cloned.1.call-done
  967.6 2.5 copy.30
  970.1 152.8 %reduce-scatter.4.cloned.1.call-done = f32[32,1,14,1024]{3,0,2,1:T(8,128)} async-done(((f32[32,8,14,1024]{3,0,2,1:T(8,128)}), f32[32,1,14,1024]{3,0,2,1:T(8,128)}) %reduce-scatter.4.cloned.1.call-update) | async-done | bytes 1835024 | tf_op jit(solution)/shard_map/reduce_scatter | solution.py:70
  1122.9 0.0 all-reduce.5.cloned.1.call-update
  1123.0 0.0 copy-done.6
  1123.0 0.6 dynamic-slice.1
  1123.6 0.0 copy-done.5
  1123.6 6.5 fusion
  1130.1 413.3 %all-reduce.5.cloned.1.call-done = (f32[32,1,14,1024]{3,0,2,1:T(8,128)}, f32[32,1,4,1536]{3,2,1,0:T(4,128)}) async-done(((f32[32,1,14,1024]{3,0,2,1:T(8,128)}, f32[32,1,4,1536]{3,2,1,0:T(4,128)}), (f32[32,1,14,1024]{3,0,2,1:T(8,128)}, f32[32,1,4,1536]{3,2,1,0:T(4,128)})) %all-reduce.5.cloned.1.call-update) | async-done | bytes 2621456
  1543.4 1.7 constant_dynamic-slice_fusion
  1545.1 2.0 dynamic-slice_bitcast_fusion
  1547.1 0.6 copy.35
  1547.8 0.0 copy-done.1
  (7 shorter events, 0.1 us)
Async XLA Ops:
  7.2 861.1 %copy-start = (bf16[1,256,3584]{2,1,0:T(8,128)(2,1)S(1)}, bf16[1,256,3584]{2,1,0:T(8,128)(2,1)}, u32[]{:S(2)}) copy-start(bf16[1,256,3584]{2,1,0:T(8,128)(2,1)} %param.5) | copy-start | bytes 5505028
  7.2 422.6 %all-gather.7.cloned.1.call-start = ((), (), s32[]{:S(2)}) async-start(), calls=%async_computation.6 | async-start | bytes 3158016 | tf_op jit(solution)/shard_map/all_gather | solution.py:33
  7.9 849.1 %all-gather.5.cloned.1.call-start = ((), (), s32[]{:S(2)}) async-start(), calls=%async_computation.5 | async-start | bytes 8421376 | tf_op jit(solution)/shard_map/all_gather | solution.py:32
  8.7 958.9 %reduce-scatter.6.cloned.1.call-start = ((), (), s32[]{:S(2)}) async-start(), calls=%async_computation.4 | async-start | bytes 7077888 | tf_op jit(solution)/shard_map/reduce_scatter | solution.py:71
  868.3 5.3 copy-start.2
  868.3 5.3 copy-start.3
  873.6 1.2 copy-start.8
  874.8 1.1 copy-start.7
  896.6 226.3 %reduce-scatter.4.cloned.1.call-start = ((), (), s32[]{:S(2)}) async-start(), calls=%async_computation.3 | async-start | bytes 16515072 | tf_op jit(solution)/shard_map/reduce_scatter | solution.py:70
  900.7 0.8 copy-start.4
  960.6 162.4 %copy-start.6 = (u32[256]{0:T(256)S(1)}, u32[256]{0:T(256)}, u32[]{:S(2)}) copy-start(u32[256]{0:T(256)} %constant.67) | copy-start | bytes 3076
  960.6 163.0 %copy-start.5 = (bf16[256,1024]{1,0:T(8,128)(2,1)S(1)}, bf16[256,1024]{1,0:T(8,128)(2,1)}, u32[]{:S(2)}) copy-start(bf16[256,1024]{1,0:T(8,128)(2,1)} %copy-done.4) | copy-start | bytes 1572868
  960.6 582.8 %all-reduce.5.cloned.1.call-start = ((), (), s32[]{:S(2)}) async-start(), calls=%async_computation.7 | async-start | bytes 5242880
  1123.6 424.2 %copy-start.1 = (bf16[1,256,3584]{2,1,0:T(8,128)(2,1)S(1)}, bf16[1,256,3584]{2,1,0:T(8,128)(2,1)}, u32[]{:S(2)}) copy-start(bf16[1,256,3584]{2,1,0:T(8,128)(2,1)} %param.5) | copy-start | bytes 5505028
Sparse Core Ops, SparseCore 0:
  9.9 419.8 all-gather.6
  431.7 425.2 all-gather.4
  896.8 70.7 reduce-scatter.5
  970.0 152.8 reduce-scatter.3
  1125.5 417.8 all-reduce.4
where the time goes:
time: 1580 us; the launch traced here: 1550 us
  waiting for transfers between devices  1380 us (87%)
  local copies, waits for them, and re-layouts  100 us (6%)
  blocking collectives  31.3 us (2%)
  matrix products  28.4 us (2%)
    all_gather x1, waiting for transfers between devices, per_device(): lax.all_gather(proj_in, ('seq', 'fsdp'), axis=0, tiled=True)  421 us
    unnamed x6, waiting for transfers between devices  415 us
    all_gather x1, waiting for transfers between devices, per_device(): lax.all_gather(proj_out, ('seq', 'fsdp'), axis=0, tiled=True)  382 us
    reduce_scatter x1, waiting for transfers between devices, per_device(): lax.psum_scatter(sectioned_in, 'fsdp', scatter_dimension=1, tiled=True)  153 us
    reshape x3, local copies, waits for them, and re-layouts, per_device(): rounded_in.astype(jnp.float32)  51.5 us
  transfers between devices with their start and end apart: 5, of which 5 were waited for; matrix products, arithmetic and copies ran while one was open for 6% of the time, Pallas kernels for 0%

commit v1 on v0

v1 whole, which is shorter than its diff:
```python
import jax
import jax.numpy as jnp
import numpy as np
from jax import lax
from jax.experimental import pallas as pl
from jax.experimental.pallas import tpu as pltpu
from jax.sharding import Mesh, PartitionSpec as P

loss_scale = 256.0
eps_norm = 1e-06

AXES = ("zh", "x", "y", "zl", "c")
SIZES = (2, 4, 4, 4, 2)
D, PH, DT, TOK = 3584, 1024, 1536, 256
HH, HO = PH // 2, DT // 2
ROWS_IN, ROWS_OUT = 112, 32
PACK = 320
bf16, f32 = jnp.bfloat16, jnp.float32
NT = (((1,), (1,)), ((), ()))
TN = (((0,), (0,)), ((), ()))


def permute(v, move):
    pairs = []
    for i in range(256):
        here = [int(a) for a in np.unravel_index(i, SIZES)]
        there = [a % s for a, s in zip(move(*here), SIZES)]
        pairs.append((i, int(np.ravel_multi_index(there, SIZES))))
    return lax.ppermute(v, AXES, pairs)


def first_axis(v, d):
    return permute(
        v, lambda zh, x, y, zl, c: (zh, x + d * (c == 0), y + d * (c == 1), zl, c)
    )


def second_axis(v, d):
    return permute(
        v, lambda zh, x, y, zl, c: (zh, x + d * (c == 1), y + d * (c == 0), zl, c)
    )


def swap_cores(v):
    return permute(v, lambda zh, x, y, zl, c: (zh, x, y, zl, 1 - c))


def place_of(core, x, y, d3, d2):
    sx = lax.rem(x + jnp.where(core == 0, d2, d3), 4)
    sy = lax.rem(y + jnp.where(core == 0, d3, d2), 4)
    return sx, sy


SHIFTS = (0, 1, 3, 2)


def head_kernel(
    place,
    latent,
    picked,
    expand,
    *refs,
):
    own, oth = refs[0:4], refs[4:8]
    grad_pre_ref, grad_pred_ref, out_own, out_oth, w_in_out = refs[8:13]
    w_in, w_out, pre, hidden, pred, gpred, sems = refs[13:]
    x, y, c = place[0], place[1], place[2]

    def copies(half_refs, core, which):
        made = []
        for k, d3 in enumerate(SHIFTS):
            for j, d2 in enumerate(SHIFTS):
                sx, sy = place_of(core, x, y, 4 - d3, 4 - d2)
                src = half_refs[k].at[j]
                if which == "in":
                    for zh in range(2):
                        made.append(
                            pltpu.make_async_copy(
                                src.at[pl.ds(zh * ROWS_IN, ROWS_IN)],
                                w_in.at[
                                    zh * 16 + sx * 4 + sy,
                                    :,
                                    pl.ds(pl.multiple_of(core * HH, HH), HH),
                                ],
                                sems.at[0],
                            )
                        )
                else:
                    for zh in range(2):
                        rows = pl.ds(
                            pl.multiple_of((zh * 16 + sx * 4 + sy) * ROWS_OUT, ROWS_OUT),
                            ROWS_OUT,
                        )
                        made.append(
                            pltpu.make_async_copy(
                                src.at[pl.ds(224 + zh * 32, 32)],
                                w_out.at[
                                    rows, pl.ds(pl.multiple_of(core * HO, 256), 512)
                                ],
                                sems.at[1],
                            )
                        )
                        made.append(
                            pltpu.make_async_copy(
                                src.at[pl.ds(288, 32), pl.ds(zh * 256, 256)],
                                w_out.at[
                                    rows,
                                    pl.ds(pl.multiple_of(core * HO + 512, 256), 256),
                                ],
                                sems.at[1],
                            )
                        )
        return made

    first = copies(own, c, "in") + copies(oth, 1 - c, "in")
    second = copies(own, c, "out") + copies(oth, 1 - c, "out")
    for one in first:
        one.start()
    for one in second:
        one.start()
    goal = jnp.dot(expand[...], picked[...], preferred_element_type=f32)
    norm_goal = jnp.sqrt(jnp.sum(goal * goal, axis=1, keepdims=True) + eps_norm)
    pltpu.make_async_copy(w_in, w_in, sems.at[0]).wait()
    keep = pltpu.make_async_copy(w_in, w_in_out, sems.at[2])
    keep.start()
    lat = latent[...]
    for j in range(4):
        cols = slice(j * 256, (j + 1) * 256)
        part = jnp.dot(
            lat,
            w_in[:, :, cols].reshape(D, 256),
            preferred_element_type=f32,
        )
        pre[:, cols] = part
        hidden[:, cols] = (part * jax.nn.sigmoid(part)).astype(bf16)
    pltpu.make_async_copy(w_out, w_out, sems.at[1]).wait()
    for j in range(6):
        cols = slice(j * 256, (j + 1) * 256)
        pred[:, cols] = jnp.dot(hidden[...], w_out[:, cols], preferred_element_type=f32)
    guess = pred[...]
    norm_pred = jnp.sqrt(jnp.sum(guess * guess, axis=1, keepdims=True) + eps_norm)
    cosv = jnp.sum(guess * goal, axis=1, keepdims=True) / (norm_pred * norm_goal)
    grad_pred = (
        -loss_scale
        * (goal / (norm_pred * norm_goal) - cosv * guess / (norm_pred * norm_pred))
    ).astype(bf16)
    gpred[...] = grad_pred
    grad_pred_ref[...] = grad_pred
    for j in range(4):
        cols = slice(j * 256, (j + 1) * 256)
        grad_hidden = lax.dot_general(
            gpred[...], w_out[cols, :], NT, preferred_element_type=f32
        )
        part = pre[:, cols]
        sig = jax.nn.sigmoid(part)
        grad_pre_ref[:, cols] = (
            grad_hidden * (sig * (1.0 + part * (1.0 - sig)))
        ).astype(bf16)
    for ref, core in ((out_oth, 1 - c), (out_own, c)):
        for j in range(3):
            grads = gpred[:, pl.ds(pl.multiple_of(core * HO + j * 256, 256), 256)]
            ref[:, j * 256 : (j + 1) * 256] = lax.dot_general(
                hidden[...], grads, TN, preferred_element_type=f32
            ).astype(bf16)
    keep.wait()


def head(place, latent, picked, expand, own, oth):
    vmem = pl.BlockSpec(memory_space=pltpu.VMEM)
    hbm = pl.BlockSpec(memory_space=pl.ANY)
    return pl.pallas_call(
        head_kernel,
        in_specs=[pl.BlockSpec(memory_space=pltpu.SMEM)] + [vmem] * 3 + [hbm] * 8,
        out_specs=[vmem, vmem, vmem, vmem, hbm],
        out_shape=[
            jax.ShapeDtypeStruct((TOK, PH), bf16),
            jax.ShapeDtypeStruct((TOK, DT), bf16),
            jax.ShapeDtypeStruct((PH, HO), bf16),
            jax.ShapeDtypeStruct((PH, HO), bf16),
            jax.ShapeDtypeStruct((32, ROWS_IN, PH), bf16),
        ],
        scratch_shapes=[
            pltpu.VMEM((32, ROWS_IN, PH), bf16),
            pltpu.VMEM((PH, DT), bf16),
            pltpu.VMEM((TOK, PH), f32),
            pltpu.VMEM((TOK, PH), bf16),
            pltpu.VMEM((TOK, DT), f32),
            pltpu.VMEM((TOK, DT), bf16),
            pltpu.SemaphoreType.DMA((3,)),
        ],
        compiler_params=pltpu.CompilerParams(vmem_limit_bytes=48 * 2**20),
        cost_estimate=pl.CostEstimate(
            flops=6_000_000_000, bytes_accessed=30_000_000, transcendentals=600_000
        ),
        name="head",
    )(place, latent, picked, expand, *own, *oth)


def part_in_kernel(place, latent, grad_pre, own, oth):
    c = place[2]
    lat = latent[...]
    for ref, core in ((oth, 1 - c), (own, c)):
        grads = grad_pre[:, pl.ds(pl.multiple_of(core * HH, HH), HH)]
        ref[...] = lax.dot_general(lat, grads, TN, preferred_element_type=f32).astype(
            bf16
        )


def part_in(place, latent, grad_pre):
    step = 512
    block = pl.BlockSpec((step, HH), lambda i: (i, 0))
    return pl.pallas_call(
        part_in_kernel,
        grid=(D // step,),
        in_specs=[
            pl.BlockSpec(memory_space=pltpu.SMEM),
            pl.BlockSpec((TOK, step), lambda i: (0, i)),
            pl.BlockSpec((TOK, PH), lambda i: (0, 0)),
        ],
        out_specs=[block, block],
        out_shape=[jax.ShapeDtypeStruct((D, HH), bf16)] * 2,
        compiler_params=pltpu.CompilerParams(vmem_limit_bytes=32 * 2**20),
        cost_estimate=pl.CostEstimate(
            flops=1_900_000_000, bytes_accessed=10_000_000, transcendentals=0
        ),
        name="part_in",
    )(place, latent, grad_pre)


def back_kernel(grad_pre, w_in, out):
    out[...] = lax.dot_general(
        grad_pre[...], w_in[...], NT, preferred_element_type=f32
    ).astype(bf16)


def back(grad_pre, w_in):
    step = 512
    return pl.pallas_call(
        back_kernel,
        grid=(D // step,),
        in_specs=[
            pl.BlockSpec((TOK, PH), lambda i: (0, 0)),
            pl.BlockSpec((step, PH), lambda i: (i, 0)),
        ],
        out_specs=pl.BlockSpec((TOK, step), lambda i: (0, i)),
        out_shape=jax.ShapeDtypeStruct((TOK, D), bf16),
        compiler_params=pltpu.CompilerParams(vmem_limit_bytes=32 * 2**20),
        cost_estimate=pl.CostEstimate(
            flops=1_900_000_000, bytes_accessed=10_000_000, transcendentals=0
        ),
        name="back",
    )(grad_pre, w_in)


def pair_kernel(place, in_own, in_rcv, out_own, out_rcv, *outs):
    d3 = pl.program_id(0)
    top = (in_own[:, 0, 0].astype(f32) + in_rcv[:, 0, 0].astype(f32)).astype(bf16)
    low = (out_own[:, 0, 0].astype(f32) + out_rcv[:, 0, 0].astype(f32)).astype(bf16)
    for k in range(4):

        @pl.when(d3 == k)
        def _(k=k):
            out = outs[k]
            out[0, 0:112] = top[0]
            out[0, 112:224] = top[1]
            out[0, 224:256] = low[0, :, 0:512]
            out[0, 256:288] = low[1, :, 0:512]
            out[0, 288:320, 0:256] = low[0, :, 512:768]
            out[0, 288:320, 256:512] = low[1, :, 512:768]


def pair_sum(place, in_own, in_rcv, out_own, out_rcv):
    def spot(i, j, place):
        sx, sy = place_of(place[2], place[0], place[1], i, j)
        return (0, sx, sy, 0, 0)

    def slot(k):
        return lambda i, j, place: (jnp.where(i == k, j, jnp.where(i < k, 0, 3)), 0, 0)

    top = pl.BlockSpec((2, 1, 1, ROWS_IN, HH), spot)
    low = pl.BlockSpec((2, 1, 1, ROWS_OUT, HO), spot)
    shape_in, shape_out = (2, 4, 4, ROWS_IN, HH), (2, 4, 4, ROWS_OUT, HO)
    return pl.pallas_call(
        pair_kernel,
        grid_spec=pltpu.PrefetchScalarGridSpec(
            num_scalar_prefetch=1,
            grid=(4, 4),
            in_specs=[top, top, low, low],
            out_specs=[pl.BlockSpec((1, PACK, HH), slot(k)) for k in range(4)],
        ),
        out_shape=[jax.ShapeDtypeStruct((4, PACK, HH), bf16)] * 4,
        compiler_params=pltpu.CompilerParams(vmem_limit_bytes=32 * 2**20),
        cost_estimate=pl.CostEstimate(
            flops=6_000_000, bytes_accessed=16_000_000, transcendentals=0
        ),
        name="pair_sum",
    )(
        place,
        in_own.reshape(shape_in),
        in_rcv.reshape(shape_in),
        out_own.reshape(shape_out),
        out_rcv.reshape(shape_out),
    )


def add4(a, b, c, d):
    return (
        (a.astype(f32) + b.astype(f32)) + (c.astype(f32) + d.astype(f32))
    ).astype(bf16)


def per_device(latent, targets, index_map, proj_in, proj_out):
    x, y, c = lax.axis_index("x"), lax.axis_index("y"), lax.axis_index("c")
    place = jnp.stack([x, y, c]).astype(jnp.int32)

    halves = jnp.concatenate(
        [
            proj_in.reshape(14, 2, HH).transpose(1, 0, 2),
            proj_out.reshape(4, 2, HO).transpose(1, 0, 2).reshape(2, 6, HH),
        ],
        axis=1,
    )
    fan = jnp.broadcast_to(halves[None], (8, 2, 20, HH)).reshape(16, 20, HH)
    column = lax.all_to_all(
        fan, ("zh", "zl", "c"), split_axis=0, concat_axis=0, tiled=True
    )
    rows_in = column[:, :14].reshape(224, HH)
    rows_out = column[:, 14:].reshape(16, 4, HO).reshape(2, ROWS_OUT, HO)
    packed = jnp.concatenate(
        [
            rows_in,
            rows_out[:, :, :512].reshape(64, 512),
            rows_out[:, :, 512:].transpose(1, 0, 2).reshape(32, 512),
        ],
        axis=0,
    )
    line = jnp.stack([packed] + [first_axis(packed, d) for d in SHIFTS[1:]])
    own = [line] + [second_axis(line, d) for d in SHIFTS[1:]]
    oth = [swap_cores(v) for v in own]

    maps = index_map[0]
    width = targets.shape[2] * 32
    row_of = maps[:, 0] // width
    slab = targets[0].transpose(1, 0, 2)
    pick = (row_of[:, None] == jnp.arange(48, dtype=jnp.int32)[None]).astype(bf16)
    sent = jnp.stack(
        [jnp.dot(pick, slab[t], preferred_element_type=f32).astype(bf16) for t in range(3)]
    )
    sent, _ = lax.optimization_barrier((sent, line))
    got = lax.all_to_all(
        sent.reshape(3, 32, 2, DT).transpose(1, 0, 2, 3).reshape(32, 6, DT),
        ("zh", "x", "y"), split_axis=0, concat_axis=0, tiled=True,
    )
    picked = got.reshape(192, DT)
    col_of = (maps[0] % width).reshape(32, 4) - 3 * jnp.arange(32, dtype=jnp.int32)[:, None]
    token = jnp.arange(TOK, dtype=jnp.int32)[:, None]
    row = jnp.arange(192, dtype=jnp.int32)[None]
    want = ((token // 4) % 32) * 6 + jnp.tile(col_of.reshape(128), 2)[:, None] * 2 + token // 128
    expand = (row == want).astype(bf16)

    block = latent[0]
    grad_pre, grad_pred, out_own, out_oth, w_in = head(
        place, block, picked, expand, own, oth
    )
    in_own, in_oth = part_in(place, block, grad_pre)
    out_rcv = swap_cores(out_oth)
    in_rcv = swap_cores(in_oth)
    sums = pair_sum(place, in_own, in_rcv, out_own, out_rcv)
    got3 = [second_axis(sums[d], d) for d in SHIFTS[1:]]
    grad_latent = back(grad_pre, w_in.reshape(D, PH))
    line_sum = [add4(sums[0][k], got3[0][k], got3[1][k], got3[2][k]) for k in range(4)]
    got2 = [first_axis(line_sum[d], d) for d in SHIFTS[1:]]
    mine = add4(line_sum[0], *got2)
    g_in = mine[:224].reshape(16, 14, HH)
    g_out = jnp.concatenate(
        [
            mine[224:288].reshape(2, 32, 512),
            mine[288:].reshape(32, 2, 256).transpose(1, 0, 2),
        ],
        axis=2,
    ).reshape(16, 4, HO).reshape(16, 6, HH)
    last = lax.all_to_all(
        jnp.concatenate([g_in, g_out], axis=1),
        ("zh", "zl", "c"), split_axis=0, concat_axis=0, tiled=True,
    )
    total = jnp.sum(last.reshape(8, 2, 20, HH).astype(f32), axis=0)
    grad_in = total[:, :14].transpose(1, 0, 2).reshape(14, PH)
    grad_out = total[:, 14:].reshape(2, 4, HO).transpose(1, 0, 2).reshape(4, DT)
    return grad_latent[None], grad_in, grad_out


def solution(mesh):
    fine = Mesh(mesh.devices.reshape(SIZES), AXES)
    seq, fsdp = ("zh", "x", "y"), ("zl", "c")
    rows = P(AXES, None)
    return jax.shard_map(
        per_device,
        mesh=fine,
        in_specs=(P(fsdp, seq, None), P(fsdp, None, seq, None), P(fsdp, None, None), rows, rows),
        out_specs=(P(fsdp, seq, None), rows, rows),
        check_vma=False,
    )
```

time: 1580 us -> 207 us (0.13); the launches traced: 1550 us -> 206 us
  waiting for transfers between devices: 1380 us -> 102 us
  local copies, waits for them, and re-layouts: 100 us -> 8.25 us
  starting transfers between devices: 0.68 us -> 41.7 us
  matrix products: 28.4 us -> 0.74 us
  Pallas kernels: 0 us -> 25.9 us
    all_gather x2 -> x0, waiting for transfers between devices: 804 us -> none  [the longest x1 421 us: per_device(): lax.all_gather(proj_in, ('seq', 'fsdp'), axis=0, tiled=True)]
    unnamed x6 -> x0, waiting for transfers between devices: 415 us -> none
    reduce_scatter x2 -> x0, waiting for transfers between devices: 160 us -> none  [the longest x1 153 us: per_device(): lax.psum_scatter(sectioned_in, 'fsdp', scatter_dimension=1, tiled=True)]
    ppermute x0 -> x18, waiting for transfers between devices: none -> 78 us  [permute(): return lax.ppermute(v, AXES, pairs)]
    reshape x6 -> x11, local copies, waits for them, and re-layouts: 70.1 us -> 3.97 us  [the longest x3 1.5 us: per_device(): sent.reshape(3, 32, 2, DT).transpose(1, 0, 2, 3).reshape(32, 6, DT)]
    dot_general x6 -> x3, matrix products: 28.4 us -> 0.74 us  [per_device(): jnp.dot(pick, slab[t], preferred_element_type=f32).astype(bf16)]
    ppermute x0 -> x18, starting transfers between devices: none -> 27.4 us  [permute(): return lax.ppermute(v, AXES, pairs)]
    pallas_call x0 -> x4, Pallas kernels: none -> 25.9 us  [the longest x1 12 us: head(): pl.pallas_call(head_kernel, in_specs=[pl.BlockSpec(memory_space=pltpu.SME...]
  transfers between devices with their start and end apart: 5 -> 20, of which waited for: 5 -> 12; matrix products, arithmetic and copies ran while one was open for 6% -> 1% of each run, Pallas kernels for 0% -> 2%
where the time goes in v1:
time: 207 us; the launch traced here: 206 us
  waiting for transfers between devices  102 us (49%)
  starting transfers between devices  41.7 us (20%)
  Pallas kernels  25.9 us (13%)
  blocking collectives  24.3 us (12%)
  local copies, waits for them, and re-layouts  8.25 us (4%)
  other arithmetic  2.43 us (1%)
    ppermute x18, waiting for transfers between devices, permute(): return lax.ppermute(v, AXES, pairs)  78 us
    ppermute x18, starting transfers between devices, permute(): return lax.ppermute(v, AXES, pairs)  27.4 us
    all_to_all x1, blocking collectives, per_device(): lax.all_to_all(fan, ('zh', 'zl', 'c'), split_axis=0, concat_axis=0, tiled...  24.3 us
    all_to_all x1, waiting for transfers between devices, per_device(): lax.all_to_all(sent.reshape(3, 32, 2, DT).transpose(1, 0, 2, 3).reshape(3...  17 us
    pallas_call x1, Pallas kernels, head(): pl.pallas_call(head_kernel, in_specs=[pl.BlockSpec(memory_space=pltpu.SME...  12 us
    all_to_all x1, starting transfers between devices, per_device(): lax.all_to_all(jnp.concatenate([g_in, g_out], axis=1), ('zh', 'zl', 'c'),...  8.15 us
    all_to_all x1, waiting for transfers between devices, per_device(): lax.all_to_all(jnp.concatenate([g_in, g_out], axis=1), ('zh', 'zl', 'c'),...  6.77 us
    all_to_all x1, starting transfers between devices, per_device(): lax.all_to_all(sent.reshape(3, 32, 2, DT).transpose(1, 0, 2, 3).reshape(3...  6.14 us
  transfers between devices with their start and end apart: 20, of which 12 were waited for; matrix products, arithmetic and copies ran while one was open for 1% of the time, Pallas kernels for 2%

profile of v1, /device:TPU:1, one launch (start us, length us, event | category | flops | bytes accessed | tf_op | source)
XLA Modules:
  0.0 206.1 jit_solution(2398864924064365255)
XLA Ops:
  0.6 0.7 reshape.234
  1.4 0.8 reshape.233
  2.1 0.1 pad_maximum_fusion.5
  2.2 24.3 %all_to_all.15 = bf16[16,20,512]{2,1,0:T(8,128)(2,1)S(1)} all-to-all(bf16[16,20,512]{2,1,0:T(8,128)(2,1)S(1)} %bitcast.91), channel_id=1, replica_groups=mesh['zh'=2,'x'=4,'y'=4,'zl'=4,'c'=2] {'zh','zl','c'}, dimensions={0} | all-to-all | bytes 655360 | tf_op jit(solution)/shard_map/all_to_all | solution.py:324
  26.6 0.1 reshape_reshape.6
  26.7 0.1 reshape.237
  26.9 2.8 %collective-permute-start.1 = (bf16[320,512]{1,0:T(8,128)(2,1)S(1)}, bf16[320,512]{1,0:T(8,128)(2,1)S(1)}, u32[]{:S(2)}, u32[]{:S(2)}) collective-permute-start(bf16[320,512]{1,0:T(8,128)(2,1)S(1)} %get-tuple-element.29), channel_id=1, source_target_pairs={{0,96},{1,25},{2,98},{3,27},{4,100},{5,29},{6,102},{7,31},{8,104},... | collective-permute-start | bytes 983048 | tf_op jit(solution)/shard_map/ppermute | solution.py:29
  29.7 1.6 collective-permute-start.2
  31.4 5.9 %collective-permute-done.1 = bf16[320,512]{1,0:T(8,128)(2,1)S(1)} collective-permute-done((bf16[320,512]{1,0:T(8,128)(2,1)S(1)}, bf16[320,512]{1,0:T(8,128)(2,1)S(1)}, u32[]{:S(2)}, u32[]{:S(2)}) %collective-permute-start.1) | collective-permute-done | bytes 327712 | tf_op jit(solution)/shard_map/ppermute | solution.py:29
  37.2 3.1 %collective-permute-done = bf16[320,512]{1,0:T(8,128)(2,1)S(1)} collective-permute-done((bf16[320,512]{1,0:T(8,128)(2,1)S(1)}, bf16[320,512]{1,0:T(8,128)(2,1)S(1)}, u32[]{:S(2)}, u32[]{:S(2)}) %collective-permute-start) | collective-permute-done | bytes 327712 | tf_op jit(solution)/shard_map/ppermute | solution.py:29
  40.4 0.2 pad_maximum_fusion.refs_0_
  40.5 2.8 %collective-permute-start.5 = (bf16[4,320,512]{2,1,0:T(8,128)(2,1)S(1)}, bf16[4,320,512]{2,1,0:T(8,128)(2,1)}, u32[]{:S(2)}, u32[]{:S(2)}) collective-permute-start(bf16[4,320,512]{2,1,0:T(8,128)(2,1)S(1)} %pad_maximum_fusion.refs_0_), channel_id=1, source_target_pairs={{0,16},{1,65},{2,18},{3,67},{4,20},{5,69},{6,22},{7,71},{8,24},{9,... | collective-permute-start | bytes 3932168 | tf_op jit(solution)/shard_map/ppermute | solution.py:29
  43.4 0.9 collective-permute-start.4
  44.2 0.6 collective-permute-start.3
  44.8 0.1 fusion.10
  45.0 0.2 fusion.2
  45.2 0.2 fusion.1
  45.5 0.2 fusion
  45.7 1.5 collective-permute-start.6
  47.2 11.8 %collective-permute-done.5.refs_3_ = bf16[4,320,512]{2,1,0:T(8,128)(2,1)} collective-permute-done((bf16[4,320,512]{2,1,0:T(8,128)(2,1)S(1)}, bf16[4,320,512]{2,1,0:T(8,128)(2,1)}, u32[]{:S(2)}, u32[]{:S(2)}) %collective-permute-start.5) | collective-permute-done | bytes 1310752 | tf_op jit(solution)/shard_map/ppermute | solution.py:29
  59.0 1.3 collective-permute-start.9
  60.3 12.8 %collective-permute-done.4.refs_2_ = bf16[4,320,512]{2,1,0:T(8,128)(2,1)} collective-permute-done((bf16[4,320,512]{2,1,0:T(8,128)(2,1)S(1)}, bf16[4,320,512]{2,1,0:T(8,128)(2,1)}, u32[]{:S(2)}, u32[]{:S(2)}) %collective-permute-start.4) | collective-permute-done | bytes 1310752 | tf_op jit(solution)/shard_map/ppermute | solution.py:29
  73.2 1.5 collective-permute-start.8
  74.7 0.0 collective-permute-start.7
  74.7 0.1 pad_maximum_fusion.1
  74.8 0.2 reshape.240
  75.0 0.1 copy.25
  75.1 1.2 copy.26
  76.3 6.1 %all-to-all-start.1 = ((bf16[32,6,1536]{2,1,0:T(8,128)(2,1)}), bf16[32,6,1536]{2,1,0:T(8,128)(2,1)S(1)}, u32[]{:S(2)}, u32[]{:S(2)}) async-start(bf16[32,6,1536]{2,1,0:T(8,128)(2,1)} %copy.26), calls=%async_computation.1 | async-start | bytes 1572864 | tf_op jit(solution)/shard_map/all_to_all | solution.py:350
  82.4 0.1 sub.32
  82.5 0.1 sub.33
  82.6 0.1 pad_add_fusion.place
  82.7 0.1 fusion.9.expand
  82.8 17.0 %all-to-all-done.1 = bf16[32,6,1536]{2,1,0:T(8,128)(2,1)S(1)} async-done(((bf16[32,6,1536]{2,1,0:T(8,128)(2,1)}), bf16[32,6,1536]{2,1,0:T(8,128)(2,1)S(1)}, u32[]{:S(2)}, u32[]{:S(2)}) %all-to-all-start.1) | async-done | bytes 589856 | tf_op jit(solution)/shard_map/all_to_all | solution.py:350
  99.9 0.2 reshape.242.picked
  100.1 12.0 %head.1 = (bf16[256,1024]{1,0:T(8,128)(2,1)S(1)}, bf16[256,1536]{1,0:T(8,128)(2,1)}, bf16[1024,768]{1,0:T(8,128)(2,1)}, bf16[1024,768]{1,0:T(8,128)(2,1)}, bf16[32,112,1024]{2,1,0:T(8,128)(2,1)}) custom-call(s32[3]{0:T(128)S(1)} %pad_add_fusion.place, bf16[256,3584]{1,0:T(8,128)(2,1)} %bitcast.87, bf16[192,1536]{1,0:T(8,128)(2,1)S(1)} %reshape.242.picked, ...), custom_call_target="tpu_custom_call" | custom-call | flops 6000000000 | bytes 30000000 | tf_op jit(solution)/shard_map/head/pallas_call | solution.py:171
  112.1 4.0 %part_in.1 = (bf16[3584,512]{1,0:T(8,128)(2,1)S(1)}, bf16[3584,512]{1,0:T(8,128)(2,1)S(1)}) custom-call(s32[3]{0:T(128)S(1)} %pad_add_fusion.place, bf16[256,3584]{1,0:T(8,128)(2,1)S(1)} %bitcast.88, bf16[256,1024]{1,0:T(8,128)(2,1)S(1)} %get-tuple-element.15.grad_pre), custom_call_target="tpu_custom_call" | custom-call | flops 1900000000 | bytes 10000000 | tf_op jit(solution)/shard_map/part_in/pallas_call | solution.py:212
  116.1 2.5 %collective-permute-start.10 = (bf16[3584,512]{1,0:T(8,128)(2,1)S(1)}, bf16[3584,512]{1,0:T(8,128)(2,1)S(1)}, u32[]{:S(2)}, u32[]{:S(2)}) collective-permute-start(bf16[3584,512]{1,0:T(8,128)(2,1)S(1)} %get-tuple-element.18), channel_id=1, source_target_pairs={{0,1},{1,0},{2,3},{3,2},{4,5},{5,4},{6,7},{7,6},{8,9},{9,8},{10,11... | collective-permute-start | bytes 11010056 | tf_op jit(solution)/shard_map/ppermute | solution.py:29
  118.6 0.1 collective-permute-start.11
  118.7 8.2 %collective-permute-done.11 = bf16[1024,768]{1,0:T(8,128)(2,1)S(1)} collective-permute-done((bf16[1024,768]{1,0:T(8,128)(2,1)S(1)}, bf16[1024,768]{1,0:T(8,128)(2,1)S(1)}, u32[]{:S(2)}, u32[]{:S(2)}) %collective-permute-start.11) | collective-permute-done | bytes 1572896 | tf_op jit(solution)/shard_map/ppermute | solution.py:29
  126.9 5.2 %pair_sum.1 = (bf16[4,320,512]{2,1,0:T(8,128)(2,1)S(1)}, bf16[4,320,512]{2,1,0:T(8,128)(2,1)S(1)}, bf16[4,320,512]{2,1,0:T(8,128)(2,1)S(1)}, bf16[4,320,512]{2,1,0:T(8,128)(2,1)S(1)}) custom-call(s32[3]{0:T(128)S(1)} %pad_add_fusion.place, bf16[2,4,4,112,512]{4,3,2,1,0:T(8,128)(2,1)S(1)} %bitcast.83, bf16[2,4,4,112,512]{4,3,2,1,0:T(8,128)(2,1)S(1)} %bitcast.84, ...), custom_call_target="tpu_custom_call" | custom-call | flops 6000000 | bytes 16000000 | tf_op jit(solution)/shard_map/pair_sum/pallas_call | solution.py:283
  132.2 4.2 %collective-permute-start.12 = (bf16[4,320,512]{2,1,0:T(8,128)(2,1)S(1)}, bf16[4,320,512]{2,1,0:T(8,128)(2,1)S(1)}, u32[]{:S(2)}, u32[]{:S(2)}) collective-permute-start(bf16[4,320,512]{2,1,0:T(8,128)(2,1)S(1)} %get-tuple-element.22), channel_id=1, source_target_pairs={{0,8},{1,33},{2,10},{3,35},{4,12},{5,37},{6,14},{7,39},{8,16},{9,4... | collective-permute-start | bytes 3932168 | tf_op jit(solution)/shard_map/ppermute | solution.py:29
  136.4 1.3 collective-permute-start.13
  137.7 1.7 collective-permute-start.14
  139.4 13.5 %collective-permute-done.12 = bf16[4,320,512]{2,1,0:T(8,128)(2,1)S(1)} collective-permute-done((bf16[4,320,512]{2,1,0:T(8,128)(2,1)S(1)}, bf16[4,320,512]{2,1,0:T(8,128)(2,1)S(1)}, u32[]{:S(2)}, u32[]{:S(2)}) %collective-permute-start.12) | collective-permute-done | bytes 1310752 | tf_op jit(solution)/shard_map/ppermute | solution.py:29
  152.9 0.3 collective-permute-done.13
  153.2 15.0 %collective-permute-done.14 = bf16[4,320,512]{2,1,0:T(8,128)(2,1)S(1)} collective-permute-done((bf16[4,320,512]{2,1,0:T(8,128)(2,1)S(1)}, bf16[4,320,512]{2,1,0:T(8,128)(2,1)S(1)}, u32[]{:S(2)}, u32[]{:S(2)}) %collective-permute-start.14) | collective-permute-done | bytes 1310752 | tf_op jit(solution)/shard_map/ppermute | solution.py:29
  168.1 0.6 fusion.6
  168.7 1.0 collective-permute-start.15
  169.7 2.7 %collective-permute-start.17 = (bf16[320,512]{1,0:T(8,128)(2,1)S(1)}, bf16[320,512]{1,0:T(8,128)(2,1)S(1)}, u32[]{:S(2)}, u32[]{:S(2)}) collective-permute-start(bf16[320,512]{1,0:T(8,128)(2,1)S(1)} %get-tuple-element.26), channel_id=1, source_target_pairs={{0,64},{1,17},{2,66},{3,19},{4,68},{5,21},{6,70},{7,23},{8,72},{9,... | collective-permute-start | bytes 983048 | tf_op jit(solution)/shard_map/ppermute | solution.py:29
  172.3 0.9 collective-permute-start.16
  173.2 3.0 %collective-permute-done.15 = bf16[320,512]{1,0:T(8,128)(2,1)S(1)} collective-permute-done((bf16[320,512]{1,0:T(8,128)(2,1)S(1)}, bf16[320,512]{1,0:T(8,128)(2,1)S(1)}, u32[]{:S(2)}, u32[]{:S(2)}) %collective-permute-start.15) | collective-permute-done | bytes 327712 | tf_op jit(solution)/shard_map/ppermute | solution.py:29
  176.2 4.4 %collective-permute-done.17 = bf16[320,512]{1,0:T(8,128)(2,1)S(1)} collective-permute-done((bf16[320,512]{1,0:T(8,128)(2,1)S(1)}, bf16[320,512]{1,0:T(8,128)(2,1)S(1)}, u32[]{:S(2)}, u32[]{:S(2)}) %collective-permute-start.17) | collective-permute-done | bytes 327712 | tf_op jit(solution)/shard_map/ppermute | solution.py:29
  180.6 0.3 fusion.4
  181.0 0.1 reshape_reshape.7
  181.1 0.1 reshape.248
  181.1 0.8 pad_maximum_fusion.2
  182.0 8.2 %all-to-all-start.2 = ((bf16[16,20,512]{2,1,0:T(8,128)(2,1)}), bf16[16,20,512]{2,1,0:T(8,128)(2,1)S(1)}, u32[]{:S(2)}, u32[]{:S(2)}) async-start(bf16[16,20,512]{2,1,0:T(8,128)(2,1)} %pad_maximum_fusion.2), calls=%async_computation.2 | async-start | bytes 786432 | tf_op jit(solution)/shard_map/all_to_all | solution.py:382
  190.1 3.1 %copy-done = bf16[32,112,1024]{2,1,0:T(8,128)(2,1)S(1)} copy-done((bf16[32,112,1024]{2,1,0:T(8,128)(2,1)S(1)}, bf16[32,112,1024]{2,1,0:T(8,128)(2,1)}, u32[]{:S(2)}) %copy-start) | copy-done | bytes 7340056
  193.2 4.7 %back.1 = bf16[256,3584]{1,0:T(8,128)(2,1)} custom-call(bf16[256,1024]{1,0:T(8,128)(2,1)S(1)} %get-tuple-element.15.grad_pre, bf16[3584,1024]{1,0:T(8,128)(2,1)S(1)} %bitcast.82), custom_call_target="tpu_custom_call" | custom-call | flops 1900000000 | bytes 10000000 | tf_op jit(solution)/shard_map/back/pallas_call | solution.py:238
  197.9 6.8 %all-to-all-done.2 = bf16[16,20,512]{2,1,0:T(8,128)(2,1)S(1)} async-done(((bf16[16,20,512]{2,1,0:T(8,128)(2,1)}), bf16[16,20,512]{2,1,0:T(8,128)(2,1)S(1)}, u32[]{:S(2)}, u32[]{:S(2)}) %all-to-all-start.2) | async-done | bytes 327712 | tf_op jit(solution)/shard_map/all_to_all | solution.py:382
  204.7 0.1 convert_reduce_fusion
  204.8 0.6 reshape.252
  205.5 0.6 copy.31
  (40 shorter events, 0.4 us)
Async XLA Ops:
  26.9 10.3 %collective-permute-start.1 = (bf16[320,512]{1,0:T(8,128)(2,1)S(1)}, bf16[320,512]{1,0:T(8,128)(2,1)S(1)}, u32[]{:S(2)}, u32[]{:S(2)}) collective-permute-start(bf16[320,512]{1,0:T(8,128)(2,1)S(1)} %get-tuple-element.29), channel_id=1, source_target_pairs={{0,96},{1,25},{2,98},{3,27},{4,100},{5,29},{6,102},{7,31},{8,104},... | collective-permute-start | bytes 983048 | tf_op jit(solution)/shard_map/ppermute | solution.py:29
  29.7 10.7 %collective-permute-start = (bf16[320,512]{1,0:T(8,128)(2,1)S(1)}, bf16[320,512]{1,0:T(8,128)(2,1)S(1)}, u32[]{:S(2)}, u32[]{:S(2)}) collective-permute-start(bf16[320,512]{1,0:T(8,128)(2,1)S(1)} %get-tuple-element.29), channel_id=1, source_target_pairs={{0,32},{1,9},{2,34},{3,11},{4,36},{5,13},{6,38},{7,15},{8,40},{9,1... | collective-permute-start | bytes 983048 | tf_op jit(solution)/shard_map/ppermute | solution.py:29
  29.7 10.7 %collective-permute-start.2 = (bf16[320,512]{1,0:T(8,128)(2,1)S(1)}, bf16[320,512]{1,0:T(8,128)(2,1)S(1)}, u32[]{:S(2)}, u32[]{:S(2)}) collective-permute-start(bf16[320,512]{1,0:T(8,128)(2,1)S(1)} %get-tuple-element.29), channel_id=1, source_target_pairs={{0,64},{1,17},{2,66},{3,19},{4,68},{5,21},{6,70},{7,23},{8,72},{9,... | collective-permute-start | bytes 983048 | tf_op jit(solution)/shard_map/ppermute | solution.py:29
  40.4 4.5 %copy-start.4 = (s32[1,64,128]{2,1,0:T(8,128)S(1)}, s32[1,64,128]{2,1,0:T(8,128)}, u32[]{:S(2)}) copy-start(s32[1,64,128]{2,1,0:T(8,128)} %param.7) | copy-start | bytes 98308
  40.4 4.6 %copy-start.3 = (bf16[1,48,3,1536]{3,1,2,0:T(8,128)(2,1)S(1)}, bf16[1,48,3,1536]{3,1,2,0:T(8,128)(2,1)}, u32[]{:S(2)}) copy-start(bf16[1,48,3,1536]{3,1,2,0:T(8,128)(2,1)} %param.6) | copy-start | bytes 1327108
  40.5 18.5 %collective-permute-start.5 = (bf16[4,320,512]{2,1,0:T(8,128)(2,1)S(1)}, bf16[4,320,512]{2,1,0:T(8,128)(2,1)}, u32[]{:S(2)}, u32[]{:S(2)}) collective-permute-start(bf16[4,320,512]{2,1,0:T(8,128)(2,1)S(1)} %pad_maximum_fusion.refs_0_), channel_id=1, source_target_pairs={{0,16},{1,65},{2,18},{3,67},{4,20},{5,69},{6,22},{7,71},{8,24},{9,... | collective-permute-start | bytes 3932168 | tf_op jit(solution)/shard_map/ppermute | solution.py:29
  43.4 29.8 %collective-permute-start.4 = (bf16[4,320,512]{2,1,0:T(8,128)(2,1)S(1)}, bf16[4,320,512]{2,1,0:T(8,128)(2,1)}, u32[]{:S(2)}, u32[]{:S(2)}) collective-permute-start(bf16[4,320,512]{2,1,0:T(8,128)(2,1)S(1)} %pad_maximum_fusion.refs_0_), channel_id=1, source_target_pairs={{0,24},{1,97},{2,26},{3,99},{4,28},{5,101},{6,30},{7,103},{8,0},{9... | collective-permute-start | bytes 3932168 | tf_op jit(solution)/shard_map/ppermute | solution.py:29
  44.2 30.5 %collective-permute-start.3 = (bf16[4,320,512]{2,1,0:T(8,128)(2,1)S(1)}, bf16[4,320,512]{2,1,0:T(8,128)(2,1)}, u32[]{:S(2)}, u32[]{:S(2)}) collective-permute-start(bf16[4,320,512]{2,1,0:T(8,128)(2,1)S(1)} %pad_maximum_fusion.refs_0_), channel_id=1, source_target_pairs={{0,8},{1,33},{2,10},{3,35},{4,12},{5,37},{6,14},{7,39},{8,16},{9,4... | collective-permute-start | bytes 3932168 | tf_op jit(solution)/shard_map/ppermute | solution.py:29
  45.7 54.3 %collective-permute-start.6 = (bf16[4,320,512]{2,1,0:T(8,128)(2,1)S(1)}, bf16[4,320,512]{2,1,0:T(8,128)(2,1)}, u32[]{:S(2)}, u32[]{:S(2)}) collective-permute-start(bf16[4,320,512]{2,1,0:T(8,128)(2,1)S(1)} %pad_maximum_fusion.refs_0_), channel_id=1, source_target_pairs={{0,1},{1,0},{2,3},{3,2},{4,5},{5,4},{6,7},{7,6},{8,9},{9,8},{10,11... | collective-permute-start | bytes 3932168 | tf_op jit(solution)/shard_map/ppermute | solution.py:29
  59.0 41.0 %collective-permute-start.9 = (bf16[4,320,512]{2,1,0:T(8,128)(2,1)}, bf16[4,320,512]{2,1,0:T(8,128)(2,1)}, u32[]{:S(2)}, u32[]{:S(2)}) collective-permute-start(bf16[4,320,512]{2,1,0:T(8,128)(2,1)} %collective-permute-done.5.refs_3_), channel_id=1, source_target_pairs={{0,1},{1,0},{2,3},{3,2},{4,5},{5,4},{6,7},{7,6},{8,9},{9,8},{10,11... | collective-permute-start | bytes 3932168 | tf_op jit(solution)/shard_map/ppermute | solution.py:29
  73.2 26.9 %collective-permute-start.8 = (bf16[4,320,512]{2,1,0:T(8,128)(2,1)}, bf16[4,320,512]{2,1,0:T(8,128)(2,1)}, u32[]{:S(2)}, u32[]{:S(2)}) collective-permute-start(bf16[4,320,512]{2,1,0:T(8,128)(2,1)} %collective-permute-done.4.refs_2_), channel_id=1, source_target_pairs={{0,1},{1,0},{2,3},{3,2},{4,5},{5,4},{6,7},{7,6},{8,9},{9,8},{10,11... | collective-permute-start | bytes 3932168 | tf_op jit(solution)/shard_map/ppermute | solution.py:29
  74.7 25.4 %collective-permute-start.7 = (bf16[4,320,512]{2,1,0:T(8,128)(2,1)}, bf16[4,320,512]{2,1,0:T(8,128)(2,1)}, u32[]{:S(2)}, u32[]{:S(2)}) collective-permute-start(bf16[4,320,512]{2,1,0:T(8,128)(2,1)} %collective-permute-done.3.refs_1_), channel_id=1, source_target_pairs={{0,1},{1,0},{2,3},{3,2},{4,5},{5,4},{6,7},{7,6},{8,9},{9,8},{10,11... | collective-permute-start | bytes 3932168 | tf_op jit(solution)/shard_map/ppermute | solution.py:29
  76.3 23.6 %all-to-all-start.1 = ((bf16[32,6,1536]{2,1,0:T(8,128)(2,1)}), bf16[32,6,1536]{2,1,0:T(8,128)(2,1)S(1)}, u32[]{:S(2)}, u32[]{:S(2)}) async-start(bf16[32,6,1536]{2,1,0:T(8,128)(2,1)} %copy.26), calls=%async_computation.1 | async-start | bytes 1572864 | tf_op jit(solution)/shard_map/all_to_all | solution.py:350
  100.1 12.0 %copy-start.2 = (bf16[1,256,3584]{2,1,0:T(8,128)(2,1)S(1)}, bf16[1,256,3584]{2,1,0:T(8,128)(2,1)}, u32[]{:S(2)}) copy-start(bf16[1,256,3584]{2,1,0:T(8,128)(2,1)} %param.5) | copy-start | bytes 5505028
  112.1 6.5 %copy-start.5 = (bf16[1024,768]{1,0:T(8,128)(2,1)S(1)}, bf16[1024,768]{1,0:T(8,128)(2,1)}, u32[]{:S(2)}) copy-start(bf16[1024,768]{1,0:T(8,128)(2,1)} %get-tuple-element.20) | copy-start | bytes 4718596
  112.1 14.8 %copy-start.1 = (bf16[1024,768]{1,0:T(8,128)(2,1)S(1)}, bf16[1024,768]{1,0:T(8,128)(2,1)}, u32[]{:S(2)}) copy-start(bf16[1024,768]{1,0:T(8,128)(2,1)} %get-tuple-element.19) | copy-start | bytes 4718596
  116.1 10.8 %collective-permute-start.10 = (bf16[3584,512]{1,0:T(8,128)(2,1)S(1)}, bf16[3584,512]{1,0:T(8,128)(2,1)S(1)}, u32[]{:S(2)}, u32[]{:S(2)}) collective-permute-start(bf16[3584,512]{1,0:T(8,128)(2,1)S(1)} %get-tuple-element.18), channel_id=1, source_target_pairs={{0,1},{1,0},{2,3},{3,2},{4,5},{5,4},{6,7},{7,6},{8,9},{9,8},{10,11... | collective-permute-start | bytes 11010056 | tf_op jit(solution)/shard_map/ppermute | solution.py:29
  118.6 8.3 %collective-permute-start.11 = (bf16[1024,768]{1,0:T(8,128)(2,1)S(1)}, bf16[1024,768]{1,0:T(8,128)(2,1)S(1)}, u32[]{:S(2)}, u32[]{:S(2)}) collective-permute-start(bf16[1024,768]{1,0:T(8,128)(2,1)S(1)} %copy-done.5), channel_id=1, source_target_pairs={{0,1},{1,0},{2,3},{3,2},{4,5},{5,4},{6,7},{7,6},{8,9},{9,8},{10,11... | collective-permute-start | bytes 4718600 | tf_op jit(solution)/shard_map/ppermute | solution.py:29
  132.2 20.7 %collective-permute-start.12 = (bf16[4,320,512]{2,1,0:T(8,128)(2,1)S(1)}, bf16[4,320,512]{2,1,0:T(8,128)(2,1)S(1)}, u32[]{:S(2)}, u32[]{:S(2)}) collective-permute-start(bf16[4,320,512]{2,1,0:T(8,128)(2,1)S(1)} %get-tuple-element.22), channel_id=1, source_target_pairs={{0,8},{1,33},{2,10},{3,35},{4,12},{5,37},{6,14},{7,39},{8,16},{9,4... | collective-permute-start | bytes 3932168 | tf_op jit(solution)/shard_map/ppermute | solution.py:29
  136.4 16.8 %collective-permute-start.13 = (bf16[4,320,512]{2,1,0:T(8,128)(2,1)S(1)}, bf16[4,320,512]{2,1,0:T(8,128)(2,1)S(1)}, u32[]{:S(2)}, u32[]{:S(2)}) collective-permute-start(bf16[4,320,512]{2,1,0:T(8,128)(2,1)S(1)} %get-tuple-element.23), channel_id=1, source_target_pairs={{0,24},{1,97},{2,26},{3,99},{4,28},{5,101},{6,30},{7,103},{8,0},{9... | collective-permute-start | bytes 3932168 | tf_op jit(solution)/shard_map/ppermute | solution.py:29
  137.7 30.4 %collective-permute-start.14 = (bf16[4,320,512]{2,1,0:T(8,128)(2,1)S(1)}, bf16[4,320,512]{2,1,0:T(8,128)(2,1)S(1)}, u32[]{:S(2)}, u32[]{:S(2)}) collective-permute-start(bf16[4,320,512]{2,1,0:T(8,128)(2,1)S(1)} %get-tuple-element.24), channel_id=1, source_target_pairs={{0,16},{1,65},{2,18},{3,67},{4,20},{5,69},{6,22},{7,71},{8,24},{9,... | collective-permute-start | bytes 3932168 | tf_op jit(solution)/shard_map/ppermute | solution.py:29
  168.7 7.5 %collective-permute-start.15 = (bf16[320,512]{1,0:T(8,128)(2,1)S(1)}, bf16[320,512]{1,0:T(8,128)(2,1)S(1)}, u32[]{:S(2)}, u32[]{:S(2)}) collective-permute-start(bf16[320,512]{1,0:T(8,128)(2,1)S(1)} %get-tuple-element.25), channel_id=1, source_target_pairs={{0,32},{1,9},{2,34},{3,11},{4,36},{5,13},{6,38},{7,15},{8,40},{9,1... | collective-permute-start | bytes 983048 | tf_op jit(solution)/shard_map/ppermute | solution.py:29
  169.7 11.0 %collective-permute-start.17 = (bf16[320,512]{1,0:T(8,128)(2,1)S(1)}, bf16[320,512]{1,0:T(8,128)(2,1)S(1)}, u32[]{:S(2)}, u32[]{:S(2)}) collective-permute-start(bf16[320,512]{1,0:T(8,128)(2,1)S(1)} %get-tuple-element.26), channel_id=1, source_target_pairs={{0,64},{1,17},{2,66},{3,19},{4,68},{5,21},{6,70},{7,23},{8,72},{9,... | collective-permute-start | bytes 983048 | tf_op jit(solution)/shard_map/ppermute | solution.py:29
  172.3 8.3 %collective-permute-start.16 = (bf16[320,512]{1,0:T(8,128)(2,1)S(1)}, bf16[320,512]{1,0:T(8,128)(2,1)S(1)}, u32[]{:S(2)}, u32[]{:S(2)}) collective-permute-start(bf16[320,512]{1,0:T(8,128)(2,1)S(1)} %get-tuple-element.27), channel_id=1, source_target_pairs={{0,96},{1,25},{2,98},{3,27},{4,100},{5,29},{6,102},{7,31},{8,104},... | collective-permute-start | bytes 983048 | tf_op jit(solution)/shard_map/ppermute | solution.py:29
  182.0 22.7 %all-to-all-start.2 = ((bf16[16,20,512]{2,1,0:T(8,128)(2,1)}), bf16[16,20,512]{2,1,0:T(8,128)(2,1)S(1)}, u32[]{:S(2)}, u32[]{:S(2)}) async-start(bf16[16,20,512]{2,1,0:T(8,128)(2,1)} %pad_maximum_fusion.2), calls=%async_computation.2 | async-start | bytes 786432 | tf_op jit(solution)/shard_map/all_to_all | solution.py:382
  190.1 3.1 %copy-start = (bf16[32,112,1024]{2,1,0:T(8,128)(2,1)S(1)}, bf16[32,112,1024]{2,1,0:T(8,128)(2,1)}, u32[]{:S(2)}) copy-start(bf16[32,112,1024]{2,1,0:T(8,128)(2,1)} %get-tuple-element.16) | copy-start | bytes 22020100

commit v2 on v1

v2 whole, which is shorter than its diff:
```python
import jax
import jax.numpy as jnp
import numpy as np
from jax import lax
from jax.experimental import pallas as pl
from jax.experimental.pallas import tpu as pltpu
from jax.sharding import Mesh, PartitionSpec as P

loss_scale = 256.0
eps_norm = 1e-06

AXES = ("zh", "x", "y", "zl", "c")
SIZES = (2, 4, 4, 4, 2)
D, PH, DT, TOK = 3584, 1024, 1536, 256
HH, HO = PH // 2, DT // 2
ROWS_IN, ROWS_OUT = 112, 32
PACK = 320
HID = HH + HO
bf16, f32 = jnp.bfloat16, jnp.float32
NT = (((1,), (1,)), ((), ()))
TN = (((0,), (0,)), ((), ()))


def permute(v, move):
    pairs = []
    for i in range(256):
        here = [int(a) for a in np.unravel_index(i, SIZES)]
        there = [a % s for a, s in zip(move(*here), SIZES)]
        pairs.append((i, int(np.ravel_multi_index(there, SIZES))))
    return lax.ppermute(v, AXES, pairs)


def first_axis(v, d):
    return permute(
        v, lambda zh, x, y, zl, c: (zh, x + d * (c == 0), y + d * (c == 1), zl, c)
    )


def second_axis(v, d):
    return permute(
        v, lambda zh, x, y, zl, c: (zh, x + d * (c == 1), y + d * (c == 0), zl, c)
    )


def swap_cores(v):
    return permute(v, lambda zh, x, y, zl, c: (zh, x, y, zl, 1 - c))


def place_of(core, x, y, d3, d2):
    sx = lax.rem(x + jnp.where(core == 0, d2, d3), 4)
    sy = lax.rem(y + jnp.where(core == 0, d3, d2), 4)
    return sx, sy


SHIFTS = (0, 1, 3, 2)


def head_kernel(place, latent, picked, expand, *refs):
    own, oth = refs[0:4], refs[4:8]
    grad_pre_ref, keep_ref, give_ref, w_in_out = refs[8:12]
    w_in, w_out, pre, pred, gpred, sems = refs[12:]
    x, y, c = place[0], place[1], place[2]

    def fetch(half_refs, core, sem_in, sem_out):
        for k, d3 in enumerate(SHIFTS):
            for j, d2 in enumerate(SHIFTS):
                sx, sy = place_of(core, x, y, 4 - d3, 4 - d2)
                src = half_refs[k].at[j]
                for zh in range(2):
                    cols = pl.ds(pl.multiple_of(core * HH, HH), HH)
                    pltpu.make_async_copy(
                        src.at[pl.ds(zh * ROWS_IN, ROWS_IN)],
                        w_in.at[zh * 16 + sx * 4 + sy, :, cols],
                        sems.at[sem_in],
                    ).start()
                    rows = pl.ds(
                        pl.multiple_of((zh * 16 + sx * 4 + sy) * ROWS_OUT, ROWS_OUT),
                        ROWS_OUT,
                    )
                    pltpu.make_async_copy(
                        src.at[pl.ds(224 + zh * 32, 32)],
                        w_out.at[rows, pl.ds(pl.multiple_of(core * HO, 256), 512)],
                        sems.at[sem_out],
                    ).start()
                    pltpu.make_async_copy(
                        src.at[pl.ds(288, 32), pl.ds(zh * 256, 256)],
                        w_out.at[rows, pl.ds(pl.multiple_of(core * HO + 512, 256), 256)],
                        sems.at[sem_out],
                    ).start()

    fetch(own, c, 0, 2)
    fetch(oth, 1 - c, 1, 2)
    goal = jnp.dot(expand[...], picked[...], preferred_element_type=f32)
    norm_goal = jnp.sqrt(jnp.sum(goal * goal, axis=1, keepdims=True) + eps_norm)
    half = w_in.at[:, :, pl.ds(0, HH)]
    for core, sem in ((c, 0), (1 - c, 1)):
        pltpu.make_async_copy(half, half, sems.at[sem]).wait()
        for j in range(2):
            cols = pl.ds(pl.multiple_of(core * HH + j * 256, 256), 256)
            part = jnp.dot(
                latent[...],
                w_in[:, :, cols].reshape(D, 256),
                preferred_element_type=f32,
            )
            pre[:, cols] = part
            keep_ref[:, pl.ds(pl.multiple_of(HID + core * HH + j * 256, 256), 256)] = (
                part * jax.nn.sigmoid(part)
            ).astype(bf16)
    save = pltpu.make_async_copy(w_in, w_in_out, sems.at[3])
    save.start()
    pltpu.make_async_copy(w_out, w_out, sems.at[2]).wait()
    for j in range(6):
        cols = slice(j * 256, (j + 1) * 256)
        pred[:, cols] = jnp.dot(
            keep_ref[:, HID:], w_out[:, cols], preferred_element_type=f32
        )
    guess = pred[...]
    norm_pred = jnp.sqrt(jnp.sum(guess * guess, axis=1, keepdims=True) + eps_norm)
    cosv = jnp.sum(guess * goal, axis=1, keepdims=True) / (norm_pred * norm_goal)
    gpred[...] = (
        -loss_scale
        * (goal / (norm_pred * norm_goal) - cosv * guess / (norm_pred * norm_pred))
    ).astype(bf16)
    for j in range(4):
        cols = slice(j * 256, (j + 1) * 256)
        grad_hidden = lax.dot_general(
            gpred[...], w_out[cols, :], NT, preferred_element_type=f32
        )
        part = pre[:, cols]
        sig = jax.nn.sigmoid(part)
        grad_pre_ref[:, cols] = (
            grad_hidden * (sig * (1.0 + part * (1.0 - sig)))
        ).astype(bf16)
    for ref, core in ((keep_ref, c), (give_ref, 1 - c)):
        ref[:, :HH] = grad_pre_ref[:, pl.ds(pl.multiple_of(core * HH, HH), HH)]
        ref[:, HH:HID] = gpred[:, pl.ds(pl.multiple_of(core * HO, 256), HO)]
    give_ref[:, HID:] = keep_ref[:, HID:]
    save.wait()


def head(place, latent, picked, expand, own, oth):
    vmem = pl.BlockSpec(memory_space=pltpu.VMEM)
    hbm = pl.BlockSpec(memory_space=pl.ANY)
    return pl.pallas_call(
        head_kernel,
        in_specs=[pl.BlockSpec(memory_space=pltpu.SMEM)] + [vmem] * 3 + [hbm] * 8,
        out_specs=[vmem, vmem, vmem, hbm],
        out_shape=[
            jax.ShapeDtypeStruct((TOK, PH), bf16),
            jax.ShapeDtypeStruct((TOK, HID + PH), bf16),
            jax.ShapeDtypeStruct((TOK, HID + PH), bf16),
            jax.ShapeDtypeStruct((32, ROWS_IN, PH), bf16),
        ],
        scratch_shapes=[
            pltpu.VMEM((32, ROWS_IN, PH), bf16),
            pltpu.VMEM((PH, DT), bf16),
            pltpu.VMEM((TOK, PH), f32),
            pltpu.VMEM((TOK, DT), f32),
            pltpu.VMEM((TOK, DT), bf16),
            pltpu.SemaphoreType.DMA((4,)),
        ],
        compiler_params=pltpu.CompilerParams(vmem_limit_bytes=40 * 2**20),
        cost_estimate=pl.CostEstimate(
            flops=5_000_000_000, bytes_accessed=30_000_000, transcendentals=600_000
        ),
        name="head",
    )(place, latent, picked, expand, *own, *oth)


def tail_kernel(place, lat_ref, keep, rcv, *refs):
    outs = refs[:4]
    p_in, p_out, sems = refs[4:]
    x, y, c = place[0], place[1], place[2]
    gpred = jnp.concatenate([keep[:, HH:HID], rcv[:, HH:HID]], axis=0)
    for zh in range(2):
        hid = slice(HID + zh * HH, HID + (zh + 1) * HH)
        hidden = jnp.concatenate([keep[:, hid], rcv[:, hid]], axis=0)
        p_out[zh * HH : (zh + 1) * HH] = lax.dot_general(
            hidden, gpred, TN, preferred_element_type=f32
        ).astype(bf16)
    gpre = jnp.concatenate([keep[:, :HH], rcv[:, :HH]], axis=0)
    for sx in range(4):
        for zh in range(2):
            b = zh * 16 + sx * 4
            rows = slice(b * ROWS_IN, (b + 4) * ROWS_IN)
            p_in[rows] = jnp.dot(
                lat_ref[rows], gpre, preferred_element_type=f32
            ).astype(bf16)
        for sy in range(4):
            dx, dy = lax.rem(sx + 4 - x, 4), lax.rem(sy + 4 - y, 4)
            d2, d3 = jnp.where(c == 0, dx, dy), jnp.where(c == 0, dy, dx)
            for k in range(4):

                @pl.when(d3 == k)
                def _(sx=sx, sy=sy, d2=d2, k=k):
                    dst = outs[k].at[d2]
                    for zh in range(2):
                        b = zh * 16 + sx * 4 + sy
                        low = pl.ds(b * ROWS_OUT, ROWS_OUT)
                        pltpu.make_async_copy(
                            p_in.at[pl.ds(b * ROWS_IN, ROWS_IN)],
                            dst.at[pl.ds(zh * ROWS_IN, ROWS_IN)],
                            sems.at[0],
                        ).start()
                        pltpu.make_async_copy(
                            p_out.at[low, pl.ds(0, 512)],
                            dst.at[pl.ds(224 + zh * 32, 32)],
                            sems.at[1],
                        ).start()
                        pltpu.make_async_copy(
                            p_out.at[low, pl.ds(512, 256)],
                            dst.at[pl.ds(288, 32), pl.ds(zh * 256, 256)],
                            sems.at[1],
                        ).start()

    pltpu.make_async_copy(p_in, p_in, sems.at[0]).wait()
    pltpu.make_async_copy(p_out, p_out, sems.at[1]).wait()


def tail(place, lat_both, keep, rcv):
    vmem = pl.BlockSpec(memory_space=pltpu.VMEM)
    hbm = pl.BlockSpec(memory_space=pl.ANY)
    return pl.pallas_call(
        tail_kernel,
        in_specs=[pl.BlockSpec(memory_space=pltpu.SMEM)] + [vmem] * 3,
        out_specs=[hbm] * 4,
        out_shape=[jax.ShapeDtypeStruct((4, PACK, HH), bf16)] * 4,
        scratch_shapes=[
            pltpu.VMEM((D, HH), bf16),
            pltpu.VMEM((PH, HO), bf16),
            pltpu.SemaphoreType.DMA((2,)),
        ],
        compiler_params=pltpu.CompilerParams(vmem_limit_bytes=40 * 2**20),
        cost_estimate=pl.CostEstimate(
            flops=2_700_000_000, bytes_accessed=12_000_000, transcendentals=0
        ),
        name="tail",
    )(place, lat_both, keep, rcv)


def back_kernel(grad_pre, w_in, out):
    out[...] = lax.dot_general(
        grad_pre[...], w_in[...], NT, preferred_element_type=f32
    ).astype(bf16)


def back(grad_pre, w_in):
    step = 512
    return pl.pallas_call(
        back_kernel,
        grid=(D // step,),
        in_specs=[
            pl.BlockSpec((TOK, PH), lambda i: (0, 0)),
            pl.BlockSpec((step, PH), lambda i: (i, 0)),
        ],
        out_specs=pl.BlockSpec((TOK, step), lambda i: (0, i)),
        out_shape=jax.ShapeDtypeStruct((TOK, D), bf16),
        compiler_params=pltpu.CompilerParams(vmem_limit_bytes=60 * 2**20),
        cost_estimate=pl.CostEstimate(
            flops=1_900_000_000, bytes_accessed=10_000_000, transcendentals=0
        ),
        name="back",
    )(grad_pre, w_in)


def add4(a, b, c, d):
    return (
        (a.astype(f32) + b.astype(f32)) + (c.astype(f32) + d.astype(f32))
    ).astype(bf16)


def per_device(latent, targets, index_map, proj_in, proj_out):
    x, y, c = lax.axis_index("x"), lax.axis_index("y"), lax.axis_index("c")
    place = jnp.stack([x, y, c]).astype(jnp.int32)

    halves = jnp.concatenate(
        [
            proj_in.reshape(14, 2, HH).transpose(1, 0, 2),
            proj_out.reshape(4, 2, HO).transpose(1, 0, 2).reshape(2, 6, HH),
        ],
        axis=1,
    )
    fan = jnp.broadcast_to(halves[None], (8, 2, 20, HH)).reshape(16, 20, HH)
    column = lax.all_to_all(
        fan, ("zh", "zl", "c"), split_axis=0, concat_axis=0, tiled=True
    )
    rows_in = column[:, :14].reshape(224, HH)
    rows_out = column[:, 14:].reshape(16, 4, HO).reshape(2, ROWS_OUT, HO)
    packed = jnp.concatenate(
        [
            rows_in,
            rows_out[:, :, :512].reshape(64, 512),
            rows_out[:, :, 512:].transpose(1, 0, 2).reshape(32, 512),
        ],
        axis=0,
    )
    maps = index_map[0]
    width = targets.shape[2] * 32
    row_of = maps[:, 0] // width
    slab = targets[0].transpose(1, 0, 2)
    pick = (row_of[:, None] == jnp.arange(48, dtype=jnp.int32)[None]).astype(bf16)
    sent = jnp.stack(
        [jnp.dot(pick, slab[t], preferred_element_type=f32).astype(bf16) for t in range(3)]
    )
    sent = sent.reshape(3, 32, 2, DT).transpose(1, 0, 2, 3).reshape(32, 6, DT)
    lat_t = latent[0].T
    packed, sent, lat_t = lax.optimization_barrier((packed, sent, lat_t))
    got = lax.all_to_all(
        sent, ("zh", "x", "y"), split_axis=0, concat_axis=0, tiled=True
    )
    line = jnp.stack([packed] + [first_axis(packed, d) for d in SHIFTS[1:]])
    lat_both = jnp.concatenate([lat_t, swap_cores(lat_t)], axis=1)
    own = [line] + [second_axis(line, d) for d in SHIFTS[1:]]
    own[1], got, lat_both = lax.optimization_barrier((own[1], got, lat_both))
    oth = [swap_cores(v) for v in own]
    picked = got.reshape(192, DT)
    col_of = (maps[0] % width).reshape(32, 4) - 3 * jnp.arange(32, dtype=jnp.int32)[:, None]
    token = jnp.arange(TOK, dtype=jnp.int32)[:, None]
    row = jnp.arange(192, dtype=jnp.int32)[None]
    want = ((token // 4) % 32) * 6 + jnp.tile(col_of.reshape(128), 2)[:, None] * 2 + token // 128
    expand = (row == want).astype(bf16)

    grad_pre, keep, give, w_in = head(place, latent[0], picked, expand, own, oth)
    rcv = swap_cores(give)
    grad_latent = back(grad_pre, w_in.reshape(D, PH))
    rcv, grad_latent = lax.optimization_barrier((rcv, grad_latent))
    sums = tail(place, lat_both, keep, rcv)
    got3 = [second_axis(sums[d], d) for d in SHIFTS[1:]]
    line_sum = [add4(sums[0][k], got3[0][k], got3[1][k], got3[2][k]) for k in range(4)]
    got2 = [first_axis(line_sum[d], d) for d in SHIFTS[1:]]
    mine = add4(line_sum[0], *got2)
    g_in = mine[:224].reshape(16, 14, HH)
    g_out = jnp.concatenate(
        [
            mine[224:288].reshape(2, 32, 512),
            mine[288:].reshape(32, 2, 256).transpose(1, 0, 2),
        ],
        axis=2,
    ).reshape(16, 4, HO).reshape(16, 6, HH)
    last = lax.all_to_all(
        jnp.concatenate([g_in, g_out], axis=1),
        ("zh", "zl", "c"), split_axis=0, concat_axis=0, tiled=True,
    )
    total = jnp.sum(last.reshape(8, 2, 20, HH).astype(f32), axis=0)
    grad_in = total[:, :14].transpose(1, 0, 2).reshape(14, PH)
    grad_out = total[:, 14:].reshape(2, 4, HO).transpose(1, 0, 2).reshape(4, DT)
    return grad_latent[None], grad_in, grad_out


def solution(mesh):
    fine = Mesh(mesh.devices.reshape(SIZES), AXES)
    seq, fsdp = ("zh", "x", "y"), ("zl", "c")
    rows = P(AXES, None)
    return jax.shard_map(
        per_device,
        mesh=fine,
        in_specs=(P(fsdp, seq, None), P(fsdp, None, seq, None), P(fsdp, None, None), rows, rows),
        out_specs=(P(fsdp, seq, None), rows, rows),
        check_vma=False,
    )
```

time: 207 us -> 189 us (0.913)
  waiting for transfers between devices: 102 us -> 77.5 us
  blocking collectives: 24.3 us -> 19.4 us
  local copies, waits for them, and re-layouts: 8.25 us -> 13.1 us
  other arithmetic: 2.43 us -> 6.17 us
  Pallas kernels: 25.9 us -> 29.2 us
    all_to_all x2, waiting for transfers between devices: 23.8 us -> 9.53 us  [the longest x1 9.53 us: per_device(): lax.all_to_all(fan, ('zh', 'zl', 'c'), split_axis=0, concat_axis=0, tiled...]
    ppermute x18, waiting for transfers between devices: 78 us -> 68 us  [permute(): return lax.ppermute(v, AXES, pairs)]
    all_to_all x1, blocking collectives: 24.3 us -> 19.4 us  [per_device(): lax.all_to_all(jnp.concatenate([g_in, g_out], axis=1), ('zh', 'zl', 'c'),...]
    concatenate x0 -> x2, other arithmetic: none -> 3.72 us  [the longest x1 3.7 us: per_device(): lat_both = jnp.concatenate([lat_t, swap_cores(lat_t)], axis=1)]
    pallas_call x1, Pallas kernels: 4.7 us -> 8.19 us  [back(): pl.pallas_call(back_kernel, grid=(D // step,), in_specs=[pl.BlockSpec((TO...]
    unnamed x15 -> x18, local copies, waits for them, and re-layouts: 3.77 us -> 6.66 us
    ppermute x18, starting transfers between devices: 27.4 us -> 24.7 us  [permute(): return lax.ppermute(v, AXES, pairs)]
    all_to_all x2, starting transfers between devices: 14.3 us -> 17 us  [the longest x1 9.98 us: per_device(): lax.all_to_all(fan, ('zh', 'zl', 'c'), split_axis=0, concat_axis=0, tiled...]
  transfers between devices with their start and end apart: 20 -> 20, of which waited for: 12 -> 11; matrix products, arithmetic and copies ran while one was open for 1% -> 6% of each run, Pallas kernels for 2% -> 4%
where the time goes in v2:
time: 189 us
  waiting for transfers between devices  77.5 us (41%)
  starting transfers between devices  41.7 us (22%)
  Pallas kernels  29.2 us (15%)
  blocking collectives  19.4 us (10%)
  local copies, waits for them, and re-layouts  13.1 us (7%)
  other arithmetic  6.17 us (3%)
    ppermute x18, waiting for transfers between devices, permute(): return lax.ppermute(v, AXES, pairs)  68 us
    ppermute x18, starting transfers between devices, permute(): return lax.ppermute(v, AXES, pairs)  24.7 us
    all_to_all x1, blocking collectives, per_device(): lax.all_to_all(jnp.concatenate([g_in, g_out], axis=1), ('zh', 'zl', 'c'),...  19.4 us
    pallas_call x1, Pallas kernels, head(): pl.pallas_call(head_kernel, in_specs=[pl.BlockSpec(memory_space=pltpu.SME...  10.7 us
    pallas_call x1, Pallas kernels, tail(): pl.pallas_call(tail_kernel, in_specs=[pl.BlockSpec(memory_space=pltpu.SME...  10.2 us
    all_to_all x1, starting transfers between devices, per_device(): lax.all_to_all(fan, ('zh', 'zl', 'c'), split_axis=0, concat_axis=0, tiled...  9.98 us
    all_to_all x1, waiting for transfers between devices, per_device(): lax.all_to_all(fan, ('zh', 'zl', 'c'), split_axis=0, concat_axis=0, tiled...  9.53 us
    pallas_call x1, Pallas kernels, back(): pl.pallas_call(back_kernel, grid=(D // step,), in_specs=[pl.BlockSpec((TO...  8.19 us
  transfers between devices with their start and end apart: 20, of which 11 were waited for; matrix products, arithmetic and copies ran while one was open for 6% of the time, Pallas kernels for 4%

profile of v2, /device:TPU:1, one launch (start us, length us, event | category | flops | bytes accessed | tf_op | source)
XLA Modules:
  0.0 188.8 jit_solution(821340591466741002)
XLA Ops:
  0.7 0.8 reshape.226
  1.4 0.8 reshape.225
  2.3 0.8 broadcast_in_dim.4
  3.1 10.0 %all-to-all-start = ((bf16[16,20,512]{2,1,0:T(8,128)(2,1)}), bf16[16,20,512]{2,1,0:T(8,128)(2,1)S(1)}, u32[]{:S(2)}, u32[]{:S(2)}) async-start(bf16[16,20,512]{2,1,0:T(8,128)(2,1)} %bitcast.8), calls=%async_computation | async-start | bytes 786432 | tf_op jit(solution)/shard_map/all_to_all | solution.py:284
  13.1 0.1 fusion.7
  13.2 0.2 convolution_convert_fusion
  13.4 0.1 stack.45
  13.6 0.2 convolution_convert_fusion.1
  13.8 0.1 stack.44
  13.9 0.2 convolution_convert_fusion.2
  14.2 0.1 stack.43
  14.3 2.9 %copy.33 = bf16[1,256,3584]{1,2,0:T(8,128)(2,1)S(1)} copy(bf16[1,256,3584]{2,1,0:T(8,128)(2,1)} %param.5) | data formatting | bytes 3670016 | tf_op args[0]
  17.2 0.9 pad_maximum_fusion.2
  18.1 9.5 %all-to-all-done = bf16[16,20,512]{2,1,0:T(8,128)(2,1)S(1)} async-done(((bf16[16,20,512]{2,1,0:T(8,128)(2,1)}), bf16[16,20,512]{2,1,0:T(8,128)(2,1)S(1)}, u32[]{:S(2)}, u32[]{:S(2)}) %all-to-all-start) | async-done | bytes 327712 | tf_op jit(solution)/shard_map/all_to_all | solution.py:284
  27.6 0.1 reshape_reshape.6
  27.8 0.1 reshape.229
  27.9 0.1 collective-permute-start.4
  28.0 3.0 %collective-permute-start.2 = (bf16[320,512]{1,0:T(8,128)(2,1)S(1)}, bf16[320,512]{1,0:T(8,128)(2,1)S(1)}, u32[]{:S(2)}, u32[]{:S(2)}) collective-permute-start(bf16[320,512]{1,0:T(8,128)(2,1)S(1)} %pad_maximum_fusion.4), channel_id=1, source_target_pairs={{0,64},{1,17},{2,66},{3,19},{4,68},{5,21},{6,70},{7,23},{8,72},{9,... | collective-permute-start | bytes 983048 | tf_op jit(solution)/shard_map/ppermute | solution.py:30
  31.0 0.8 collective-permute-start.1
  31.8 0.7 collective-permute-start
  32.5 3.3 %collective-permute-done.2 = bf16[320,512]{1,0:T(8,128)(2,1)S(1)} collective-permute-done((bf16[320,512]{1,0:T(8,128)(2,1)S(1)}, bf16[320,512]{1,0:T(8,128)(2,1)S(1)}, u32[]{:S(2)}, u32[]{:S(2)}) %collective-permute-start.2) | collective-permute-done | bytes 327712 | tf_op jit(solution)/shard_map/ppermute | solution.py:30
  35.8 3.9 %collective-permute-done.1 = bf16[320,512]{1,0:T(8,128)(2,1)S(1)} collective-permute-done((bf16[320,512]{1,0:T(8,128)(2,1)S(1)}, bf16[320,512]{1,0:T(8,128)(2,1)S(1)}, u32[]{:S(2)}, u32[]{:S(2)}) %collective-permute-start.1) | collective-permute-done | bytes 327712 | tf_op jit(solution)/shard_map/ppermute | solution.py:30
  39.7 0.2 pad_maximum_fusion.1.refs_0_
  39.9 2.8 %collective-permute-start.6 = (bf16[4,320,512]{2,1,0:T(8,128)(2,1)S(1)}, bf16[4,320,512]{2,1,0:T(8,128)(2,1)}, u32[]{:S(2)}, u32[]{:S(2)}) collective-permute-start(bf16[4,320,512]{2,1,0:T(8,128)(2,1)S(1)} %pad_maximum_fusion.1.refs_0_), channel_id=1, source_target_pairs={{0,16},{1,65},{2,18},{3,67},{4,20},{5,69},{6,22},{7,71},{8,24},{9,... | collective-permute-start | bytes 3932168 | tf_op jit(solution)/shard_map/ppermute | solution.py:30
  42.7 0.9 collective-permute-start.5
  43.6 0.6 collective-permute-start.3
  44.2 1.2 copy.39
  45.4 7.0 %all-to-all-start.1 = ((bf16[32,6,1536]{2,1,0:T(8,128)(2,1)}), bf16[32,6,1536]{2,1,0:T(8,128)(2,1)}, u32[]{:S(2)}, u32[]{:S(2)}) async-start(bf16[32,6,1536]{2,1,0:T(8,128)(2,1)} %copy.39), calls=%async_computation.1 | async-start | bytes 1572864 | tf_op jit(solution)/shard_map/all_to_all | solution.py:308
  52.4 2.1 %collective-permute-start.7 = (bf16[4,320,512]{2,1,0:T(8,128)(2,1)S(1)}, bf16[4,320,512]{2,1,0:T(8,128)(2,1)}, u32[]{:S(2)}, u32[]{:S(2)}) collective-permute-start(bf16[4,320,512]{2,1,0:T(8,128)(2,1)S(1)} %pad_maximum_fusion.1.refs_0_), channel_id=1, source_target_pairs={{0,1},{1,0},{2,3},{3,2},{4,5},{5,4},{6,7},{7,6},{8,9},{9,8},{10,11... | collective-permute-start | bytes 3932168 | tf_op jit(solution)/shard_map/ppermute | solution.py:30
  54.5 6.3 %collective-permute-done.6.refs_3_ = bf16[4,320,512]{2,1,0:T(8,128)(2,1)} collective-permute-done((bf16[4,320,512]{2,1,0:T(8,128)(2,1)S(1)}, bf16[4,320,512]{2,1,0:T(8,128)(2,1)}, u32[]{:S(2)}, u32[]{:S(2)}) %collective-permute-start.6) | collective-permute-done | bytes 1310752 | tf_op jit(solution)/shard_map/ppermute | solution.py:30
  60.8 2.0 %collective-permute-start.10 = (bf16[4,320,512]{2,1,0:T(8,128)(2,1)}, bf16[4,320,512]{2,1,0:T(8,128)(2,1)}, u32[]{:S(2)}, u32[]{:S(2)}) collective-permute-start(bf16[4,320,512]{2,1,0:T(8,128)(2,1)} %collective-permute-done.6.refs_3_), channel_id=1, source_target_pairs={{0,1},{1,0},{2,3},{3,2},{4,5},{5,4},{6,7},{7,6},{8,9},{9,8},{10,11... | collective-permute-start | bytes 3932168 | tf_op jit(solution)/shard_map/ppermute | solution.py:30
  62.7 16.1 %collective-permute-done.5.refs_2_ = bf16[4,320,512]{2,1,0:T(8,128)(2,1)} collective-permute-done((bf16[4,320,512]{2,1,0:T(8,128)(2,1)S(1)}, bf16[4,320,512]{2,1,0:T(8,128)(2,1)}, u32[]{:S(2)}, u32[]{:S(2)}) %collective-permute-start.5) | collective-permute-done | bytes 1310752 | tf_op jit(solution)/shard_map/ppermute | solution.py:30
  78.8 4.1 %collective-permute-start.9 = (bf16[4,320,512]{2,1,0:T(8,128)(2,1)}, bf16[4,320,512]{2,1,0:T(8,128)(2,1)}, u32[]{:S(2)}, u32[]{:S(2)}) collective-permute-start(bf16[4,320,512]{2,1,0:T(8,128)(2,1)} %collective-permute-done.5.refs_2_), channel_id=1, source_target_pairs={{0,1},{1,0},{2,3},{3,2},{4,5},{5,4},{6,7},{7,6},{8,9},{9,8},{10,11... | collective-permute-start | bytes 3932168 | tf_op jit(solution)/shard_map/ppermute | solution.py:30
  82.9 3.7 %pad_maximum_fusion.lat_ref = bf16[3584,512]{1,0:T(8,128)(2,1)} fusion(bf16[3584,256]{1,0:T(8,128)(2,1)} %collective-permute-done.4, bf16[3584,256]{1,0:T(8,128)(2,1)S(1)} %bitcast.75), kind=kLoop, calls=%fused_computation | loop fusion | flops 7340032 | bytes 7340032 | tf_op jit(solution)/shard_map/concatenate | solution.py:312
  86.6 0.1 sub.32
  86.7 0.1 sub.33
  86.8 0.1 pad_add_fusion.place
  86.9 0.1 fusion.6.expand
  87.0 1.4 reshape.233.picked
  88.4 1.6 collective-permute-done.8.refs_5_
  90.0 10.7 %head.1 = (bf16[256,1024]{1,0:T(8,128)(2,1)S(1)}, bf16[256,2304]{1,0:T(8,128)(2,1)S(1)}, bf16[256,2304]{1,0:T(8,128)(2,1)}, bf16[32,112,1024]{2,1,0:T(8,128)(2,1)}) custom-call(s32[3]{0:T(128)S(1)} %pad_add_fusion.place, bf16[256,3584]{1,0:T(8,128)(2,1)} %bitcast.79, bf16[192,1536]{1,0:T(8,128)(2,1)S(1)} %reshape.233.picked, ...), custom_call_target="tpu_custom_call" | custom-call | flops 5000000000 | bytes 30000000 | tf_op jit(solution)/shard_map/head/pallas_call | solution.py:144
  100.7 0.8 copy-done.1
  101.6 1.0 copy-done.2
  102.6 0.1 collective-permute-start.11
  102.7 8.2 %back.1 = bf16[256,3584]{1,0:T(8,128)(2,1)} custom-call(bf16[256,1024]{1,0:T(8,128)(2,1)} %copy-done.1, bf16[3584,1024]{1,0:T(8,128)(2,1)} %bitcast.76), custom_call_target="tpu_custom_call" | custom-call | flops 1900000000 | bytes 10000000 | tf_op jit(solution)/shard_map/back/pallas_call | solution.py:249
  110.9 1.3 copy-done.3
  112.2 10.2 %tail.1 = (bf16[4,320,512]{2,1,0:T(8,128)(2,1)S(1)}, bf16[4,320,512]{2,1,0:T(8,128)(2,1)S(1)}, bf16[4,320,512]{2,1,0:T(8,128)(2,1)S(1)}, bf16[4,320,512]{2,1,0:T(8,128)(2,1)S(1)}) custom-call(s32[3]{0:T(128)S(1)} %pad_add_fusion.place, bf16[3584,512]{1,0:T(8,128)(2,1)S(1)} %copy-done, bf16[256,2304]{1,0:T(8,128)(2,1)S(1)} %copy-done.3, ...), custom_call_target="tpu_custom_call" | custom-call | flops 2700000000 | bytes 12000000 | tf_op jit(solution)/shard_map/tail/pallas_call | solution.py:223
  122.4 1.1 collective-permute-start.12
  123.5 1.7 collective-permute-start.13
  125.2 1.2 collective-permute-start.14
  126.4 14.0 %collective-permute-done.12 = bf16[4,320,512]{2,1,0:T(8,128)(2,1)S(1)} collective-permute-done((bf16[4,320,512]{2,1,0:T(8,128)(2,1)S(1)}, bf16[4,320,512]{2,1,0:T(8,128)(2,1)S(1)}, u32[]{:S(2)}, u32[]{:S(2)}) %collective-permute-start.12) | collective-permute-done | bytes 1310752 | tf_op jit(solution)/shard_map/ppermute | solution.py:30
  140.5 13.3 %collective-permute-done.13 = bf16[4,320,512]{2,1,0:T(8,128)(2,1)S(1)} collective-permute-done((bf16[4,320,512]{2,1,0:T(8,128)(2,1)S(1)}, bf16[4,320,512]{2,1,0:T(8,128)(2,1)S(1)}, u32[]{:S(2)}, u32[]{:S(2)}) %collective-permute-start.13) | collective-permute-done | bytes 1310752 | tf_op jit(solution)/shard_map/ppermute | solution.py:30
  153.8 1.2 collective-permute-done.14
  155.0 0.6 fusion.3
  155.5 0.4 collective-permute-start.15
  155.9 3.1 %collective-permute-start.17 = (bf16[320,512]{1,0:T(8,128)(2,1)S(1)}, bf16[320,512]{1,0:T(8,128)(2,1)S(1)}, u32[]{:S(2)}, u32[]{:S(2)}) collective-permute-start(bf16[320,512]{1,0:T(8,128)(2,1)S(1)} %get-tuple-element.36), channel_id=1, source_target_pairs={{0,64},{1,17},{2,66},{3,19},{4,68},{5,21},{6,70},{7,23},{8,72},{9,... | collective-permute-start | bytes 983048 | tf_op jit(solution)/shard_map/ppermute | solution.py:30
  159.1 4.0 %collective-permute-done.15 = bf16[320,512]{1,0:T(8,128)(2,1)S(1)} collective-permute-done((bf16[320,512]{1,0:T(8,128)(2,1)S(1)}, bf16[320,512]{1,0:T(8,128)(2,1)S(1)}, u32[]{:S(2)}, u32[]{:S(2)}) %collective-permute-start.15) | collective-permute-done | bytes 327712 | tf_op jit(solution)/shard_map/ppermute | solution.py:30
  163.1 4.3 %collective-permute-done.17 = bf16[320,512]{1,0:T(8,128)(2,1)S(1)} collective-permute-done((bf16[320,512]{1,0:T(8,128)(2,1)S(1)}, bf16[320,512]{1,0:T(8,128)(2,1)S(1)}, u32[]{:S(2)}, u32[]{:S(2)}) %collective-permute-start.17) | collective-permute-done | bytes 327712 | tf_op jit(solution)/shard_map/ppermute | solution.py:30
  167.3 0.3 fusion.1
  167.8 0.1 reshape.235
  167.9 0.1 pad_maximum_fusion.3
  168.0 19.4 %all_to_all.15 = bf16[16,20,512]{2,1,0:T(8,128)(2,1)S(1)} all-to-all(bf16[16,20,512]{2,1,0:T(8,128)(2,1)S(1)} %pad_maximum_fusion.3), channel_id=1, replica_groups=mesh['zh'=2,'x'=4,'y'=4,'zl'=4,'c'=2] {'zh','zl','c'}, dimensions={0} | all-to-all | bytes 655360 | tf_op jit(solution)/shard_map/all_to_all | solution.py:340
  187.5 0.6 reshape.239
  188.1 0.6 copy.46
  (47 shorter events, 0.6 us)
Async XLA Ops:
  0.6 12.4 %copy-start.6 = (s32[1,64,128]{2,1,0:T(8,128)S(1)}, s32[1,64,128]{2,1,0:T(8,128)}, u32[]{:S(2)}) copy-start(s32[1,64,128]{2,1,0:T(8,128)} %param.7) | copy-start | bytes 98308
  0.6 12.5 %copy-start.5 = (bf16[1,48,3,1536]{3,1,2,0:T(8,128)(2,1)S(1)}, bf16[1,48,3,1536]{3,1,2,0:T(8,128)(2,1)}, u32[]{:S(2)}) copy-start(bf16[1,48,3,1536]{3,1,2,0:T(8,128)(2,1)} %param.6) | copy-start | bytes 1327108
  3.1 24.5 %all-to-all-start = ((bf16[16,20,512]{2,1,0:T(8,128)(2,1)}), bf16[16,20,512]{2,1,0:T(8,128)(2,1)S(1)}, u32[]{:S(2)}, u32[]{:S(2)}) async-start(bf16[16,20,512]{2,1,0:T(8,128)(2,1)} %bitcast.8), calls=%async_computation | async-start | bytes 786432 | tf_op jit(solution)/shard_map/all_to_all | solution.py:284
  27.9 55.0 %collective-permute-start.4 = (bf16[3584,256]{1,0:T(8,128)(2,1)S(1)}, bf16[3584,256]{1,0:T(8,128)(2,1)}, u32[]{:S(2)}, u32[]{:S(2)}) collective-permute-start(bf16[3584,256]{1,0:T(8,128)(2,1)S(1)} %bitcast.74), channel_id=1, source_target_pairs={{0,1},{1,0},{2,3},{3,2},{4,5},{5,4},{6,7},{7,6},{8,9},{9,8},{10,11... | collective-permute-start | bytes 5505032 | tf_op jit(solution)/shard_map/ppermute | solution.py:30
  28.0 7.8 %collective-permute-start.2 = (bf16[320,512]{1,0:T(8,128)(2,1)S(1)}, bf16[320,512]{1,0:T(8,128)(2,1)S(1)}, u32[]{:S(2)}, u32[]{:S(2)}) collective-permute-start(bf16[320,512]{1,0:T(8,128)(2,1)S(1)} %pad_maximum_fusion.4), channel_id=1, source_target_pairs={{0,64},{1,17},{2,66},{3,19},{4,68},{5,21},{6,70},{7,23},{8,72},{9,... | collective-permute-start | bytes 983048 | tf_op jit(solution)/shard_map/ppermute | solution.py:30
  31.0 8.7 %collective-permute-start.1 = (bf16[320,512]{1,0:T(8,128)(2,1)S(1)}, bf16[320,512]{1,0:T(8,128)(2,1)S(1)}, u32[]{:S(2)}, u32[]{:S(2)}) collective-permute-start(bf16[320,512]{1,0:T(8,128)(2,1)S(1)} %pad_maximum_fusion.4), channel_id=1, source_target_pairs={{0,96},{1,25},{2,98},{3,27},{4,100},{5,29},{6,102},{7,31},{8,104},... | collective-permute-start | bytes 983048 | tf_op jit(solution)/shard_map/ppermute | solution.py:30
  31.8 7.9 %collective-permute-start = (bf16[320,512]{1,0:T(8,128)(2,1)S(1)}, bf16[320,512]{1,0:T(8,128)(2,1)S(1)}, u32[]{:S(2)}, u32[]{:S(2)}) collective-permute-start(bf16[320,512]{1,0:T(8,128)(2,1)S(1)} %pad_maximum_fusion.4), channel_id=1, source_target_pairs={{0,32},{1,9},{2,34},{3,11},{4,36},{5,13},{6,38},{7,15},{8,40},{9,1... | collective-permute-start | bytes 983048 | tf_op jit(solution)/shard_map/ppermute | solution.py:30
  39.7 4.5 %copy-start.4 = (bf16[3,32,2,1536]{3,1,2,0:T(8,128)(2,1)S(1)}, bf16[3,32,2,1536]{3,1,2,0:T(8,128)(2,1)}, u32[]{:S(2)}) copy-start(bf16[3,32,2,1536]{3,1,2,0:T(8,128)(2,1)} %pad_maximum_fusion.2) | copy-start | bytes 1769476
  39.9 20.9 %collective-permute-start.6 = (bf16[4,320,512]{2,1,0:T(8,128)(2,1)S(1)}, bf16[4,320,512]{2,1,0:T(8,128)(2,1)}, u32[]{:S(2)}, u32[]{:S(2)}) collective-permute-start(bf16[4,320,512]{2,1,0:T(8,128)(2,1)S(1)} %pad_maximum_fusion.1.refs_0_), channel_id=1, source_target_pairs={{0,16},{1,65},{2,18},{3,67},{4,20},{5,69},{6,22},{7,71},{8,24},{9,... | collective-permute-start | bytes 3932168 | tf_op jit(solution)/shard_map/ppermute | solution.py:30
  42.7 36.1 %collective-permute-start.5 = (bf16[4,320,512]{2,1,0:T(8,128)(2,1)S(1)}, bf16[4,320,512]{2,1,0:T(8,128)(2,1)}, u32[]{:S(2)}, u32[]{:S(2)}) collective-permute-start(bf16[4,320,512]{2,1,0:T(8,128)(2,1)S(1)} %pad_maximum_fusion.1.refs_0_), channel_id=1, source_target_pairs={{0,24},{1,97},{2,26},{3,99},{4,28},{5,101},{6,30},{7,103},{8,0},{9... | collective-permute-start | bytes 3932168 | tf_op jit(solution)/shard_map/ppermute | solution.py:30
  43.6 43.0 %collective-permute-start.3 = (bf16[4,320,512]{2,1,0:T(8,128)(2,1)S(1)}, bf16[4,320,512]{2,1,0:T(8,128)(2,1)}, u32[]{:S(2)}, u32[]{:S(2)}) collective-permute-start(bf16[4,320,512]{2,1,0:T(8,128)(2,1)S(1)} %pad_maximum_fusion.1.refs_0_), channel_id=1, source_target_pairs={{0,8},{1,33},{2,10},{3,35},{4,12},{5,37},{6,14},{7,39},{8,16},{9,4... | collective-permute-start | bytes 3932168 | tf_op jit(solution)/shard_map/ppermute | solution.py:30
  45.4 41.2 %all-to-all-start.1 = ((bf16[32,6,1536]{2,1,0:T(8,128)(2,1)}), bf16[32,6,1536]{2,1,0:T(8,128)(2,1)}, u32[]{:S(2)}, u32[]{:S(2)}) async-start(bf16[32,6,1536]{2,1,0:T(8,128)(2,1)} %copy.39), calls=%async_computation.1 | async-start | bytes 1572864 | tf_op jit(solution)/shard_map/all_to_all | solution.py:308
  52.4 36.0 %collective-permute-start.7 = (bf16[4,320,512]{2,1,0:T(8,128)(2,1)S(1)}, bf16[4,320,512]{2,1,0:T(8,128)(2,1)}, u32[]{:S(2)}, u32[]{:S(2)}) collective-permute-start(bf16[4,320,512]{2,1,0:T(8,128)(2,1)S(1)} %pad_maximum_fusion.1.refs_0_), channel_id=1, source_target_pairs={{0,1},{1,0},{2,3},{3,2},{4,5},{5,4},{6,7},{7,6},{8,9},{9,8},{10,11... | collective-permute-start | bytes 3932168 | tf_op jit(solution)/shard_map/ppermute | solution.py:30
  60.8 27.7 %collective-permute-start.10 = (bf16[4,320,512]{2,1,0:T(8,128)(2,1)}, bf16[4,320,512]{2,1,0:T(8,128)(2,1)}, u32[]{:S(2)}, u32[]{:S(2)}) collective-permute-start(bf16[4,320,512]{2,1,0:T(8,128)(2,1)} %collective-permute-done.6.refs_3_), channel_id=1, source_target_pairs={{0,1},{1,0},{2,3},{3,2},{4,5},{5,4},{6,7},{7,6},{8,9},{9,8},{10,11... | collective-permute-start | bytes 3932168 | tf_op jit(solution)/shard_map/ppermute | solution.py:30
  78.8 9.6 %collective-permute-start.9 = (bf16[4,320,512]{2,1,0:T(8,128)(2,1)}, bf16[4,320,512]{2,1,0:T(8,128)(2,1)}, u32[]{:S(2)}, u32[]{:S(2)}) collective-permute-start(bf16[4,320,512]{2,1,0:T(8,128)(2,1)} %collective-permute-done.5.refs_2_), channel_id=1, source_target_pairs={{0,1},{1,0},{2,3},{3,2},{4,5},{5,4},{6,7},{7,6},{8,9},{9,8},{10,11... | collective-permute-start | bytes 3932168 | tf_op jit(solution)/shard_map/ppermute | solution.py:30
  86.6 3.4 %collective-permute-start.8 = (bf16[4,320,512]{2,1,0:T(8,128)(2,1)}, bf16[4,320,512]{2,1,0:T(8,128)(2,1)}, u32[]{:S(2)}, u32[]{:S(2)}) collective-permute-start(bf16[4,320,512]{2,1,0:T(8,128)(2,1)} %collective-permute-done.3.refs_1_), channel_id=1, source_target_pairs={{0,1},{1,0},{2,3},{3,2},{4,5},{5,4},{6,7},{7,6},{8,9},{9,8},{10,11... | collective-permute-start | bytes 3932168 | tf_op jit(solution)/shard_map/ppermute | solution.py:30
  100.7 0.8 copy-start.1
  101.6 1.0 copy-start.2
  102.6 8.3 %collective-permute-start.11 = (bf16[256,2304]{1,0:T(8,128)(2,1)}, bf16[256,2304]{1,0:T(8,128)(2,1)}, u32[]{:S(2)}, u32[]{:S(2)}) collective-permute-start(bf16[256,2304]{1,0:T(8,128)(2,1)} %get-tuple-element.24), channel_id=1, source_target_pairs={{0,1},{1,0},{2,3},{3,2},{4,5},{5,4},{6,7},{7,6},{8,9},{9,8},{10,11... | collective-permute-start | bytes 3538952 | tf_op jit(solution)/shard_map/ppermute | solution.py:30
  102.7 8.2 %copy-start = (bf16[3584,512]{1,0:T(8,128)(2,1)S(1)}, bf16[3584,512]{1,0:T(8,128)(2,1)}, u32[]{:S(2)}) copy-start(bf16[3584,512]{1,0:T(8,128)(2,1)} %pad_maximum_fusion.lat_ref) | copy-start | bytes 11010052
  110.9 1.3 copy-start.3
  122.4 18.0 %collective-permute-start.12 = (bf16[4,320,512]{2,1,0:T(8,128)(2,1)S(1)}, bf16[4,320,512]{2,1,0:T(8,128)(2,1)S(1)}, u32[]{:S(2)}, u32[]{:S(2)}) collective-permute-start(bf16[4,320,512]{2,1,0:T(8,128)(2,1)S(1)} %get-tuple-element.32), channel_id=1, source_target_pairs={{0,8},{1,33},{2,10},{3,35},{4,12},{5,37},{6,14},{7,39},{8,16},{9,4... | collective-permute-start | bytes 3932168 | tf_op jit(solution)/shard_map/ppermute | solution.py:30
  123.5 30.3 %collective-permute-start.13 = (bf16[4,320,512]{2,1,0:T(8,128)(2,1)S(1)}, bf16[4,320,512]{2,1,0:T(8,128)(2,1)S(1)}, u32[]{:S(2)}, u32[]{:S(2)}) collective-permute-start(bf16[4,320,512]{2,1,0:T(8,128)(2,1)S(1)} %get-tuple-element.33), channel_id=1, source_target_pairs={{0,24},{1,97},{2,26},{3,99},{4,28},{5,101},{6,30},{7,103},{8,0},{9... | collective-permute-start | bytes 3932168 | tf_op jit(solution)/shard_map/ppermute | solution.py:30
  125.2 29.8 %collective-permute-start.14 = (bf16[4,320,512]{2,1,0:T(8,128)(2,1)S(1)}, bf16[4,320,512]{2,1,0:T(8,128)(2,1)S(1)}, u32[]{:S(2)}, u32[]{:S(2)}) collective-permute-start(bf16[4,320,512]{2,1,0:T(8,128)(2,1)S(1)} %get-tuple-element.34), channel_id=1, source_target_pairs={{0,16},{1,65},{2,18},{3,67},{4,20},{5,69},{6,22},{7,71},{8,24},{9,... | collective-permute-start | bytes 3932168 | tf_op jit(solution)/shard_map/ppermute | solution.py:30
  155.5 7.5 %collective-permute-start.15 = (bf16[320,512]{1,0:T(8,128)(2,1)S(1)}, bf16[320,512]{1,0:T(8,128)(2,1)S(1)}, u32[]{:S(2)}, u32[]{:S(2)}) collective-permute-start(bf16[320,512]{1,0:T(8,128)(2,1)S(1)} %get-tuple-element.35), channel_id=1, source_target_pairs={{0,32},{1,9},{2,34},{3,11},{4,36},{5,13},{6,38},{7,15},{8,40},{9,1... | collective-permute-start | bytes 983048 | tf_op jit(solution)/shard_map/ppermute | solution.py:30
  155.9 11.4 %collective-permute-start.17 = (bf16[320,512]{1,0:T(8,128)(2,1)S(1)}, bf16[320,512]{1,0:T(8,128)(2,1)S(1)}, u32[]{:S(2)}, u32[]{:S(2)}) collective-permute-start(bf16[320,512]{1,0:T(8,128)(2,1)S(1)} %get-tuple-element.36), channel_id=1, source_target_pairs={{0,64},{1,17},{2,66},{3,19},{4,68},{5,21},{6,70},{7,23},{8,72},{9,... | collective-permute-start | bytes 983048 | tf_op jit(solution)/shard_map/ppermute | solution.py:30
  159.1 8.3 %collective-permute-start.16 = (bf16[320,512]{1,0:T(8,128)(2,1)S(1)}, bf16[320,512]{1,0:T(8,128)(2,1)S(1)}, u32[]{:S(2)}, u32[]{:S(2)}) collective-permute-start(bf16[320,512]{1,0:T(8,128)(2,1)S(1)} %get-tuple-element.37), channel_id=1, source_target_pairs={{0,96},{1,25},{2,98},{3,27},{4,100},{5,29},{6,102},{7,31},{8,104},... | collective-permute-start | bytes 983048 | tf_op jit(solution)/shard_map/ppermute | solution.py:30

commit v3 on v2

v3 whole, which is shorter than its diff:
```python
import jax
import jax.numpy as jnp
import numpy as np
from jax import lax
from jax.experimental import pallas as pl
from jax.experimental.pallas import tpu as pltpu
from jax.sharding import Mesh, PartitionSpec as P

loss_scale = 256.0
eps_norm = 1e-06

AXES = ("zh", "x", "y", "zl", "c")
SIZES = (2, 4, 4, 4, 2)
D, PH, DT, TOK = 3584, 1024, 1536, 256
HH, HO = PH // 2, DT // 2
ROWS_IN, ROWS_OUT = 112, 32
PACK = 320
HID = HH + HO
bf16, f32 = jnp.bfloat16, jnp.float32
NT = (((1,), (1,)), ((), ()))
TN = (((0,), (0,)), ((), ()))


def permute(v, move):
    pairs = []
    for i in range(256):
        here = [int(a) for a in np.unravel_index(i, SIZES)]
        there = [a % s for a, s in zip(move(*here), SIZES)]
        pairs.append((i, int(np.ravel_multi_index(there, SIZES))))
    return lax.ppermute(v, AXES, pairs)


def first_axis(v, d):
    return permute(
        v, lambda zh, x, y, zl, c: (zh, x + d * (c == 0), y + d * (c == 1), zl, c)
    )


def second_axis(v, d):
    return permute(
        v, lambda zh, x, y, zl, c: (zh, x + d * (c == 1), y + d * (c == 0), zl, c)
    )


def swap_cores(v):
    return permute(v, lambda zh, x, y, zl, c: (zh, x, y, zl, 1 - c))


def place_of(core, x, y, d3, d2):
    sx = lax.rem(x + jnp.where(core == 0, d2, d3), 4)
    sy = lax.rem(y + jnp.where(core == 0, d3, d2), 4)
    return sx, sy


SHIFTS = (0, 1, 3, 2)
PIECES = ((0, 0, 512), (1, 0, 256), (3, 256, 256), (1, 256, 256), (3, 0, 256), (2, 0, 256), (2, 256, 256))


def head_kernel(place, latent, picked, expand, *refs):
    own, oth = refs[0:7], refs[7:14]
    grad_pre_ref, keep_ref, give_ref, w_in_out = refs[14:18]
    w_in, w_out, pre, pred, gpred, sems = refs[18:]
    x, y, c = place[0], place[1], place[2]

    def fetch(pieces, core, sem_in, sem_out):
        for ref, (d3, left, wide) in zip(pieces, PIECES):
            for j, d2 in enumerate(SHIFTS):
                sx, sy = place_of(core, x, y, 4 - d3, 4 - d2)
                b = sx * 4 + sy
                src = ref.at[j]

                def bring(rows, cols, dst, sem):
                    pltpu.make_async_copy(src.at[rows, cols], dst, sems.at[sem]).start()

                def lane(first, start, size):
                    return pl.ds(pl.multiple_of(first + start, 256), size)

                every = pl.ds(0, wide)
                bring(
                    pl.ds(0, 224),
                    every,
                    w_in.at[b, :, lane(core * HH, left, wide)],
                    sem_in,
                )
                bring(
                    pl.ds(224, 64),
                    every,
                    w_out.at[b, :, lane(core * HO, left, wide)],
                    sem_out,
                )
                for at in range(0, wide, 256):
                    zh = (left + at) // 256
                    bring(
                        pl.ds(288, 32),
                        pl.ds(at, 256),
                        w_out.at[b, pl.ds(zh * 32, 32), lane(core * HO, 512, 256)],
                        sem_out,
                    )

    fetch(own, c, 0, 2)
    fetch(oth, 1 - c, 1, 2)
    goal = jnp.dot(expand[...], picked[...], preferred_element_type=f32)
    norm_goal = jnp.sqrt(jnp.sum(goal * goal, axis=1, keepdims=True) + eps_norm)
    half = w_in.at[:, :, pl.ds(0, HH)]
    for core, sem in ((c, 0), (1 - c, 1)):
        pltpu.make_async_copy(half, half, sems.at[sem]).wait()
        for j in range(2):
            cols = pl.ds(pl.multiple_of(core * HH + j * 256, 256), 256)
            part = jnp.zeros((TOK, 256), f32)
            for zh in range(2):
                part += jnp.dot(
                    latent[:, zh * 1792 : (zh + 1) * 1792],
                    w_in[:, zh * ROWS_IN : (zh + 1) * ROWS_IN, cols].reshape(1792, 256),
                    preferred_element_type=f32,
                )
            pre[:, cols] = part
            keep_ref[:, pl.ds(pl.multiple_of(HID + core * HH + j * 256, 256), 256)] = (
                part * jax.nn.sigmoid(part)
            ).astype(bf16)
    save = pltpu.make_async_copy(w_in, w_in_out, sems.at[3])
    save.start()
    pltpu.make_async_copy(w_out, w_out, sems.at[2]).wait()
    for j in range(6):
        cols = slice(j * 256, (j + 1) * 256)
        part = jnp.zeros((TOK, 256), f32)
        for zh in range(2):
            part += jnp.dot(
                keep_ref[:, HID + zh * HH : HID + (zh + 1) * HH],
                w_out[:, zh * 32 : (zh + 1) * 32, cols].reshape(HH, 256),
                preferred_element_type=f32,
            )
        pred[:, cols] = part
    guess = pred[...]
    norm_pred = jnp.sqrt(jnp.sum(guess * guess, axis=1, keepdims=True) + eps_norm)
    cosv = jnp.sum(guess * goal, axis=1, keepdims=True) / (norm_pred * norm_goal)
    gpred[...] = (
        -loss_scale
        * (goal / (norm_pred * norm_goal) - cosv * guess / (norm_pred * norm_pred))
    ).astype(bf16)
    for j in range(4):
        cols = slice(j * 256, (j + 1) * 256)
        zh, b = j // 2, j % 2 * 8
        grad_hidden = lax.dot_general(
            gpred[...],
            w_out[b : b + 8, zh * 32 : (zh + 1) * 32, :].reshape(256, DT),
            NT,
            preferred_element_type=f32,
        )
        part = pre[:, cols]
        sig = jax.nn.sigmoid(part)
        grad_pre_ref[:, cols] = (
            grad_hidden * (sig * (1.0 + part * (1.0 - sig)))
        ).astype(bf16)
    for ref, core in ((keep_ref, c), (give_ref, 1 - c)):
        ref[:, :HH] = grad_pre_ref[:, pl.ds(pl.multiple_of(core * HH, HH), HH)]
        ref[:, HH:HID] = gpred[:, pl.ds(pl.multiple_of(core * HO, 256), HO)]
    give_ref[:, HID:] = keep_ref[:, HID:]
    save.wait()


def head(place, latent, picked, expand, own, oth):
    vmem = pl.BlockSpec(memory_space=pltpu.VMEM)
    hbm = pl.BlockSpec(memory_space=pl.ANY)
    return pl.pallas_call(
        head_kernel,
        in_specs=[pl.BlockSpec(memory_space=pltpu.SMEM)] + [vmem] * 3 + [hbm] * 14,
        out_specs=[vmem, vmem, vmem, hbm],
        out_shape=[
            jax.ShapeDtypeStruct((TOK, PH), bf16),
            jax.ShapeDtypeStruct((TOK, HID + PH), bf16),
            jax.ShapeDtypeStruct((TOK, HID + PH), bf16),
            jax.ShapeDtypeStruct((16, 2 * ROWS_IN, PH), bf16),
        ],
        scratch_shapes=[
            pltpu.VMEM((16, 2 * ROWS_IN, PH), bf16),
            pltpu.VMEM((16, 2 * ROWS_OUT, DT), bf16),
            pltpu.VMEM((TOK, PH), f32),
            pltpu.VMEM((TOK, DT), f32),
            pltpu.VMEM((TOK, DT), bf16),
            pltpu.SemaphoreType.DMA((4,)),
        ],
        compiler_params=pltpu.CompilerParams(vmem_limit_bytes=40 * 2**20),
        cost_estimate=pl.CostEstimate(
            flops=5_000_000_000, bytes_accessed=30_000_000, transcendentals=600_000
        ),
        name="head",
    )(place, latent, picked, expand, *own, *oth)


def tail_kernel(place, lat_a, lat_b, keep, rcv, *refs):
    outs = refs[:8]
    p_in, p_out = refs[8:]
    x, y, c = place[0], place[1], place[2]
    gpred = jnp.concatenate([keep[:, HH:HID], rcv[:, HH:HID]], axis=0)
    for zh in range(2):
        hid = slice(HID + zh * HH, HID + (zh + 1) * HH)
        hidden = jnp.concatenate([keep[:, hid], rcv[:, hid]], axis=0)
        p_out[zh * HH : (zh + 1) * HH] = lax.dot_general(
            hidden, gpred, TN, preferred_element_type=f32
        ).astype(bf16)
    for t in range(8):
        rows = slice(t * 448, (t + 1) * 448)
        p_in[rows] = (
            jnp.dot(lat_a[rows], keep[:, :HH], preferred_element_type=f32)
            + jnp.dot(lat_b[rows], rcv[:, :HH], preferred_element_type=f32)
        ).astype(bf16)
    for d3 in range(4):
        for d2 in range(4):
            sx, sy = place_of(c, x, y, d3, d2)
            b = sx * 4 + sy
            for zh in range(2):
                top = pl.ds(pl.multiple_of((zh * 16 + b) * ROWS_IN, 16), ROWS_IN)
                low = pl.ds(pl.multiple_of((zh * 16 + b) * ROWS_OUT, 32), ROWS_OUT)
                for h in range(2):
                    out = outs[d3 * 2 + h]
                    cols = slice(h * 256, (h + 1) * 256)
                    out[d2, zh * ROWS_IN : (zh + 1) * ROWS_IN] = p_in[top, cols]
                    out[d2, 224 + zh * 32 : 256 + zh * 32] = p_out[low, cols]
                outs[d3 * 2 + zh][d2, 288:320] = p_out[low, 512:768]


def tail(place, lat_a, lat_b, keep, rcv):
    vmem = pl.BlockSpec(memory_space=pltpu.VMEM)
    return pl.pallas_call(
        tail_kernel,
        in_specs=[pl.BlockSpec(memory_space=pltpu.SMEM)] + [vmem] * 4,
        out_specs=[vmem] * 8,
        out_shape=[jax.ShapeDtypeStruct((4, PACK, 256), bf16)] * 8,
        scratch_shapes=[pltpu.VMEM((D, HH), bf16), pltpu.VMEM((PH, HO), bf16)],
        compiler_params=pltpu.CompilerParams(vmem_limit_bytes=40 * 2**20),
        cost_estimate=pl.CostEstimate(
            flops=2_700_000_000, bytes_accessed=12_000_000, transcendentals=0
        ),
        name="tail",
    )(place, lat_a, lat_b, keep, rcv)


def back_kernel(grad_pre, w_in, out):
    out[...] = lax.dot_general(
        grad_pre[...], w_in[...].reshape(896, PH), NT, preferred_element_type=f32
    ).astype(bf16)


def back(grad_pre, w_in):
    return pl.pallas_call(
        back_kernel,
        grid=(4,),
        in_specs=[
            pl.BlockSpec((TOK, PH), lambda i: (0, 0)),
            pl.BlockSpec((8, ROWS_IN, PH), lambda i: (i % 2, i // 2, 0)),
        ],
        out_specs=pl.BlockSpec((TOK, 896), lambda i: (0, i)),
        out_shape=jax.ShapeDtypeStruct((TOK, D), bf16),
        compiler_params=pltpu.CompilerParams(vmem_limit_bytes=32 * 2**20),
        cost_estimate=pl.CostEstimate(
            flops=1_900_000_000, bytes_accessed=10_000_000, transcendentals=0
        ),
        name="back",
    )(grad_pre, w_in)


def add(*terms):
    return sum(t.astype(f32) for t in terms).astype(bf16)


def per_device(latent, targets, index_map, proj_in, proj_out):
    x, y, c = lax.axis_index("x"), lax.axis_index("y"), lax.axis_index("c")
    place = jnp.stack([x, y, c]).astype(jnp.int32)

    halves = jnp.concatenate(
        [
            proj_in.reshape(14, 2, HH).transpose(1, 0, 2),
            proj_out.reshape(4, 2, HO).transpose(1, 0, 2).reshape(2, 6, HH),
        ],
        axis=1,
    )
    fan = jnp.broadcast_to(halves[None], (8, 2, 20, HH)).reshape(16, 20, HH)
    column = lax.all_to_all(
        fan, ("zh", "zl", "c"), split_axis=0, concat_axis=0, tiled=True
    )
    rows_in = column[:, :14].reshape(224, HH)
    rows_out = column[:, 14:].reshape(16, 4, HO).reshape(2, ROWS_OUT, HO)
    packed = jnp.concatenate(
        [
            rows_in,
            rows_out[:, :, :512].reshape(64, 512),
            rows_out[:, :, 512:].transpose(1, 0, 2).reshape(32, 512),
        ],
        axis=0,
    )
    maps = index_map[0]
    width = targets.shape[2] * 32
    row_of = maps[:, 0] // width
    slab = targets[0].transpose(1, 0, 2)
    pick = (row_of[:, None] == jnp.arange(48, dtype=jnp.int32)[None]).astype(bf16)
    sent = jnp.stack(
        [jnp.dot(pick, slab[t], preferred_element_type=f32).astype(bf16) for t in range(3)]
    )
    sent = sent.reshape(3, 32, 2, DT).transpose(1, 0, 2, 3).reshape(32, 6, DT)
    lat_t = latent[0].T
    packed, sent, lat_t = lax.optimization_barrier((packed, sent, lat_t))
    got = lax.all_to_all(
        sent, ("zh", "x", "y"), split_axis=0, concat_axis=0, tiled=True
    )
    picked = got.reshape(192, DT)
    line = jnp.stack([packed] + [first_axis(packed, d) for d in SHIFTS[1:]])
    lat_o = swap_cores(lat_t)
    left, right = lax.optimization_barrier((line[..., :256], line[..., 256:]))
    left1, right3 = second_axis(left, 1), second_axis(right, 3)
    right1, left3 = second_axis(right, 1), second_axis(left, 3)
    left2, right2 = second_axis(left1, 1), second_axis(right3, 3)
    col_of = (maps[0] % width).reshape(32, 4) - 3 * jnp.arange(32, dtype=jnp.int32)[:, None]
    token = jnp.arange(TOK, dtype=jnp.int32)[:, None]
    row = jnp.arange(192, dtype=jnp.int32)[None]
    want = ((token // 4) % 32) * 6 + jnp.tile(col_of.reshape(128), 2)[:, None] * 2 + token // 128
    expand = (row == want).astype(bf16)

    right2, picked, expand = lax.optimization_barrier((right2, picked, expand))
    own = [line, left1, right3, right1, left3, left2, right2]
    oth = [swap_cores(v) for v in own]

    grad_pre, keep, give, w_in = head(place, latent[0], picked, expand, own, oth)
    rcv = swap_cores(give)
    sums = tail(place, lat_t, lat_o, keep, rcv)
    lefts, rights = sums[0::2], sums[1::2]
    via_left, via_right = second_axis(lefts[2], 1), second_axis(rights[2], 3)
    rights1, lefts3 = second_axis(rights[1], 1), second_axis(lefts[3], 3)
    lefts1 = second_axis(add(lefts[1], via_left), 1)
    rights3 = second_axis(add(rights[3], via_right), 3)
    grad_latent = back(grad_pre, w_in)
    lefts1, grad_latent = lax.optimization_barrier((lefts1, grad_latent))
    line_sum = [
        jnp.concatenate(
            [
                add(lefts[0][k], lefts1[k], lefts3[k]),
                add(rights[0][k], rights1[k], rights3[k]),
            ],
            axis=1,
        )
        for k in range(4)
    ]
    got2 = [first_axis(line_sum[d], d) for d in SHIFTS[1:]]
    mine = add(line_sum[0], *got2)
    g_in = mine[:224].reshape(16, 14, HH)
    g_out = jnp.concatenate(
        [
            mine[224:288].reshape(2, 32, 512),
            mine[288:].reshape(32, 2, 256).transpose(1, 0, 2),
        ],
        axis=2,
    ).reshape(16, 4, HO).reshape(16, 6, HH)
    last = lax.all_to_all(
        jnp.concatenate([g_in, g_out], axis=1),
        ("zh", "zl", "c"), split_axis=0, concat_axis=0, tiled=True,
    )
    total = jnp.sum(last.reshape(8, 2, 20, HH).astype(f32), axis=0)
    grad_in = total[:, :14].transpose(1, 0, 2).reshape(14, PH)
    grad_out = total[:, 14:].reshape(2, 4, HO).transpose(1, 0, 2).reshape(4, DT)
    return grad_latent[None], grad_in, grad_out


def solution(mesh):
    fine = Mesh(mesh.devices.reshape(SIZES), AXES)
    seq, fsdp = ("zh", "x", "y"), ("zl", "c")
    rows = P(AXES, None)
    return jax.shard_map(
        per_device,
        mesh=fine,
        in_specs=(P(fsdp, seq, None), P(fsdp, None, seq, None), P(fsdp, None, None), rows, rows),
        out_specs=(P(fsdp, seq, None), rows, rows),
        check_vma=False,
    )
```

time: 189 us -> 167 us (0.88)
  waiting for transfers between devices: 77.5 us -> 56.2 us
  Pallas kernels: 29.2 us -> 18.9 us
  starting transfers between devices: 41.7 us -> 50.3 us
  blocking collectives: 19.4 us -> 23.8 us
  other arithmetic: 6.17 us -> 2.65 us
    ppermute x18 -> x27, waiting for transfers between devices: 68 us -> 46.7 us  [permute(): return lax.ppermute(v, AXES, pairs)]
    ppermute x18 -> x27, starting transfers between devices: 24.7 us -> 32.7 us  [permute(): return lax.ppermute(v, AXES, pairs)]
    pallas_call x1, Pallas kernels: 10.2 us -> 4.94 us  [tail(): pl.pallas_call(tail_kernel, in_specs=[pl.BlockSpec(memory_space=pltpu.SME...]
    all_to_all x1, blocking collectives: 19.4 us -> 23.8 us  [per_device(): lax.all_to_all(jnp.concatenate([g_in, g_out], axis=1), ('zh', 'zl', 'c'),...]
    pallas_call x1, Pallas kernels: 8.19 us -> 4.33 us  [back(): pl.pallas_call(back_kernel, grid=(4,), in_specs=[pl.BlockSpec((TOK, PH),...]
    concatenate x1 -> x3, other arithmetic: 3.7 us -> 0.07 us  [per_device(): jnp.concatenate([add(lefts[0][k], lefts1[k], lefts3[k]), add(rights[0][k]...]
    unnamed x18 -> x14, local copies, waits for them, and re-layouts: 6.66 us -> 4.64 us
  transfers between devices with their start and end apart: 20 -> 29, of which waited for: 11 -> 12; matrix products, arithmetic and copies ran while one was open for 6% -> 6% of each run, Pallas kernels for 4% -> 8%
where the time goes in v3:
time: 167 us
  waiting for transfers between devices  56.2 us (34%)
  starting transfers between devices  50.3 us (30%)
  blocking collectives  23.8 us (14%)
  Pallas kernels  18.9 us (11%)
  local copies, waits for them, and re-layouts  13 us (8%)
  other arithmetic  2.65 us (2%)
    ppermute x27, waiting for transfers between devices, permute(): return lax.ppermute(v, AXES, pairs)  46.7 us
    ppermute x27, starting transfers between devices, permute(): return lax.ppermute(v, AXES, pairs)  32.7 us
    all_to_all x1, blocking collectives, per_device(): lax.all_to_all(jnp.concatenate([g_in, g_out], axis=1), ('zh', 'zl', 'c'),...  23.8 us
    all_to_all x1, starting transfers between devices, per_device(): lax.all_to_all(fan, ('zh', 'zl', 'c'), split_axis=0, concat_axis=0, tiled...  9.98 us
    pallas_call x1, Pallas kernels, head(): pl.pallas_call(head_kernel, in_specs=[pl.BlockSpec(memory_space=pltpu.SME...  9.64 us
    all_to_all x1, waiting for transfers between devices, per_device(): lax.all_to_all(fan, ('zh', 'zl', 'c'), split_axis=0, concat_axis=0, tiled...  9.53 us
    all_to_all x1, starting transfers between devices, per_device(): lax.all_to_all(sent, ('zh', 'x', 'y'), split_axis=0, concat_axis=0, tiled...  7.61 us
    pallas_call x1, Pallas kernels, tail(): pl.pallas_call(tail_kernel, in_specs=[pl.BlockSpec(memory_space=pltpu.SME...  4.94 us
  transfers between devices with their start and end apart: 29, of which 12 were waited for; matrix products, arithmetic and copies ran while one was open for 6% of the time, Pallas kernels for 8%

profile of v3, /device:TPU:1, one launch (start us, length us, event | category | flops | bytes accessed | tf_op | source)
XLA Modules:
  0.0 166.7 jit_solution(3482332427631596509)
XLA Ops:
  0.7 0.8 reshape.239
  1.4 0.8 reshape.238
  2.3 0.8 broadcast_in_dim.4
  3.1 10.0 %all-to-all-start = ((bf16[16,20,512]{2,1,0:T(8,128)(2,1)}), bf16[16,20,512]{2,1,0:T(8,128)(2,1)S(1)}, u32[]{:S(2)}, u32[]{:S(2)}) async-start(bf16[16,20,512]{2,1,0:T(8,128)(2,1)} %bitcast.6), calls=%async_computation | async-start | bytes 786432 | tf_op jit(solution)/shard_map/all_to_all | solution.py:278
  13.1 0.1 fusion.9
  13.2 0.2 convolution_convert_fusion
  13.6 0.2 convolution_convert_fusion.1
  13.9 0.2 convolution_convert_fusion.2
  14.3 2.9 %copy.38 = bf16[1,256,3584]{1,2,0:T(8,128)(2,1)S(1)} copy(bf16[1,256,3584]{2,1,0:T(8,128)(2,1)} %param.5) | data formatting | bytes 3670016 | tf_op args[0]
  17.2 0.9 pad_maximum_fusion.1
  18.1 9.5 %all-to-all-done = bf16[16,20,512]{2,1,0:T(8,128)(2,1)S(1)} async-done(((bf16[16,20,512]{2,1,0:T(8,128)(2,1)}), bf16[16,20,512]{2,1,0:T(8,128)(2,1)S(1)}, u32[]{:S(2)}, u32[]{:S(2)}) %all-to-all-start) | async-done | bytes 327712 | tf_op jit(solution)/shard_map/all_to_all | solution.py:278
  27.9 3.0 %collective-permute-start.3 = (bf16[320,512]{1,0:T(8,128)(2,1)S(1)}, bf16[320,512]{1,0:T(8,128)(2,1)S(1)}, u32[]{:S(2)}, u32[]{:S(2)}) collective-permute-start(bf16[320,512]{1,0:T(8,128)(2,1)S(1)} %pad_maximum_fusion.3), channel_id=1, source_target_pairs={{0,64},{1,17},{2,66},{3,19},{4,68},{5,21},{6,70},{7,23},{8,72},{9,... | collective-permute-start | bytes 983048 | tf_op jit(solution)/shard_map/ppermute | solution.py:30
  30.9 0.8 collective-permute-start.2
  31.7 0.7 collective-permute-start.1
  32.4 3.1 %collective-permute-done.3 = bf16[320,512]{1,0:T(8,128)(2,1)S(1)} collective-permute-done((bf16[320,512]{1,0:T(8,128)(2,1)S(1)}, bf16[320,512]{1,0:T(8,128)(2,1)S(1)}, u32[]{:S(2)}, u32[]{:S(2)}) %collective-permute-start.3) | collective-permute-done | bytes 327712 | tf_op jit(solution)/shard_map/ppermute | solution.py:30
  35.4 3.9 %collective-permute-done.2 = bf16[320,512]{1,0:T(8,128)(2,1)S(1)} collective-permute-done((bf16[320,512]{1,0:T(8,128)(2,1)S(1)}, bf16[320,512]{1,0:T(8,128)(2,1)S(1)}, u32[]{:S(2)}, u32[]{:S(2)}) %collective-permute-start.2) | collective-permute-done | bytes 327712 | tf_op jit(solution)/shard_map/ppermute | solution.py:30
  39.3 0.2 pad_maximum_fusion.refs_0_
  39.5 1.2 fusion.21
  40.7 2.5 %collective-permute-start.4 = (bf16[4,320,256]{2,1,0:T(8,128)(2,1)}, bf16[4,320,256]{2,1,0:T(8,128)(2,1)}, u32[]{:S(2)}, u32[]{:S(2)}) collective-permute-start(bf16[4,320,256]{2,1,0:T(8,128)(2,1)} %get-tuple-element.27), channel_id=1, source_target_pairs={{0,24},{1,97},{2,26},{3,99},{4,28},{5,101},{6,30},{7,103},{8,0},{9... | collective-permute-start | bytes 1966088 | tf_op jit(solution)/shard_map/ppermute | solution.py:30
  43.2 2.7 %collective-permute-start.8 = (bf16[4,320,256]{2,1,0:T(8,128)(2,1)}, bf16[4,320,256]{2,1,0:T(8,128)(2,1)}, u32[]{:S(2)}, u32[]{:S(2)}) collective-permute-start(bf16[4,320,256]{2,1,0:T(8,128)(2,1)} %get-tuple-element.31), channel_id=1, source_target_pairs={{0,24},{1,97},{2,26},{3,99},{4,28},{5,101},{6,30},{7,103},{8,0},{9... | collective-permute-start | bytes 1966088 | tf_op jit(solution)/shard_map/ppermute | solution.py:30
  45.8 1.2 copy.39
  47.1 7.6 %all-to-all-start.1 = ((bf16[32,6,1536]{2,1,0:T(8,128)(2,1)}), bf16[32,6,1536]{2,1,0:T(8,128)(2,1)}, u32[]{:S(2)}, u32[]{:S(2)}) async-start(bf16[32,6,1536]{2,1,0:T(8,128)(2,1)} %copy.39), calls=%async_computation.1 | async-start | bytes 1572864 | tf_op jit(solution)/shard_map/all_to_all | solution.py:302
  54.7 2.5 %collective-permute-start.5 = (bf16[4,320,256]{2,1,0:T(8,128)(2,1)}, bf16[4,320,256]{2,1,0:T(8,128)(2,1)}, u32[]{:S(2)}, u32[]{:S(2)}) collective-permute-start(bf16[4,320,256]{2,1,0:T(8,128)(2,1)} %collective-permute-done.4.refs_2_), channel_id=1, source_target_pairs={{0,24},{1,97},{2,26},{3,99},{4,28},{5,101},{6,30},{7,103},{8,0},{9... | collective-permute-start | bytes 1966088 | tf_op jit(solution)/shard_map/ppermute | solution.py:30
  57.2 0.1 sub.33
  57.3 3.4 %collective-permute-start.10 = (bf16[4,320,512]{2,1,0:T(8,128)(2,1)S(1)}, bf16[4,320,512]{2,1,0:T(8,128)(2,1)}, u32[]{:S(2)}, u32[]{:S(2)}) collective-permute-start(bf16[4,320,512]{2,1,0:T(8,128)(2,1)S(1)} %pad_maximum_fusion.refs_0_), channel_id=1, source_target_pairs={{0,1},{1,0},{2,3},{3,2},{4,5},{5,4},{6,7},{7,6},{8,9},{9,8},{10,11... | collective-permute-start | bytes 3932168 | tf_op jit(solution)/shard_map/ppermute | solution.py:30
  60.7 0.1 collective-permute-start.12
  60.8 0.4 collective-permute-start.13
  61.2 1.8 %collective-permute-done.6.refs_1_ = bf16[4,320,256]{2,1,0:T(8,128)(2,1)} collective-permute-done((bf16[4,320,256]{2,1,0:T(8,128)(2,1)}, bf16[4,320,256]{2,1,0:T(8,128)(2,1)}, u32[]{:S(2)}, u32[]{:S(2)}) %collective-permute-start.6) | collective-permute-done | bytes 655392 | tf_op jit(solution)/shard_map/ppermute | solution.py:30
  63.0 1.5 collective-permute-start.9
  64.5 9.0 %collective-permute-done.5.refs_6_ = bf16[4,320,256]{2,1,0:T(8,128)(2,1)} collective-permute-done((bf16[4,320,256]{2,1,0:T(8,128)(2,1)}, bf16[4,320,256]{2,1,0:T(8,128)(2,1)}, u32[]{:S(2)}, u32[]{:S(2)}) %collective-permute-start.5) | collective-permute-done | bytes 655392 | tf_op jit(solution)/shard_map/ppermute | solution.py:30
  73.5 1.8 %collective-permute-start.14 = (bf16[4,320,256]{2,1,0:T(8,128)(2,1)}, bf16[4,320,256]{2,1,0:T(8,128)(2,1)}, u32[]{:S(2)}, u32[]{:S(2)}) collective-permute-start(bf16[4,320,256]{2,1,0:T(8,128)(2,1)} %collective-permute-done.8.refs_4_), channel_id=1, source_target_pairs={{0,1},{1,0},{2,3},{3,2},{4,5},{5,4},{6,7},{7,6},{8,9},{9,8},{10,11... | collective-permute-start | bytes 1966088 | tf_op jit(solution)/shard_map/ppermute | solution.py:30
  75.2 0.1 fusion.expand
  75.4 2.1 %reshape.246.picked = bf16[192,1536]{1,0:T(8,128)(2,1)} reshape(bf16[32,6,1536]{2,1,0:T(8,128)(2,1)} %all-to-all-done.1) | data formatting | bytes 1179648 | tf_op jit(solution)/shard_map/reshape | solution.py:305
  77.4 2.5 %collective-permute-start.11 = (bf16[4,320,256]{2,1,0:T(8,128)(2,1)}, bf16[4,320,256]{2,1,0:T(8,128)(2,1)}, u32[]{:S(2)}, u32[]{:S(2)}) collective-permute-start(bf16[4,320,256]{2,1,0:T(8,128)(2,1)} %collective-permute-done.6.refs_1_), channel_id=1, source_target_pairs={{0,1},{1,0},{2,3},{3,2},{4,5},{5,4},{6,7},{7,6},{8,9},{9,8},{10,11... | collective-permute-start | bytes 1966088 | tf_op jit(solution)/shard_map/ppermute | solution.py:30
  79.9 0.1 collective-permute-start.16
  80.0 0.4 collective-permute-start.15
  80.4 0.1 collective-permute-start
  80.6 1.4 collective-permute-done.11.refs_8_
  82.0 1.9 %collective-permute-done.16.refs_13_ = bf16[4,320,256]{2,1,0:T(8,128)(2,1)} collective-permute-done((bf16[4,320,256]{2,1,0:T(8,128)(2,1)}, bf16[4,320,256]{2,1,0:T(8,128)(2,1)}, u32[]{:S(2)}, u32[]{:S(2)}) %collective-permute-start.16) | collective-permute-done | bytes 655392 | tf_op jit(solution)/shard_map/ppermute | solution.py:30
  83.9 1.9 %collective-permute-done.15.refs_12_ = bf16[4,320,256]{2,1,0:T(8,128)(2,1)} collective-permute-done((bf16[4,320,256]{2,1,0:T(8,128)(2,1)}, bf16[4,320,256]{2,1,0:T(8,128)(2,1)}, u32[]{:S(2)}, u32[]{:S(2)}) %collective-permute-start.15) | collective-permute-done | bytes 655392 | tf_op jit(solution)/shard_map/ppermute | solution.py:30
  85.7 1.1 copy-done.1
  86.8 9.6 %head.1 = (bf16[256,1024]{1,0:T(8,128)(2,1)S(1)}, bf16[256,2304]{1,0:T(8,128)(2,1)S(1)}, bf16[256,2304]{1,0:T(8,128)(2,1)S(1)}, bf16[16,224,1024]{2,1,0:T(8,128)(2,1)}) custom-call(s32[3]{0:T(128)S(1)} %pad_add_fusion.place, bf16[256,3584]{1,0:T(8,128)(2,1)} %bitcast.82, bf16[192,1536]{1,0:T(8,128)(2,1)S(1)} %copy-done.1, bf16[256,192]{1,0:T(8,128)(2,1)S(1)} %fusion.expand, ...), custom_call_target="tpu_custom_call" | custom-call | flops 5000000000 | bytes 30000000 | tf_op jit(solution)/shard_map/head/pallas_call | solution.py:164
  96.4 0.5 collective-permute-start.17
  96.9 2.5 %collective-permute-done.17.rcv = bf16[256,2304]{1,0:T(8,128)(2,1)S(1)} collective-permute-done((bf16[256,2304]{1,0:T(8,128)(2,1)S(1)}, bf16[256,2304]{1,0:T(8,128)(2,1)S(1)}, u32[]{:S(2)}, u32[]{:S(2)}) %collective-permute-start.17) | collective-permute-done | bytes 1179680 | tf_op jit(solution)/shard_map/ppermute | solution.py:30
  99.4 4.9 %tail.1 = (bf16[4,320,256]{2,1,0:T(8,128)(2,1)S(1)}, bf16[4,320,256]{2,1,0:T(8,128)(2,1)S(1)}, bf16[4,320,256]{2,1,0:T(8,128)(2,1)S(1)}, bf16[4,320,256]{2,1,0:T...) custom-call(s32[3]{0:T(128)S(1)} %pad_add_fusion.place, ...), custom_call_target="tpu_custom_call" | custom-call | flops 2700000000 | bytes 12000000 | tf_op jit(solution)/shard_map/tail/pallas_call | solution.py:224
  104.3 0.1 collective-permute-start.18
  104.4 2.7 %collective-permute-start.22 = (bf16[4,320,256]{2,1,0:T(8,128)(2,1)S(1)}, bf16[4,320,256]{2,1,0:T(8,128)(2,1)S(1)}, u32[]{:S(2)}, u32[]{:S(2)}) collective-permute-start(bf16[4,320,256]{2,1,0:T(8,128)(2,1)S(1)} %get-tuple-element.46), channel_id=1, source_target_pairs={{0,24},{1,97},{2,26},{3,99},{4,28},{5,101},{6,30},{7,103},{8,0},{9... | collective-permute-start | bytes 1966088 | tf_op jit(solution)/shard_map/ppermute | solution.py:30
  107.1 1.4 collective-permute-start.21
  108.5 6.8 %collective-permute-done.18 = bf16[4,320,256]{2,1,0:T(8,128)(2,1)S(1)} collective-permute-done((bf16[4,320,256]{2,1,0:T(8,128)(2,1)S(1)}, bf16[4,320,256]{2,1,0:T(8,128)(2,1)S(1)}, u32[]{:S(2)}, u32[]{:S(2)}) %collective-permute-start.18) | collective-permute-done | bytes 655392 | tf_op jit(solution)/shard_map/ppermute | solution.py:30
  115.3 0.2 add_convert_fusion.1
  115.6 0.2 add_convert_fusion
  115.8 2.7 %collective-permute-start.23 = (bf16[4,320,256]{2,1,0:T(8,128)(2,1)S(1)}, bf16[4,320,256]{2,1,0:T(8,128)(2,1)S(1)}, u32[]{:S(2)}, u32[]{:S(2)}) collective-permute-start(bf16[4,320,256]{2,1,0:T(8,128)(2,1)S(1)} %add_convert_fusion), channel_id=1, source_target_pairs={{0,24},{1,97},{2,26},{3,99},{4,28},{5,101},{6,30},{7,103},{8,0},{9... | collective-permute-start | bytes 1966088 | tf_op jit(solution)/shard_map/ppermute | solution.py:30
  118.5 4.3 %back.1 = bf16[256,3584]{1,0:T(8,128)(2,1)} custom-call(bf16[256,1024]{1,0:T(8,128)(2,1)S(1)} %get-tuple-element.37.grad_pre, bf16[16,224,1024]{2,1,0:T(8,128)(2,1)S(1)} %copy-done), custom_call_target="tpu_custom_call" | custom-call | flops 1900000000 | bytes 10000000 | tf_op jit(solution)/shard_map/back/pallas_call | solution.py:245
  122.9 6.5 %collective-permute-done.19 = bf16[4,320,256]{2,1,0:T(8,128)(2,1)S(1)} collective-permute-done((bf16[4,320,256]{2,1,0:T(8,128)(2,1)S(1)}, bf16[4,320,256]{2,1,0:T(8,128)(2,1)S(1)}, u32[]{:S(2)}, u32[]{:S(2)}) %collective-permute-start.19) | collective-permute-done | bytes 655392 | tf_op jit(solution)/shard_map/ppermute | solution.py:30
  129.4 0.2 fusion.1
  129.7 0.2 fusion.2
  130.1 2.7 %collective-permute-start.25 = (bf16[320,512]{1,0:T(8,128)(2,1)S(1)}, bf16[320,512]{1,0:T(8,128)(2,1)S(1)}, u32[]{:S(2)}, u32[]{:S(2)}) collective-permute-start(bf16[320,512]{1,0:T(8,128)(2,1)S(1)} %pad_maximum_fusion.5), channel_id=1, source_target_pairs={{0,96},{1,25},{2,98},{3,27},{4,100},{5,29},{6,102},{7,31},{8,104},... | collective-permute-start | bytes 983048 | tf_op jit(solution)/shard_map/ppermute | solution.py:30
  132.8 0.1 collective-permute-start.26
  132.9 8.0 %collective-permute-done.24 = bf16[320,512]{1,0:T(8,128)(2,1)S(1)} collective-permute-done((bf16[320,512]{1,0:T(8,128)(2,1)S(1)}, bf16[320,512]{1,0:T(8,128)(2,1)S(1)}, u32[]{:S(2)}, u32[]{:S(2)}) %collective-permute-start.24) | collective-permute-done | bytes 327712 | tf_op jit(solution)/shard_map/ppermute | solution.py:30
  141.0 0.2 add_convert_fusion.2
  141.4 0.1 pad_maximum_fusion.2
  141.5 23.8 %all_to_all.15 = bf16[16,20,512]{2,1,0:T(8,128)(2,1)S(1)} all-to-all(bf16[16,20,512]{2,1,0:T(8,128)(2,1)S(1)} %pad_maximum_fusion.2), channel_id=1, replica_groups=mesh['zh'=2,'x'=4,'y'=4,'zl'=4,'c'=2] {'zh','zl','c'}, dimensions={0} | all-to-all | bytes 655360 | tf_op jit(solution)/shard_map/all_to_all | solution.py:352
  165.4 0.6 reshape.251
  166.0 0.6 copy.46
  (67 shorter events, 1.4 us)
Async XLA Ops:
  0.6 12.4 %copy-start.4 = (s32[1,64,128]{2,1,0:T(8,128)S(1)}, s32[1,64,128]{2,1,0:T(8,128)}, u32[]{:S(2)}) copy-start(s32[1,64,128]{2,1,0:T(8,128)} %param.7) | copy-start | bytes 98308
  0.6 12.5 %copy-start.3 = (bf16[1,48,3,1536]{3,1,2,0:T(8,128)(2,1)S(1)}, bf16[1,48,3,1536]{3,1,2,0:T(8,128)(2,1)}, u32[]{:S(2)}) copy-start(bf16[1,48,3,1536]{3,1,2,0:T(8,128)(2,1)} %param.6) | copy-start | bytes 1327108
  3.1 24.5 %all-to-all-start = ((bf16[16,20,512]{2,1,0:T(8,128)(2,1)}), bf16[16,20,512]{2,1,0:T(8,128)(2,1)S(1)}, u32[]{:S(2)}, u32[]{:S(2)}) async-start(bf16[16,20,512]{2,1,0:T(8,128)(2,1)} %bitcast.6), calls=%async_computation | async-start | bytes 786432 | tf_op jit(solution)/shard_map/all_to_all | solution.py:278
  27.9 7.5 %collective-permute-start.3 = (bf16[320,512]{1,0:T(8,128)(2,1)S(1)}, bf16[320,512]{1,0:T(8,128)(2,1)S(1)}, u32[]{:S(2)}, u32[]{:S(2)}) collective-permute-start(bf16[320,512]{1,0:T(8,128)(2,1)S(1)} %pad_maximum_fusion.3), channel_id=1, source_target_pairs={{0,64},{1,17},{2,66},{3,19},{4,68},{5,21},{6,70},{7,23},{8,72},{9,... | collective-permute-start | bytes 983048 | tf_op jit(solution)/shard_map/ppermute | solution.py:30
  30.9 8.4 %collective-permute-start.2 = (bf16[320,512]{1,0:T(8,128)(2,1)S(1)}, bf16[320,512]{1,0:T(8,128)(2,1)S(1)}, u32[]{:S(2)}, u32[]{:S(2)}) collective-permute-start(bf16[320,512]{1,0:T(8,128)(2,1)S(1)} %pad_maximum_fusion.3), channel_id=1, source_target_pairs={{0,96},{1,25},{2,98},{3,27},{4,100},{5,29},{6,102},{7,31},{8,104},... | collective-permute-start | bytes 983048 | tf_op jit(solution)/shard_map/ppermute | solution.py:30
  31.7 7.6 %collective-permute-start.1 = (bf16[320,512]{1,0:T(8,128)(2,1)S(1)}, bf16[320,512]{1,0:T(8,128)(2,1)S(1)}, u32[]{:S(2)}, u32[]{:S(2)}) collective-permute-start(bf16[320,512]{1,0:T(8,128)(2,1)S(1)} %pad_maximum_fusion.3), channel_id=1, source_target_pairs={{0,32},{1,9},{2,34},{3,11},{4,36},{5,13},{6,38},{7,15},{8,40},{9,1... | collective-permute-start | bytes 983048 | tf_op jit(solution)/shard_map/ppermute | solution.py:30
  39.5 6.4 %copy-start.2 = (bf16[3,32,2,1536]{3,1,2,0:T(8,128)(2,1)S(1)}, bf16[3,32,2,1536]{3,1,2,0:T(8,128)(2,1)}, u32[]{:S(2)}) copy-start(bf16[3,32,2,1536]{3,1,2,0:T(8,128)(2,1)} %pad_maximum_fusion.1) | copy-start | bytes 1769476
  40.7 14.0 %collective-permute-start.4 = (bf16[4,320,256]{2,1,0:T(8,128)(2,1)}, bf16[4,320,256]{2,1,0:T(8,128)(2,1)}, u32[]{:S(2)}, u32[]{:S(2)}) collective-permute-start(bf16[4,320,256]{2,1,0:T(8,128)(2,1)} %get-tuple-element.27), channel_id=1, source_target_pairs={{0,24},{1,97},{2,26},{3,99},{4,28},{5,101},{6,30},{7,103},{8,0},{9... | collective-permute-start | bytes 1966088 | tf_op jit(solution)/shard_map/ppermute | solution.py:30
  43.2 17.5 %collective-permute-start.7 = (bf16[4,320,256]{2,1,0:T(8,128)(2,1)}, bf16[4,320,256]{2,1,0:T(8,128)(2,1)}, u32[]{:S(2)}, u32[]{:S(2)}) collective-permute-start(bf16[4,320,256]{2,1,0:T(8,128)(2,1)} %get-tuple-element.27), channel_id=1, source_target_pairs={{0,8},{1,33},{2,10},{3,35},{4,12},{5,37},{6,14},{7,39},{8,16},{9,4... | collective-permute-start | bytes 1966088 | tf_op jit(solution)/shard_map/ppermute | solution.py:30
  43.2 17.7 %collective-permute-start.8 = (bf16[4,320,256]{2,1,0:T(8,128)(2,1)}, bf16[4,320,256]{2,1,0:T(8,128)(2,1)}, u32[]{:S(2)}, u32[]{:S(2)}) collective-permute-start(bf16[4,320,256]{2,1,0:T(8,128)(2,1)} %get-tuple-element.31), channel_id=1, source_target_pairs={{0,24},{1,97},{2,26},{3,99},{4,28},{5,101},{6,30},{7,103},{8,0},{9... | collective-permute-start | bytes 1966088 | tf_op jit(solution)/shard_map/ppermute | solution.py:30
  45.8 17.2 %collective-permute-start.6 = (bf16[4,320,256]{2,1,0:T(8,128)(2,1)}, bf16[4,320,256]{2,1,0:T(8,128)(2,1)}, u32[]{:S(2)}, u32[]{:S(2)}) collective-permute-start(bf16[4,320,256]{2,1,0:T(8,128)(2,1)} %get-tuple-element.31), channel_id=1, source_target_pairs={{0,8},{1,33},{2,10},{3,35},{4,12},{5,37},{6,14},{7,39},{8,16},{9,4... | collective-permute-start | bytes 1966088 | tf_op jit(solution)/shard_map/ppermute | solution.py:30
  47.1 28.3 %all-to-all-start.1 = ((bf16[32,6,1536]{2,1,0:T(8,128)(2,1)}), bf16[32,6,1536]{2,1,0:T(8,128)(2,1)}, u32[]{:S(2)}, u32[]{:S(2)}) async-start(bf16[32,6,1536]{2,1,0:T(8,128)(2,1)} %copy.39), calls=%async_computation.1 | async-start | bytes 1572864 | tf_op jit(solution)/shard_map/all_to_all | solution.py:302
  54.7 18.8 %collective-permute-start.5 = (bf16[4,320,256]{2,1,0:T(8,128)(2,1)}, bf16[4,320,256]{2,1,0:T(8,128)(2,1)}, u32[]{:S(2)}, u32[]{:S(2)}) collective-permute-start(bf16[4,320,256]{2,1,0:T(8,128)(2,1)} %collective-permute-done.4.refs_2_), channel_id=1, source_target_pairs={{0,24},{1,97},{2,26},{3,99},{4,28},{5,101},{6,30},{7,103},{8,0},{9... | collective-permute-start | bytes 1966088 | tf_op jit(solution)/shard_map/ppermute | solution.py:30
  57.3 24.7 %collective-permute-start.10 = (bf16[4,320,512]{2,1,0:T(8,128)(2,1)S(1)}, bf16[4,320,512]{2,1,0:T(8,128)(2,1)}, u32[]{:S(2)}, u32[]{:S(2)}) collective-permute-start(bf16[4,320,512]{2,1,0:T(8,128)(2,1)S(1)} %pad_maximum_fusion.refs_0_), channel_id=1, source_target_pairs={{0,1},{1,0},{2,3},{3,2},{4,5},{5,4},{6,7},{7,6},{8,9},{9,8},{10,11... | collective-permute-start | bytes 3932168 | tf_op jit(solution)/shard_map/ppermute | solution.py:30
  60.7 19.2 %collective-permute-start.12 = (bf16[4,320,256]{2,1,0:T(8,128)(2,1)}, bf16[4,320,256]{2,1,0:T(8,128)(2,1)}, u32[]{:S(2)}, u32[]{:S(2)}) collective-permute-start(bf16[4,320,256]{2,1,0:T(8,128)(2,1)} %collective-permute-done.4.refs_2_), channel_id=1, source_target_pairs={{0,1},{1,0},{2,3},{3,2},{4,5},{5,4},{6,7},{7,6},{8,9},{9,8},{10,11... | collective-permute-start | bytes 1966088 | tf_op jit(solution)/shard_map/ppermute | solution.py:30
  60.8 16.6 %collective-permute-start.13 = (bf16[4,320,256]{2,1,0:T(8,128)(2,1)}, bf16[4,320,256]{2,1,0:T(8,128)(2,1)}, u32[]{:S(2)}, u32[]{:S(2)}) collective-permute-start(bf16[4,320,256]{2,1,0:T(8,128)(2,1)} %collective-permute-done.7.refs_3_), channel_id=1, source_target_pairs={{0,1},{1,0},{2,3},{3,2},{4,5},{5,4},{6,7},{7,6},{8,9},{9,8},{10,11... | collective-permute-start | bytes 1966088 | tf_op jit(solution)/shard_map/ppermute | solution.py:30
  63.0 17.0 %collective-permute-start.9 = (bf16[4,320,256]{2,1,0:T(8,128)(2,1)}, bf16[4,320,256]{2,1,0:T(8,128)(2,1)}, u32[]{:S(2)}, u32[]{:S(2)}) collective-permute-start(bf16[4,320,256]{2,1,0:T(8,128)(2,1)} %collective-permute-done.6.refs_1_), channel_id=1, source_target_pairs={{0,8},{1,33},{2,10},{3,35},{4,12},{5,37},{6,14},{7,39},{8,16},{9,4... | collective-permute-start | bytes 1966088 | tf_op jit(solution)/shard_map/ppermute | solution.py:30
  73.5 7.0 %collective-permute-start.14 = (bf16[4,320,256]{2,1,0:T(8,128)(2,1)}, bf16[4,320,256]{2,1,0:T(8,128)(2,1)}, u32[]{:S(2)}, u32[]{:S(2)}) collective-permute-start(bf16[4,320,256]{2,1,0:T(8,128)(2,1)} %collective-permute-done.8.refs_4_), channel_id=1, source_target_pairs={{0,1},{1,0},{2,3},{3,2},{4,5},{5,4},{6,7},{7,6},{8,9},{9,8},{10,11... | collective-permute-start | bytes 1966088 | tf_op jit(solution)/shard_map/ppermute | solution.py:30
  77.4 4.5 %collective-permute-start.11 = (bf16[4,320,256]{2,1,0:T(8,128)(2,1)}, bf16[4,320,256]{2,1,0:T(8,128)(2,1)}, u32[]{:S(2)}, u32[]{:S(2)}) collective-permute-start(bf16[4,320,256]{2,1,0:T(8,128)(2,1)} %collective-permute-done.6.refs_1_), channel_id=1, source_target_pairs={{0,1},{1,0},{2,3},{3,2},{4,5},{5,4},{6,7},{7,6},{8,9},{9,8},{10,11... | collective-permute-start | bytes 1966088 | tf_op jit(solution)/shard_map/ppermute | solution.py:30
  79.9 3.9 %collective-permute-start.16 = (bf16[4,320,256]{2,1,0:T(8,128)(2,1)}, bf16[4,320,256]{2,1,0:T(8,128)(2,1)}, u32[]{:S(2)}, u32[]{:S(2)}) collective-permute-start(bf16[4,320,256]{2,1,0:T(8,128)(2,1)} %collective-permute-done.5.refs_6_), channel_id=1, source_target_pairs={{0,1},{1,0},{2,3},{3,2},{4,5},{5,4},{6,7},{7,6},{8,9},{9,8},{10,11... | collective-permute-start | bytes 1966088 | tf_op jit(solution)/shard_map/ppermute | solution.py:30
  80.0 5.7 %collective-permute-start.15 = (bf16[4,320,256]{2,1,0:T(8,128)(2,1)}, bf16[4,320,256]{2,1,0:T(8,128)(2,1)}, u32[]{:S(2)}, u32[]{:S(2)}) collective-permute-start(bf16[4,320,256]{2,1,0:T(8,128)(2,1)} %collective-permute-done.9.refs_5_), channel_id=1, source_target_pairs={{0,1},{1,0},{2,3},{3,2},{4,5},{5,4},{6,7},{7,6},{8,9},{9,8},{10,11... | collective-permute-start | bytes 1966088 | tf_op jit(solution)/shard_map/ppermute | solution.py:30
  80.4 16.5 %collective-permute-start = (bf16[3584,256]{1,0:T(8,128)(2,1)S(1)}, bf16[3584,256]{1,0:T(8,128)(2,1)}, u32[]{:S(2)}, u32[]{:S(2)}) collective-permute-start(bf16[3584,256]{1,0:T(8,128)(2,1)S(1)} %bitcast.78), channel_id=1, source_target_pairs={{0,1},{1,0},{2,3},{3,2},{4,5},{5,4},{6,7},{7,6},{8,9},{9,8},{10,11... | collective-permute-start | bytes 5505032 | tf_op jit(solution)/shard_map/ppermute | solution.py:30
  85.7 1.1 copy-start.1
  96.4 2.9 %collective-permute-start.17 = (bf16[256,2304]{1,0:T(8,128)(2,1)S(1)}, bf16[256,2304]{1,0:T(8,128)(2,1)S(1)}, u32[]{:S(2)}, u32[]{:S(2)}) collective-permute-start(bf16[256,2304]{1,0:T(8,128)(2,1)S(1)} %get-tuple-element.34), channel_id=1, source_target_pairs={{0,1},{1,0},{2,3},{3,2},{4,5},{5,4},{6,7},{7,6},{8,9},{9,8},{10,11... | collective-permute-start | bytes 3538952 | tf_op jit(solution)/shard_map/ppermute | solution.py:30
  99.4 19.1 %copy-start = (bf16[16,224,1024]{2,1,0:T(8,128)(2,1)S(1)}, bf16[16,224,1024]{2,1,0:T(8,128)(2,1)}, u32[]{:S(2)}) copy-start(bf16[16,224,1024]{2,1,0:T(8,128)(2,1)} %get-tuple-element.38.w_in) | copy-start | bytes 22020100
  104.3 11.0 %collective-permute-start.18 = (bf16[4,320,256]{2,1,0:T(8,128)(2,1)S(1)}, bf16[4,320,256]{2,1,0:T(8,128)(2,1)S(1)}, u32[]{:S(2)}, u32[]{:S(2)}) collective-permute-start(bf16[4,320,256]{2,1,0:T(8,128)(2,1)S(1)} %get-tuple-element.36), channel_id=1, source_target_pairs={{0,8},{1,33},{2,10},{3,35},{4,12},{5,37},{6,14},{7,39},{8,16},{9,4... | collective-permute-start | bytes 1966088 | tf_op jit(solution)/shard_map/ppermute | solution.py:30
  104.4 11.2 %collective-permute-start.22 = (bf16[4,320,256]{2,1,0:T(8,128)(2,1)S(1)}, bf16[4,320,256]{2,1,0:T(8,128)(2,1)S(1)}, u32[]{:S(2)}, u32[]{:S(2)}) collective-permute-start(bf16[4,320,256]{2,1,0:T(8,128)(2,1)S(1)} %get-tuple-element.46), channel_id=1, source_target_pairs={{0,24},{1,97},{2,26},{3,99},{4,28},{5,101},{6,30},{7,103},{8,0},{9... | collective-permute-start | bytes 1966088 | tf_op jit(solution)/shard_map/ppermute | solution.py:30
  107.1 22.3 %collective-permute-start.20 = (bf16[4,320,256]{2,1,0:T(8,128)(2,1)S(1)}, bf16[4,320,256]{2,1,0:T(8,128)(2,1)S(1)}, u32[]{:S(2)}, u32[]{:S(2)}) collective-permute-start(bf16[4,320,256]{2,1,0:T(8,128)(2,1)S(1)} %get-tuple-element.42), channel_id=1, source_target_pairs={{0,24},{1,97},{2,26},{3,99},{4,28},{5,101},{6,30},{7,103},{8,0},{9... | collective-permute-start | bytes 1966088 | tf_op jit(solution)/shard_map/ppermute | solution.py:30
  107.1 22.5 %collective-permute-start.21 = (bf16[4,320,256]{2,1,0:T(8,128)(2,1)S(1)}, bf16[4,320,256]{2,1,0:T(8,128)(2,1)S(1)}, u32[]{:S(2)}, u32[]{:S(2)}) collective-permute-start(bf16[4,320,256]{2,1,0:T(8,128)(2,1)S(1)} %get-tuple-element.44), channel_id=1, source_target_pairs={{0,8},{1,33},{2,10},{3,35},{4,12},{5,37},{6,14},{7,39},{8,16},{9,4... | collective-permute-start | bytes 1966088 | tf_op jit(solution)/shard_map/ppermute | solution.py:30
  115.5 13.9 %collective-permute-start.19 = (bf16[4,320,256]{2,1,0:T(8,128)(2,1)S(1)}, bf16[4,320,256]{2,1,0:T(8,128)(2,1)S(1)}, u32[]{:S(2)}, u32[]{:S(2)}) collective-permute-start(bf16[4,320,256]{2,1,0:T(8,128)(2,1)S(1)} %add_convert_fusion.1), channel_id=1, source_target_pairs={{0,8},{1,33},{2,10},{3,35},{4,12},{5,37},{6,14},{7,39},{8,16},{9,4... | collective-permute-start | bytes 1966088 | tf_op jit(solution)/shard_map/ppermute | solution.py:30
  115.8 13.9 %collective-permute-start.23 = (bf16[4,320,256]{2,1,0:T(8,128)(2,1)S(1)}, bf16[4,320,256]{2,1,0:T(8,128)(2,1)S(1)}, u32[]{:S(2)}, u32[]{:S(2)}) collective-permute-start(bf16[4,320,256]{2,1,0:T(8,128)(2,1)S(1)} %add_convert_fusion), channel_id=1, source_target_pairs={{0,24},{1,97},{2,26},{3,99},{4,28},{5,101},{6,30},{7,103},{8,0},{9... | collective-permute-start | bytes 1966088 | tf_op jit(solution)/shard_map/ppermute | solution.py:30
  129.9 11.0 %collective-permute-start.24 = (bf16[320,512]{1,0:T(8,128)(2,1)S(1)}, bf16[320,512]{1,0:T(8,128)(2,1)S(1)}, u32[]{:S(2)}, u32[]{:S(2)}) collective-permute-start(bf16[320,512]{1,0:T(8,128)(2,1)S(1)} %pad_maximum_fusion.4), channel_id=1, source_target_pairs={{0,32},{1,9},{2,34},{3,11},{4,36},{5,13},{6,38},{7,15},{8,40},{9,1... | collective-permute-start | bytes 983048 | tf_op jit(solution)/shard_map/ppermute | solution.py:30
  130.1 10.9 %collective-permute-start.25 = (bf16[320,512]{1,0:T(8,128)(2,1)S(1)}, bf16[320,512]{1,0:T(8,128)(2,1)S(1)}, u32[]{:S(2)}, u32[]{:S(2)}) collective-permute-start(bf16[320,512]{1,0:T(8,128)(2,1)S(1)} %pad_maximum_fusion.5), channel_id=1, source_target_pairs={{0,96},{1,25},{2,98},{3,27},{4,100},{5,29},{6,102},{7,31},{8,104},... | collective-permute-start | bytes 983048 | tf_op jit(solution)/shard_map/ppermute | solution.py:30
  132.8 8.1 %collective-permute-start.26 = (bf16[320,512]{1,0:T(8,128)(2,1)S(1)}, bf16[320,512]{1,0:T(8,128)(2,1)S(1)}, u32[]{:S(2)}, u32[]{:S(2)}) collective-permute-start(bf16[320,512]{1,0:T(8,128)(2,1)S(1)} %pad_maximum_fusion.6), channel_id=1, source_target_pairs={{0,64},{1,17},{2,66},{3,19},{4,68},{5,21},{6,70},{7,23},{8,72},{9,... | collective-permute-start | bytes 983048 | tf_op jit(solution)/shard_map/ppermute | solution.py:30

commit v4 on v3

--- a/solution.py
+++ b/solution.py
@@ -56,50 +56,47 @@
 PIECES = ((0, 0, 512), (1, 0, 256), (3, 256, 256), (1, 256, 256), (3, 0, 256), (2, 0, 256), (2, 256, 256))
 
 
-def head_kernel(place, latent, picked, expand, *refs):
+def head_kernel(place, latent, picked, *refs):
     own, oth = refs[0:7], refs[7:14]
     grad_pre_ref, keep_ref, give_ref, w_in_out = refs[14:18]
     w_in, w_out, pre, pred, gpred, sems = refs[18:]
     x, y, c = place[0], place[1], place[2]
 
-    def fetch(pieces, core, sem_in, sem_out):
+    def fetch(pieces, core, top, sem):
         for ref, (d3, left, wide) in zip(pieces, PIECES):
             for j, d2 in enumerate(SHIFTS):
                 sx, sy = place_of(core, x, y, 4 - d3, 4 - d2)
                 b = sx * 4 + sy
                 src = ref.at[j]
 
-                def bring(rows, cols, dst, sem):
-                    pltpu.make_async_copy(src.at[rows, cols], dst, sems.at[sem]).start()
-
-                def lane(first, start, size):
-                    return pl.ds(pl.multiple_of(first + start, 256), size)
-
-                every = pl.ds(0, wide)
-                bring(
-                    pl.ds(0, 224),
-                    every,
-                    w_in.at[b, :, lane(core * HH, left, wide)],
-                    sem_in,
-                )
-                bring(
-                    pl.ds(224, 64),
-                    every,
-                    w_out.at[b, :, lane(core * HO, left, wide)],
-                    sem_out,
-                )
-                for at in range(0, wide, 256):
-                    zh = (left + at) // 256
+                def bring(first, rows, at, size, dst):
+                    pltpu.make_async_copy(
+                        src.at[pl.ds(first, rows), pl.ds(at, size)], dst, sems.at[sem]
+                    ).start()
+
+                def lane(first, size):
+                    return pl.ds(pl.multiple_of(first, 256), size)
+
+                if top:
+                    bring(0, 224, 0, wide, w_in.at[b, :, lane(core * HH + left, wide)])
+                else:
                     bring(
-                        pl.ds(288, 32),
-                        pl.ds(at, 256),
-                        w_out.at[b, pl.ds(zh * 32, 32), lane(core * HO, 512, 256)],
-                        sem_out,
+                        224, 64, 0, wide, w_out.at[b, :, lane(core * HO + left, wide)]
                     )
-
-    fetch(own, c, 0, 2)
-    fetch(oth, 1 - c, 1, 2)
-    goal = jnp.dot(expand[...], picked[...], preferred_element_type=f32)
+                    for at in range(0, wide, 256):
+                        rows = pl.ds((left + at) // 8, 32)
+                        dst = w_out.at[b, rows, lane(core * HO + 512, 256)]
+                        bring(288, 32, at, 256, dst)
+
+    fetch(own, c, True, 0)
+    fetch(oth, 1 - c, True, 1)
+    fetch(own, c, False, 2)
+    fetch(oth, 1 - c, False, 2)
+    token = lax.broadcasted_iota(jnp.int32, (TOK, TOK), 0)
+    row = lax.broadcasted_iota(jnp.int32, (TOK, TOK), 1)
+    want = (token // 4 % 32) * 8 + token // 128 * 4 + token % 4
+    expand = jnp.where(row == want, 1.0, 0.0).astype(bf16)
+    goal = jnp.dot(expand, picked[...], preferred_element_type=f32)
     norm_goal = jnp.sqrt(jnp.sum(goal * goal, axis=1, keepdims=True) + eps_norm)
     half = w_in.at[:, :, pl.ds(0, HH)]
     for core, sem in ((c, 0), (1 - c, 1)):
@@ -158,12 +155,12 @@
     save.wait()
 
 
-def head(place, latent, picked, expand, own, oth):
+def head(place, latent, picked, own, oth):
     vmem = pl.BlockSpec(memory_space=pltpu.VMEM)
-    hbm = pl.BlockSpec(memory_space=pl.ANY)
+    hbm = pl.BlockSpec(memory_space=pltpu.HBM)
     return pl.pallas_call(
         head_kernel,
-        in_specs=[pl.BlockSpec(memory_space=pltpu.SMEM)] + [vmem] * 3 + [hbm] * 14,
+        in_specs=[pl.BlockSpec(memory_space=pltpu.SMEM)] + [vmem] * 2 + [hbm] * 14,
         out_specs=[vmem, vmem, vmem, hbm],
         out_shape=[
             jax.ShapeDtypeStruct((TOK, PH), bf16),
@@ -184,7 +181,7 @@
             flops=5_000_000_000, bytes_accessed=30_000_000, transcendentals=600_000
         ),
         name="head",
-    )(place, latent, picked, expand, *own, *oth)
+    )(place, latent, picked, *own, *oth)
 
 
 def tail_kernel(place, lat_a, lat_b, keep, rcv, *refs):
@@ -263,63 +260,97 @@
     return sum(t.astype(f32) for t in terms).astype(bf16)
 
 
+def fan_kernel(top, low, out):
+    for h in range(2):
+        lows = low[:, h * HO : (h + 1) * HO].astype(f32)
+        block = jnp.concatenate(
+            [
+                top[:, h * HH : (h + 1) * HH].astype(f32),
+                lows[:, :512],
+                jnp.concatenate([lows[0:2, 512:], lows[2:4, 512:]], axis=1),
+            ],
+            axis=0,
+        ).astype(bf16)
+        for z in range(8):
+            out[z * 2 + h] = block
+
+
+def fan_out(proj_in, proj_out):
+    return pl.pallas_call(
+        fan_kernel,
+        out_shape=jax.ShapeDtypeStruct((16, 20, HH), bf16),
+        name="fan_out",
+    )(proj_in, proj_out)
+
+
+def fan_in_kernel(last, top, low):
+    for h in range(2):
+        total = last[h].astype(f32)
+        for z in range(1, 8):
+            total += last[z * 2 + h].astype(f32)
+        top[:, h * HH : (h + 1) * HH] = total[:14]
+        low[:, h * HO : h * HO + 512] = total[14:18]
+        low[0:2, h * HO + 512 : (h + 1) * HO] = total[18:20, :256]
+        low[2:4, h * HO + 512 : (h + 1) * HO] = total[18:20, 256:]
+
+
+def fan_in(last):
+    return pl.pallas_call(
+        fan_in_kernel,
+        out_shape=[
+            jax.ShapeDtypeStruct((14, PH), f32),
+            jax.ShapeDtypeStruct((4, DT), f32),
+        ],
+        name="fan_in",
+    )(last)
+
+
 def per_device(latent, targets, index_map, proj_in, proj_out):
     x, y, c = lax.axis_index("x"), lax.axis_index("y"), lax.axis_index("c")
     place = jnp.stack([x, y, c]).astype(jnp.int32)
 
-    halves = jnp.concatenate(
-        [
-            proj_in.reshape(14, 2, HH).transpose(1, 0, 2),
-            proj_out.reshape(4, 2, HO).transpose(1, 0, 2).reshape(2, 6, HH),
-        ],
-        axis=1,
-    )
-    fan = jnp.broadcast_to(halves[None], (8, 2, 20, HH)).reshape(16, 20, HH)
     column = lax.all_to_all(
-        fan, ("zh", "zl", "c"), split_axis=0, concat_axis=0, tiled=True
-    )
-    rows_in = column[:, :14].reshape(224, HH)
-    rows_out = column[:, 14:].reshape(16, 4, HO).reshape(2, ROWS_OUT, HO)
+        fan_out(proj_in, proj_out),
+        ("zh", "zl", "c"), split_axis=0, concat_axis=0, tiled=True,
+    )
+    third = jnp.concatenate([column[:, 18:, :256], column[:, 18:, 256:]], axis=1)
     packed = jnp.concatenate(
         [
-            rows_in,
-            rows_out[:, :, :512].reshape(64, 512),
-            rows_out[:, :, 512:].transpose(1, 0, 2).reshape(32, 512),
+            column[:, :14].reshape(224, HH),
+            column[:, 14:18].reshape(64, HH),
+            third.reshape(2, 32, 256).transpose(1, 0, 2).reshape(32, HH),
         ],
         axis=0,
     )
-    maps = index_map[0]
-    width = targets.shape[2] * 32
-    row_of = maps[:, 0] // width
+
+    seq = lax.axis_index("zh") * 16 + x * 4 + y
     slab = targets[0].transpose(1, 0, 2)
-    pick = (row_of[:, None] == jnp.arange(48, dtype=jnp.int32)[None]).astype(bf16)
-    sent = jnp.stack(
-        [jnp.dot(pick, slab[t], preferred_element_type=f32).astype(bf16) for t in range(3)]
-    )
-    sent = sent.reshape(3, 32, 2, DT).transpose(1, 0, 2, 3).reshape(32, 6, DT)
+    wide, tall = slab.shape[:2]
+    cell = lax.dynamic_slice_in_dim(index_map[0], seq * 4, 4, 1)
+    cell = (cell % (wide * 32) - seq * wide) * tall + cell // (wide * 32)
+    pick = (
+        cell.reshape(TOK)[:, None] == jnp.arange(wide * tall, dtype=jnp.int32)[None]
+    ).astype(bf16)
+    sent = jnp.dot(
+        pick, slab.reshape(wide * tall, DT), preferred_element_type=f32
+    ).astype(bf16).reshape(32, 8, DT)
     lat_t = latent[0].T
     packed, sent, lat_t = lax.optimization_barrier((packed, sent, lat_t))
     got = lax.all_to_all(
         sent, ("zh", "x", "y"), split_axis=0, concat_axis=0, tiled=True
     )
-    picked = got.reshape(192, DT)
+    picked = got.reshape(TOK, DT)
     line = jnp.stack([packed] + [first_axis(packed, d) for d in SHIFTS[1:]])
     lat_o = swap_cores(lat_t)
     left, right = lax.optimization_barrier((line[..., :256], line[..., 256:]))
     left1, right3 = second_axis(left, 1), second_axis(right, 3)
     right1, left3 = second_axis(right, 1), second_axis(left, 3)
     left2, right2 = second_axis(left1, 1), second_axis(right3, 3)
-    col_of = (maps[0] % width).reshape(32, 4) - 3 * jnp.arange(32, dtype=jnp.int32)[:, None]
-    token = jnp.arange(TOK, dtype=jnp.int32)[:, None]
-    row = jnp.arange(192, dtype=jnp.int32)[None]
-    want = ((token // 4) % 32) * 6 + jnp.tile(col_of.reshape(128), 2)[:, None] * 2 + token // 128
-    expand = (row == want).astype(bf16)
-
-    right2, picked, expand = lax.optimization_barrier((right2, picked, expand))
+    right2, picked = lax.optimization_barrier((right2, picked))
     own = [line, left1, right3, right1, left3, left2, right2]
     oth = [swap_cores(v) for v in own]
 
-    grad_pre, keep, give, w_in = head(place, latent[0], picked, expand, own, oth)
+    grad_pre, keep, give, w_in = head(place, latent[0], picked, own, oth)
     rcv = swap_cores(give)
     sums = tail(place, lat_t, lat_o, keep, rcv)
     lefts, rights = sums[0::2], sums[1::2]
@@ -341,21 +372,19 @@
     ]
     got2 = [first_axis(line_sum[d], d) for d in SHIFTS[1:]]
     mine = add(line_sum[0], *got2)
-    g_in = mine[:224].reshape(16, 14, HH)
-    g_out = jnp.concatenate(
-        [
-            mine[224:288].reshape(2, 32, 512),
-            mine[288:].reshape(32, 2, 256).transpose(1, 0, 2),
-        ],
-        axis=2,
-    ).reshape(16, 4, HO).reshape(16, 6, HH)
+    third = mine[288:].reshape(32, 2, 256).transpose(1, 0, 2).reshape(16, 4, 256)
     last = lax.all_to_all(
-        jnp.concatenate([g_in, g_out], axis=1),
+        jnp.concatenate(
+            [
+                mine[:224].reshape(16, 14, HH),
+                mine[224:288].reshape(16, 4, HH),
+                jnp.concatenate([third[:, :2], third[:, 2:]], axis=2),
+            ],
+            axis=1,
+        ),
         ("zh", "zl", "c"), split_axis=0, concat_axis=0, tiled=True,
     )
-    total = jnp.sum(last.reshape(8, 2, 20, HH).astype(f32), axis=0)
-    grad_in = total[:, :14].transpose(1, 0, 2).reshape(14, PH)
-    grad_out = total[:, 14:].reshape(2, 4, HO).transpose(1, 0, 2).reshape(4, DT)
+    grad_in, grad_out = fan_in(last)
     return grad_latent[None], grad_in, grad_out
 
 

time: 167 us -> 163 us (0.976)
  local copies, waits for them, and re-layouts: 13 us -> 7.31 us
  Pallas kernels: 18.9 us -> 20.9 us
    reshape x8, local copies, waits for them, and re-layouts: 4.41 us -> 0.26 us  [the longest x1 0.07 us: per_device(): column[:, :14].reshape(224, HH)]
    pallas_call x0 -> x2, Pallas kernels: none -> 3.26 us  [the longest x1 1.67 us: fan_in(): pl.pallas_call(fan_in_kernel, out_shape=[jax.ShapeDtypeStruct((14, PH), f...]
    unnamed x14 -> x16, local copies, waits for them, and re-layouts: 4.64 us -> 6.49 us
  transfers between devices with their start and end apart: 29 -> 29, of which waited for: 12 -> 12; matrix products, arithmetic and copies ran while one was open for 6% -> 5% of each run, Pallas kernels for 8% -> 8%
where the time goes in v4:
time: 163 us
  waiting for transfers between devices  54.8 us (34%)
  starting transfers between devices  49.5 us (30%)
  blocking collectives  24.4 us (15%)
  Pallas kernels  20.9 us (13%)
  local copies, waits for them, and re-layouts  7.31 us (4%)
  other arithmetic  3.38 us (2%)
    ppermute x27, waiting for transfers between devices, permute(): return lax.ppermute(v, AXES, pairs)  46.6 us
    ppermute x27, starting transfers between devices, permute(): return lax.ppermute(v, AXES, pairs)  32.8 us
    all_to_all x1, blocking collectives, per_device(): lax.all_to_all(jnp.concatenate([mine[:224].reshape(16, 14, HH), mine[224:...  24.4 us
    all_to_all x1, starting transfers between devices, per_device(): lax.all_to_all(fan_out(proj_in, proj_out), ('zh', 'zl', 'c'), split_axis=...  9.98 us
    pallas_call x1, Pallas kernels, head(): pl.pallas_call(head_kernel, in_specs=[pl.BlockSpec(memory_space=pltpu.SME...  8.39 us
    all_to_all x1, waiting for transfers between devices, per_device(): lax.all_to_all(fan_out(proj_in, proj_out), ('zh', 'zl', 'c'), split_axis=...  8.15 us
    all_to_all x1, starting transfers between devices, per_device(): lax.all_to_all(sent, ('zh', 'x', 'y'), split_axis=0, concat_axis=0, tiled...  6.73 us
    unnamed x16, local copies, waits for them, and re-layouts  6.49 us
  transfers between devices with their start and end apart: 29, of which 12 were waited for; matrix products, arithmetic and copies ran while one was open for 5% of the time, Pallas kernels for 8%

profile of v4, /device:TPU:1, one launch (start us, length us, event | category | flops | bytes accessed | tf_op | source)
XLA Modules:
  0.0 162.6 jit_solution(692235126044642771)
XLA Ops:
  0.7 1.6 fan_out.1
  2.2 10.0 %all-to-all-start = ((bf16[16,20,512]{2,1,0:T(8,128)(2,1)}), bf16[16,20,512]{2,1,0:T(8,128)(2,1)S(1)}, u32[]{:S(2)}, u32[]{:S(2)}) async-start(bf16[16,20,512]{2,1,0:T(8,128)(2,1)} %fan_out.1), calls=%async_computation | async-start | bytes 786432 | tf_op jit(solution)/shard_map/all_to_all | solution.py:312
  12.2 0.8 sign_compare_fusion
  13.1 0.1 ne.39
  13.2 0.1 dynamic-slice_remainder_fusion
  13.3 0.1 rem.24
  13.4 0.1 div.14
  13.5 3.8 %copy.13 = bf16[1,256,3584]{1,2,0:T(8,128)(2,1)} copy(bf16[1,256,3584]{2,1,0:T(8,128)(2,1)} %param.5) | data formatting | bytes 3670016 | tf_op args[0]
  17.3 1.3 fusion
  18.6 8.2 %all-to-all-done = bf16[16,20,512]{2,1,0:T(8,128)(2,1)S(1)} async-done(((bf16[16,20,512]{2,1,0:T(8,128)(2,1)}), bf16[16,20,512]{2,1,0:T(8,128)(2,1)S(1)}, u32[]{:S(2)}, u32[]{:S(2)}) %all-to-all-start) | async-done | bytes 327712 | tf_op jit(solution)/shard_map/all_to_all | solution.py:312
  27.0 0.1 reshape.120
  27.2 3.0 %collective-permute-start.3 = (bf16[320,512]{1,0:T(8,128)(2,1)S(1)}, bf16[320,512]{1,0:T(8,128)(2,1)S(1)}, u32[]{:S(2)}, u32[]{:S(2)}) collective-permute-start(bf16[320,512]{1,0:T(8,128)(2,1)S(1)} %pad_maximum_fusion.1), channel_id=1, source_target_pairs={{0,64},{1,17},{2,66},{3,19},{4,68},{5,21},{6,70},{7,23},{8,72},{9,... | collective-permute-start | bytes 983048 | tf_op jit(solution)/shard_map/ppermute | solution.py:30
  30.2 0.8 collective-permute-start.2
  30.9 0.7 collective-permute-start.1
  31.6 6.7 %all-to-all-start.1 = ((bf16[32,8,1536]{2,1,0:T(8,128)(2,1)}), bf16[32,8,1536]{2,1,0:T(8,128)(2,1)S(1)}, u32[]{:S(2)}, u32[]{:S(2)}) async-start(bf16[32,8,1536]{2,1,0:T(8,128)(2,1)} %fusion), calls=%async_computation.1 | async-start | bytes 1572864 | tf_op jit(solution)/shard_map/all_to_all | solution.py:339
  38.4 0.2 collective-permute-done.2
  38.6 0.7 copy-done.5
  39.3 1.1 pad_maximum_fusion.refs_0_
  40.4 0.1 fusion.12
  40.5 2.6 %collective-permute-start.4 = (bf16[4,320,256]{2,1,0:T(8,128)(2,1)S(1)}, bf16[4,320,256]{2,1,0:T(8,128)(2,1)S(1)}, u32[]{:S(2)}, u32[]{:S(2)}) collective-permute-start(bf16[4,320,256]{2,1,0:T(8,128)(2,1)S(1)} %get-tuple-element.28), channel_id=1, source_target_pairs={{0,24},{1,97},{2,26},{3,99},{4,28},{5,101},{6,30},{7,103},{8,0},{9... | collective-permute-start | bytes 1966088 | tf_op jit(solution)/shard_map/ppermute | solution.py:30
  43.1 2.7 %collective-permute-start.8 = (bf16[4,320,256]{2,1,0:T(8,128)(2,1)S(1)}, bf16[4,320,256]{2,1,0:T(8,128)(2,1)}, u32[]{:S(2)}, u32[]{:S(2)}) collective-permute-start(bf16[4,320,256]{2,1,0:T(8,128)(2,1)S(1)} %get-tuple-element.31), channel_id=1, source_target_pairs={{0,24},{1,97},{2,26},{3,99},{4,28},{5,101},{6,30},{7,103},{8,0},{9... | collective-permute-start | bytes 1966088 | tf_op jit(solution)/shard_map/ppermute | solution.py:30
  45.8 10.7 %collective-permute-done.4.refs_2_ = bf16[4,320,256]{2,1,0:T(8,128)(2,1)S(1)} collective-permute-done((bf16[4,320,256]{2,1,0:T(8,128)(2,1)S(1)}, bf16[4,320,256]{2,1,0:T(8,128)(2,1)S(1)}, u32[]{:S(2)}, u32[]{:S(2)}) %collective-permute-start.4) | collective-permute-done | bytes 655392 | tf_op jit(solution)/shard_map/ppermute | solution.py:30
  56.5 2.4 %collective-permute-start.5 = (bf16[4,320,256]{2,1,0:T(8,128)(2,1)S(1)}, bf16[4,320,256]{2,1,0:T(8,128)(2,1)S(1)}, u32[]{:S(2)}, u32[]{:S(2)}) collective-permute-start(bf16[4,320,256]{2,1,0:T(8,128)(2,1)S(1)} %collective-permute-done.4.refs_2_), channel_id=1, source_target_pairs={{0,24},{1,97},{2,26},{3,99},{4,28},{5,101},{6,30},{7,103},{8,0},{9... | collective-permute-start | bytes 1966088 | tf_op jit(solution)/shard_map/ppermute | solution.py:30
  58.9 2.3 %collective-permute-start.13 = (bf16[4,320,256]{2,1,0:T(8,128)(2,1)}, bf16[4,320,256]{2,1,0:T(8,128)(2,1)}, u32[]{:S(2)}, u32[]{:S(2)}) collective-permute-start(bf16[4,320,256]{2,1,0:T(8,128)(2,1)} %collective-permute-done.7.refs_3_), channel_id=1, source_target_pairs={{0,1},{1,0},{2,3},{3,2},{4,5},{5,4},{6,7},{7,6},{8,9},{9,8},{10,11... | collective-permute-start | bytes 1966088 | tf_op jit(solution)/shard_map/ppermute | solution.py:30
  61.2 2.4 %collective-permute-done.8.refs_4_ = bf16[4,320,256]{2,1,0:T(8,128)(2,1)} collective-permute-done((bf16[4,320,256]{2,1,0:T(8,128)(2,1)S(1)}, bf16[4,320,256]{2,1,0:T(8,128)(2,1)}, u32[]{:S(2)}, u32[]{:S(2)}) %collective-permute-start.8) | collective-permute-done | bytes 655392 | tf_op jit(solution)/shard_map/ppermute | solution.py:30
  63.5 1.7 %collective-permute-start.10 = (bf16[4,320,512]{2,1,0:T(8,128)(2,1)S(1)}, bf16[4,320,512]{2,1,0:T(8,128)(2,1)}, u32[]{:S(2)}, u32[]{:S(2)}) collective-permute-start(bf16[4,320,512]{2,1,0:T(8,128)(2,1)S(1)} %pad_maximum_fusion.refs_0_), channel_id=1, source_target_pairs={{0,1},{1,0},{2,3},{3,2},{4,5},{5,4},{6,7},{7,6},{8,9},{9,8},{10,11... | collective-permute-start | bytes 3932168 | tf_op jit(solution)/shard_map/ppermute | solution.py:30
  65.3 0.2 collective-permute-done.6.refs_1_
  65.5 0.8 collective-permute-start.9
  66.3 4.1 %collective-permute-done.5.refs_6_ = bf16[4,320,256]{2,1,0:T(8,128)(2,1)S(1)} collective-permute-done((bf16[4,320,256]{2,1,0:T(8,128)(2,1)S(1)}, bf16[4,320,256]{2,1,0:T(8,128)(2,1)S(1)}, u32[]{:S(2)}, u32[]{:S(2)}) %collective-permute-start.5) | collective-permute-done | bytes 655392 | tf_op jit(solution)/shard_map/ppermute | solution.py:30
  70.4 0.9 copy-done.3
  71.3 1.7 %collective-permute-start.14 = (bf16[4,320,256]{2,1,0:T(8,128)(2,1)}, bf16[4,320,256]{2,1,0:T(8,128)(2,1)}, u32[]{:S(2)}, u32[]{:S(2)}) collective-permute-start(bf16[4,320,256]{2,1,0:T(8,128)(2,1)} %collective-permute-done.8.refs_4_), channel_id=1, source_target_pairs={{0,1},{1,0},{2,3},{3,2},{4,5},{5,4},{6,7},{7,6},{8,9},{9,8},{10,11... | collective-permute-start | bytes 1966088 | tf_op jit(solution)/shard_map/ppermute | solution.py:30
  73.0 0.1 collective-permute-start.11
  73.1 0.4 collective-permute-start.16
  73.6 3.2 %collective-permute-done.9.refs_5_ = bf16[4,320,256]{2,1,0:T(8,128)(2,1)} collective-permute-done((bf16[4,320,256]{2,1,0:T(8,128)(2,1)}, bf16[4,320,256]{2,1,0:T(8,128)(2,1)}, u32[]{:S(2)}, u32[]{:S(2)}) %collective-permute-start.9) | collective-permute-done | bytes 655392 | tf_op jit(solution)/shard_map/ppermute | solution.py:30
  76.7 3.2 %collective-permute-start.15 = (bf16[4,320,256]{2,1,0:T(8,128)(2,1)}, bf16[4,320,256]{2,1,0:T(8,128)(2,1)}, u32[]{:S(2)}, u32[]{:S(2)}) collective-permute-start(bf16[4,320,256]{2,1,0:T(8,128)(2,1)} %collective-permute-done.9.refs_5_), channel_id=1, source_target_pairs={{0,1},{1,0},{2,3},{3,2},{4,5},{5,4},{6,7},{7,6},{8,9},{9,8},{10,11... | collective-permute-start | bytes 1966088 | tf_op jit(solution)/shard_map/ppermute | solution.py:30
  79.9 0.1 pad_add_fusion.place
  80.0 2.0 %collective-permute-done.15.refs_12_ = bf16[4,320,256]{2,1,0:T(8,128)(2,1)} collective-permute-done((bf16[4,320,256]{2,1,0:T(8,128)(2,1)}, bf16[4,320,256]{2,1,0:T(8,128)(2,1)}, u32[]{:S(2)}, u32[]{:S(2)}) %collective-permute-start.15) | collective-permute-done | bytes 655392 | tf_op jit(solution)/shard_map/ppermute | solution.py:30
  82.0 1.1 copy-done.4
  83.1 8.4 %head.1 = (bf16[256,1024]{1,0:T(8,128)(2,1)S(1)}, bf16[256,2304]{1,0:T(8,128)(2,1)S(1)}, bf16[256,2304]{1,0:T(8,128)(2,1)S(1)}, bf16[16,224,1024]{2,1,0:T(8,128)(2,1)}) custom-call(s32[3]{0:T(128)S(1)} %pad_add_fusion.place, bf16[256,3584]{1,0:T(8,128)(2,1)} %bitcast.52, bf16[256,1536]{1,0:T(8,128)(2,1)S(1)} %bitcast.50, ...), custom_call_target="tpu_custom_call" | custom-call | flops 5000000000 | bytes 30000000 | tf_op jit(solution)/shard_map/head/pallas_call | solution.py:161
  91.5 0.5 collective-permute-start.17
  91.9 2.5 %collective-permute-done.17.rcv = bf16[256,2304]{1,0:T(8,128)(2,1)S(1)} collective-permute-done((bf16[256,2304]{1,0:T(8,128)(2,1)S(1)}, bf16[256,2304]{1,0:T(8,128)(2,1)S(1)}, u32[]{:S(2)}, u32[]{:S(2)}) %collective-permute-start.17) | collective-permute-done | bytes 1179680 | tf_op jit(solution)/shard_map/ppermute | solution.py:30
  94.4 4.9 %tail.1 = (bf16[4,320,256]{2,1,0:T(8,128)(2,1)S(1)}, bf16[4,320,256]{2,1,0:T(8,128)(2,1)S(1)}, bf16[4,320,256]{2,1,0:T(8,128)(2,1)S(1)}, bf16[4,320,256]{2,1,0:T...) custom-call(s32[3]{0:T(128)S(1)} %pad_add_fusion.place, ...), custom_call_target="tpu_custom_call" | custom-call | flops 2700000000 | bytes 12000000 | tf_op jit(solution)/shard_map/tail/pallas_call | solution.py:221
  99.4 1.1 collective-permute-start.18
  100.5 1.6 collective-permute-start.22
  102.1 0.8 collective-permute-start.20
  102.9 0.7 collective-permute-start.21
  103.6 6.8 %collective-permute-done.18 = bf16[4,320,256]{2,1,0:T(8,128)(2,1)S(1)} collective-permute-done((bf16[4,320,256]{2,1,0:T(8,128)(2,1)S(1)}, bf16[4,320,256]{2,1,0:T(8,128)(2,1)S(1)}, u32[]{:S(2)}, u32[]{:S(2)}) %collective-permute-start.18) | collective-permute-done | bytes 655392 | tf_op jit(solution)/shard_map/ppermute | solution.py:30
  110.4 0.2 add_convert_fusion.1
  110.6 0.1 collective-permute-start.19
  110.7 0.2 add_convert_fusion
  110.8 2.7 %collective-permute-start.23 = (bf16[4,320,256]{2,1,0:T(8,128)(2,1)S(1)}, bf16[4,320,256]{2,1,0:T(8,128)(2,1)S(1)}, u32[]{:S(2)}, u32[]{:S(2)}) collective-permute-start(bf16[4,320,256]{2,1,0:T(8,128)(2,1)S(1)} %add_convert_fusion), channel_id=1, source_target_pairs={{0,24},{1,97},{2,26},{3,99},{4,28},{5,101},{6,30},{7,103},{8,0},{9... | collective-permute-start | bytes 1966088 | tf_op jit(solution)/shard_map/ppermute | solution.py:30
  113.6 4.3 %back.1 = bf16[256,3584]{1,0:T(8,128)(2,1)} custom-call(bf16[256,1024]{1,0:T(8,128)(2,1)S(1)} %get-tuple-element.37.grad_pre, bf16[16,224,1024]{2,1,0:T(8,128)(2,1)S(1)} %copy-done.1), custom_call_target="tpu_custom_call" | custom-call | flops 1900000000 | bytes 10000000 | tf_op jit(solution)/shard_map/back/pallas_call | solution.py:242
  117.9 6.5 %collective-permute-done.19 = bf16[4,320,256]{2,1,0:T(8,128)(2,1)S(1)} collective-permute-done((bf16[4,320,256]{2,1,0:T(8,128)(2,1)S(1)}, bf16[4,320,256]{2,1,0:T(8,128)(2,1)S(1)}, u32[]{:S(2)}, u32[]{:S(2)}) %collective-permute-start.19) | collective-permute-done | bytes 655392 | tf_op jit(solution)/shard_map/ppermute | solution.py:30
  124.4 0.2 fusion.1
  124.7 0.2 fusion.2
  125.0 0.1 collective-permute-start.24
  125.1 2.7 %collective-permute-start.25 = (bf16[320,512]{1,0:T(8,128)(2,1)S(1)}, bf16[320,512]{1,0:T(8,128)(2,1)S(1)}, u32[]{:S(2)}, u32[]{:S(2)}) collective-permute-start(bf16[320,512]{1,0:T(8,128)(2,1)S(1)} %pad_maximum_fusion.3), channel_id=1, source_target_pairs={{0,96},{1,25},{2,98},{3,27},{4,100},{5,29},{6,102},{7,31},{8,104},... | collective-permute-start | bytes 983048 | tf_op jit(solution)/shard_map/ppermute | solution.py:30
  127.9 0.1 collective-permute-start.26
  128.0 8.0 %collective-permute-done.24 = bf16[320,512]{1,0:T(8,128)(2,1)S(1)} collective-permute-done((bf16[320,512]{1,0:T(8,128)(2,1)S(1)}, bf16[320,512]{1,0:T(8,128)(2,1)S(1)}, u32[]{:S(2)}, u32[]{:S(2)}) %collective-permute-start.24) | collective-permute-done | bytes 327712 | tf_op jit(solution)/shard_map/ppermute | solution.py:30
  136.0 0.2 add_convert_fusion.2
  136.3 0.1 reshape.127
  136.4 0.1 maximum_maximum_fusion
  136.5 24.4 %all_to_all.15.last = bf16[16,20,512]{2,1,0:T(8,128)(2,1)} all-to-all(bf16[16,20,512]{2,1,0:T(8,128)(2,1)S(1)} %maximum_maximum_fusion), channel_id=1, replica_groups=mesh['zh'=2,'x'=4,'y'=4,'zl'=4,'c'=2] {'zh','zl','c'}, dimensions={0} | all-to-all | bytes 655360 | tf_op jit(solution)/shard_map/all_to_all | solution.py:376
  160.9 1.7 %fan_in.1 = (f32[14,1024]{1,0:T(8,128)}, f32[4,1536]{1,0:T(4,128)}) custom-call(bf16[16,20,512]{2,1,0:T(8,128)(2,1)} %all_to_all.15.last), custom_call_target="tpu_custom_call" | custom-call | tf_op jit(solution)/shard_map/fan_in/pallas_call | solution.py:298
  (52 shorter events, 0.5 us)
Async XLA Ops:
  0.6 16.7 %copy-start = (bf16[1,48,3,1536]{3,1,2,0:T(8,128)(2,1)S(1)}, bf16[1,48,3,1536]{3,1,2,0:T(8,128)(2,1)}, u32[]{:S(2)}) copy-start(bf16[1,48,3,1536]{3,1,2,0:T(8,128)(2,1)} %param.6) | copy-start | bytes 1327108
  0.6 12.5 %copy-start.6 = (s32[1,64,128]{2,1,0:T(8,128)S(1)}, s32[1,64,128]{2,1,0:T(8,128)}, u32[]{:S(2)}) copy-start(s32[1,64,128]{2,1,0:T(8,128)} %param.7) | copy-start | bytes 98308
  2.2 24.5 %all-to-all-start = ((bf16[16,20,512]{2,1,0:T(8,128)(2,1)}), bf16[16,20,512]{2,1,0:T(8,128)(2,1)S(1)}, u32[]{:S(2)}, u32[]{:S(2)}) async-start(bf16[16,20,512]{2,1,0:T(8,128)(2,1)} %fan_out.1), calls=%async_computation | async-start | bytes 786432 | tf_op jit(solution)/shard_map/all_to_all | solution.py:312
  27.2 11.2 %collective-permute-start.3 = (bf16[320,512]{1,0:T(8,128)(2,1)S(1)}, bf16[320,512]{1,0:T(8,128)(2,1)S(1)}, u32[]{:S(2)}, u32[]{:S(2)}) collective-permute-start(bf16[320,512]{1,0:T(8,128)(2,1)S(1)} %pad_maximum_fusion.1), channel_id=1, source_target_pairs={{0,64},{1,17},{2,66},{3,19},{4,68},{5,21},{6,70},{7,23},{8,72},{9,... | collective-permute-start | bytes 983048 | tf_op jit(solution)/shard_map/ppermute | solution.py:30
  30.2 8.4 %collective-permute-start.2 = (bf16[320,512]{1,0:T(8,128)(2,1)S(1)}, bf16[320,512]{1,0:T(8,128)(2,1)S(1)}, u32[]{:S(2)}, u32[]{:S(2)}) collective-permute-start(bf16[320,512]{1,0:T(8,128)(2,1)S(1)} %pad_maximum_fusion.1), channel_id=1, source_target_pairs={{0,96},{1,25},{2,98},{3,27},{4,100},{5,29},{6,102},{7,31},{8,104},... | collective-permute-start | bytes 983048 | tf_op jit(solution)/shard_map/ppermute | solution.py:30
  30.9 7.6 %collective-permute-start.1 = (bf16[320,512]{1,0:T(8,128)(2,1)S(1)}, bf16[320,512]{1,0:T(8,128)(2,1)S(1)}, u32[]{:S(2)}, u32[]{:S(2)}) collective-permute-start(bf16[320,512]{1,0:T(8,128)(2,1)S(1)} %pad_maximum_fusion.1), channel_id=1, source_target_pairs={{0,32},{1,9},{2,34},{3,11},{4,36},{5,13},{6,38},{7,15},{8,40},{9,1... | collective-permute-start | bytes 983048 | tf_op jit(solution)/shard_map/ppermute | solution.py:30
  31.6 41.4 %all-to-all-start.1 = ((bf16[32,8,1536]{2,1,0:T(8,128)(2,1)}), bf16[32,8,1536]{2,1,0:T(8,128)(2,1)S(1)}, u32[]{:S(2)}, u32[]{:S(2)}) async-start(bf16[32,8,1536]{2,1,0:T(8,128)(2,1)} %fusion), calls=%async_computation.1 | async-start | bytes 1572864 | tf_op jit(solution)/shard_map/all_to_all | solution.py:339
  38.6 0.7 copy-start.5
  40.5 16.0 %collective-permute-start.4 = (bf16[4,320,256]{2,1,0:T(8,128)(2,1)S(1)}, bf16[4,320,256]{2,1,0:T(8,128)(2,1)S(1)}, u32[]{:S(2)}, u32[]{:S(2)}) collective-permute-start(bf16[4,320,256]{2,1,0:T(8,128)(2,1)S(1)} %get-tuple-element.28), channel_id=1, source_target_pairs={{0,24},{1,97},{2,26},{3,99},{4,28},{5,101},{6,30},{7,103},{8,0},{9... | collective-permute-start | bytes 1966088 | tf_op jit(solution)/shard_map/ppermute | solution.py:30
  43.1 15.8 %collective-permute-start.7 = (bf16[4,320,256]{2,1,0:T(8,128)(2,1)S(1)}, bf16[4,320,256]{2,1,0:T(8,128)(2,1)}, u32[]{:S(2)}, u32[]{:S(2)}) collective-permute-start(bf16[4,320,256]{2,1,0:T(8,128)(2,1)S(1)} %get-tuple-element.28), channel_id=1, source_target_pairs={{0,8},{1,33},{2,10},{3,35},{4,12},{5,37},{6,14},{7,39},{8,16},{9,4... | collective-permute-start | bytes 1966088 | tf_op jit(solution)/shard_map/ppermute | solution.py:30
  43.1 20.4 %collective-permute-start.8 = (bf16[4,320,256]{2,1,0:T(8,128)(2,1)S(1)}, bf16[4,320,256]{2,1,0:T(8,128)(2,1)}, u32[]{:S(2)}, u32[]{:S(2)}) collective-permute-start(bf16[4,320,256]{2,1,0:T(8,128)(2,1)S(1)} %get-tuple-element.31), channel_id=1, source_target_pairs={{0,24},{1,97},{2,26},{3,99},{4,28},{5,101},{6,30},{7,103},{8,0},{9... | collective-permute-start | bytes 1966088 | tf_op jit(solution)/shard_map/ppermute | solution.py:30
  45.8 19.7 %collective-permute-start.6 = (bf16[4,320,256]{2,1,0:T(8,128)(2,1)S(1)}, bf16[4,320,256]{2,1,0:T(8,128)(2,1)}, u32[]{:S(2)}, u32[]{:S(2)}) collective-permute-start(bf16[4,320,256]{2,1,0:T(8,128)(2,1)S(1)} %get-tuple-element.31), channel_id=1, source_target_pairs={{0,8},{1,33},{2,10},{3,35},{4,12},{5,37},{6,14},{7,39},{8,16},{9,4... | collective-permute-start | bytes 1966088 | tf_op jit(solution)/shard_map/ppermute | solution.py:30
  56.5 13.9 %collective-permute-start.5 = (bf16[4,320,256]{2,1,0:T(8,128)(2,1)S(1)}, bf16[4,320,256]{2,1,0:T(8,128)(2,1)S(1)}, u32[]{:S(2)}, u32[]{:S(2)}) collective-permute-start(bf16[4,320,256]{2,1,0:T(8,128)(2,1)S(1)} %collective-permute-done.4.refs_2_), channel_id=1, source_target_pairs={{0,24},{1,97},{2,26},{3,99},{4,28},{5,101},{6,30},{7,103},{8,0},{9... | collective-permute-start | bytes 1966088 | tf_op jit(solution)/shard_map/ppermute | solution.py:30
  58.9 14.2 %collective-permute-start.13 = (bf16[4,320,256]{2,1,0:T(8,128)(2,1)}, bf16[4,320,256]{2,1,0:T(8,128)(2,1)}, u32[]{:S(2)}, u32[]{:S(2)}) collective-permute-start(bf16[4,320,256]{2,1,0:T(8,128)(2,1)} %collective-permute-done.7.refs_3_), channel_id=1, source_target_pairs={{0,1},{1,0},{2,3},{3,2},{4,5},{5,4},{6,7},{7,6},{8,9},{9,8},{10,11... | collective-permute-start | bytes 1966088 | tf_op jit(solution)/shard_map/ppermute | solution.py:30
  61.2 12.0 %collective-permute-start.12 = (bf16[4,320,256]{2,1,0:T(8,128)(2,1)S(1)}, bf16[4,320,256]{2,1,0:T(8,128)(2,1)}, u32[]{:S(2)}, u32[]{:S(2)}) collective-permute-start(bf16[4,320,256]{2,1,0:T(8,128)(2,1)S(1)} %collective-permute-done.4.refs_2_), channel_id=1, source_target_pairs={{0,1},{1,0},{2,3},{3,2},{4,5},{5,4},{6,7},{7,6},{8,9},{9,8},{10,11... | collective-permute-start | bytes 1966088 | tf_op jit(solution)/shard_map/ppermute | solution.py:30
  63.5 16.5 %collective-permute-start.10 = (bf16[4,320,512]{2,1,0:T(8,128)(2,1)S(1)}, bf16[4,320,512]{2,1,0:T(8,128)(2,1)}, u32[]{:S(2)}, u32[]{:S(2)}) collective-permute-start(bf16[4,320,512]{2,1,0:T(8,128)(2,1)S(1)} %pad_maximum_fusion.refs_0_), channel_id=1, source_target_pairs={{0,1},{1,0},{2,3},{3,2},{4,5},{5,4},{6,7},{7,6},{8,9},{9,8},{10,11... | collective-permute-start | bytes 3932168 | tf_op jit(solution)/shard_map/ppermute | solution.py:30
  65.5 11.3 %collective-permute-start.9 = (bf16[4,320,256]{2,1,0:T(8,128)(2,1)}, bf16[4,320,256]{2,1,0:T(8,128)(2,1)}, u32[]{:S(2)}, u32[]{:S(2)}) collective-permute-start(bf16[4,320,256]{2,1,0:T(8,128)(2,1)} %collective-permute-done.6.refs_1_), channel_id=1, source_target_pairs={{0,8},{1,33},{2,10},{3,35},{4,12},{5,37},{6,14},{7,39},{8,16},{9,4... | collective-permute-start | bytes 1966088 | tf_op jit(solution)/shard_map/ppermute | solution.py:30
  70.4 0.9 copy-start.3
  71.3 8.6 %collective-permute-start.14 = (bf16[4,320,256]{2,1,0:T(8,128)(2,1)}, bf16[4,320,256]{2,1,0:T(8,128)(2,1)}, u32[]{:S(2)}, u32[]{:S(2)}) collective-permute-start(bf16[4,320,256]{2,1,0:T(8,128)(2,1)} %collective-permute-done.8.refs_4_), channel_id=1, source_target_pairs={{0,1},{1,0},{2,3},{3,2},{4,5},{5,4},{6,7},{7,6},{8,9},{9,8},{10,11... | collective-permute-start | bytes 1966088 | tf_op jit(solution)/shard_map/ppermute | solution.py:30
  73.0 7.0 %collective-permute-start.11 = (bf16[4,320,256]{2,1,0:T(8,128)(2,1)}, bf16[4,320,256]{2,1,0:T(8,128)(2,1)}, u32[]{:S(2)}, u32[]{:S(2)}) collective-permute-start(bf16[4,320,256]{2,1,0:T(8,128)(2,1)} %collective-permute-done.6.refs_1_), channel_id=1, source_target_pairs={{0,1},{1,0},{2,3},{3,2},{4,5},{5,4},{6,7},{7,6},{8,9},{9,8},{10,11... | collective-permute-start | bytes 1966088 | tf_op jit(solution)/shard_map/ppermute | solution.py:30
  73.1 6.9 %collective-permute-start.16 = (bf16[4,320,256]{2,1,0:T(8,128)(2,1)}, bf16[4,320,256]{2,1,0:T(8,128)(2,1)}, u32[]{:S(2)}, u32[]{:S(2)}) collective-permute-start(bf16[4,320,256]{2,1,0:T(8,128)(2,1)} %copy-done.3), channel_id=1, source_target_pairs={{0,1},{1,0},{2,3},{3,2},{4,5},{5,4},{6,7},{7,6},{8,9},{9,8},{10,11... | collective-permute-start | bytes 1966088 | tf_op jit(solution)/shard_map/ppermute | solution.py:30
  76.7 5.3 %collective-permute-start.15 = (bf16[4,320,256]{2,1,0:T(8,128)(2,1)}, bf16[4,320,256]{2,1,0:T(8,128)(2,1)}, u32[]{:S(2)}, u32[]{:S(2)}) collective-permute-start(bf16[4,320,256]{2,1,0:T(8,128)(2,1)} %collective-permute-done.9.refs_5_), channel_id=1, source_target_pairs={{0,1},{1,0},{2,3},{3,2},{4,5},{5,4},{6,7},{7,6},{8,9},{9,8},{10,11... | collective-permute-start | bytes 1966088 | tf_op jit(solution)/shard_map/ppermute | solution.py:30
  79.9 12.0 %collective-permute-start = (bf16[3584,256]{1,0:T(8,128)(2,1)}, bf16[3584,256]{1,0:T(8,128)(2,1)}, u32[]{:S(2)}, u32[]{:S(2)}) collective-permute-start(bf16[3584,256]{1,0:T(8,128)(2,1)} %bitcast.48), channel_id=1, source_target_pairs={{0,1},{1,0},{2,3},{3,2},{4,5},{5,4},{6,7},{7,6},{8,9},{9,8},{10,11... | collective-permute-start | bytes 5505032 | tf_op jit(solution)/shard_map/ppermute | solution.py:30
  82.0 1.1 copy-start.4
  83.1 11.3 %copy-start.2 = (bf16[1,256,3584]{1,2,0:T(8,128)(2,1)S(1)}, bf16[1,256,3584]{1,2,0:T(8,128)(2,1)}, u32[]{:S(2)}) copy-start(bf16[1,256,3584]{1,2,0:T(8,128)(2,1)} %copy.13) | copy-start | bytes 5505028
  91.5 2.9 %collective-permute-start.17 = (bf16[256,2304]{1,0:T(8,128)(2,1)S(1)}, bf16[256,2304]{1,0:T(8,128)(2,1)S(1)}, u32[]{:S(2)}, u32[]{:S(2)}) collective-permute-start(bf16[256,2304]{1,0:T(8,128)(2,1)S(1)} %get-tuple-element.34), channel_id=1, source_target_pairs={{0,1},{1,0},{2,3},{3,2},{4,5},{5,4},{6,7},{7,6},{8,9},{9,8},{10,11... | collective-permute-start | bytes 3538952 | tf_op jit(solution)/shard_map/ppermute | solution.py:30
  94.4 19.1 %copy-start.1 = (bf16[16,224,1024]{2,1,0:T(8,128)(2,1)S(1)}, bf16[16,224,1024]{2,1,0:T(8,128)(2,1)}, u32[]{:S(2)}) copy-start(bf16[16,224,1024]{2,1,0:T(8,128)(2,1)} %get-tuple-element.38.w_in) | copy-start | bytes 22020100
  99.4 11.0 %collective-permute-start.18 = (bf16[4,320,256]{2,1,0:T(8,128)(2,1)S(1)}, bf16[4,320,256]{2,1,0:T(8,128)(2,1)S(1)}, u32[]{:S(2)}, u32[]{:S(2)}) collective-permute-start(bf16[4,320,256]{2,1,0:T(8,128)(2,1)S(1)} %get-tuple-element.36), channel_id=1, source_target_pairs={{0,8},{1,33},{2,10},{3,35},{4,12},{5,37},{6,14},{7,39},{8,16},{9,4... | collective-permute-start | bytes 1966088 | tf_op jit(solution)/shard_map/ppermute | solution.py:30
  100.5 10.2 %collective-permute-start.22 = (bf16[4,320,256]{2,1,0:T(8,128)(2,1)S(1)}, bf16[4,320,256]{2,1,0:T(8,128)(2,1)S(1)}, u32[]{:S(2)}, u32[]{:S(2)}) collective-permute-start(bf16[4,320,256]{2,1,0:T(8,128)(2,1)S(1)} %get-tuple-element.46), channel_id=1, source_target_pairs={{0,24},{1,97},{2,26},{3,99},{4,28},{5,101},{6,30},{7,103},{8,0},{9... | collective-permute-start | bytes 1966088 | tf_op jit(solution)/shard_map/ppermute | solution.py:30
  102.1 22.3 %collective-permute-start.20 = (bf16[4,320,256]{2,1,0:T(8,128)(2,1)S(1)}, bf16[4,320,256]{2,1,0:T(8,128)(2,1)S(1)}, u32[]{:S(2)}, u32[]{:S(2)}) collective-permute-start(bf16[4,320,256]{2,1,0:T(8,128)(2,1)S(1)} %get-tuple-element.42), channel_id=1, source_target_pairs={{0,24},{1,97},{2,26},{3,99},{4,28},{5,101},{6,30},{7,103},{8,0},{9... | collective-permute-start | bytes 1966088 | tf_op jit(solution)/shard_map/ppermute | solution.py:30
  102.9 21.8 %collective-permute-start.21 = (bf16[4,320,256]{2,1,0:T(8,128)(2,1)S(1)}, bf16[4,320,256]{2,1,0:T(8,128)(2,1)S(1)}, u32[]{:S(2)}, u32[]{:S(2)}) collective-permute-start(bf16[4,320,256]{2,1,0:T(8,128)(2,1)S(1)} %get-tuple-element.44), channel_id=1, source_target_pairs={{0,8},{1,33},{2,10},{3,35},{4,12},{5,37},{6,14},{7,39},{8,16},{9,4... | collective-permute-start | bytes 1966088 | tf_op jit(solution)/shard_map/ppermute | solution.py:30
  110.6 13.9 %collective-permute-start.19 = (bf16[4,320,256]{2,1,0:T(8,128)(2,1)S(1)}, bf16[4,320,256]{2,1,0:T(8,128)(2,1)S(1)}, u32[]{:S(2)}, u32[]{:S(2)}) collective-permute-start(bf16[4,320,256]{2,1,0:T(8,128)(2,1)S(1)} %add_convert_fusion.1), channel_id=1, source_target_pairs={{0,8},{1,33},{2,10},{3,35},{4,12},{5,37},{6,14},{7,39},{8,16},{9,4... | collective-permute-start | bytes 1966088 | tf_op jit(solution)/shard_map/ppermute | solution.py:30
  110.8 13.9 %collective-permute-start.23 = (bf16[4,320,256]{2,1,0:T(8,128)(2,1)S(1)}, bf16[4,320,256]{2,1,0:T(8,128)(2,1)S(1)}, u32[]{:S(2)}, u32[]{:S(2)}) collective-permute-start(bf16[4,320,256]{2,1,0:T(8,128)(2,1)S(1)} %add_convert_fusion), channel_id=1, source_target_pairs={{0,24},{1,97},{2,26},{3,99},{4,28},{5,101},{6,30},{7,103},{8,0},{9... | collective-permute-start | bytes 1966088 | tf_op jit(solution)/shard_map/ppermute | solution.py:30
  125.0 11.0 %collective-permute-start.24 = (bf16[320,512]{1,0:T(8,128)(2,1)S(1)}, bf16[320,512]{1,0:T(8,128)(2,1)S(1)}, u32[]{:S(2)}, u32[]{:S(2)}) collective-permute-start(bf16[320,512]{1,0:T(8,128)(2,1)S(1)} %pad_maximum_fusion.2), channel_id=1, source_target_pairs={{0,32},{1,9},{2,34},{3,11},{4,36},{5,13},{6,38},{7,15},{8,40},{9,1... | collective-permute-start | bytes 983048 | tf_op jit(solution)/shard_map/ppermute | solution.py:30
  125.1 10.9 %collective-permute-start.25 = (bf16[320,512]{1,0:T(8,128)(2,1)S(1)}, bf16[320,512]{1,0:T(8,128)(2,1)S(1)}, u32[]{:S(2)}, u32[]{:S(2)}) collective-permute-start(bf16[320,512]{1,0:T(8,128)(2,1)S(1)} %pad_maximum_fusion.3), channel_id=1, source_target_pairs={{0,96},{1,25},{2,98},{3,27},{4,100},{5,29},{6,102},{7,31},{8,104},... | collective-permute-start | bytes 983048 | tf_op jit(solution)/shard_map/ppermute | solution.py:30
  127.9 8.1 %collective-permute-start.26 = (bf16[320,512]{1,0:T(8,128)(2,1)S(1)}, bf16[320,512]{1,0:T(8,128)(2,1)S(1)}, u32[]{:S(2)}, u32[]{:S(2)}) collective-permute-start(bf16[320,512]{1,0:T(8,128)(2,1)S(1)} %pad_maximum_fusion.4), channel_id=1, source_target_pairs={{0,64},{1,17},{2,66},{3,19},{4,68},{5,21},{6,70},{7,23},{8,72},{9,... | collective-permute-start | bytes 983048 | tf_op jit(solution)/shard_map/ppermute | solution.py:30

commit v5 on v4

--- a/solution.py
+++ b/solution.py
@@ -346,7 +346,7 @@
     left1, right3 = second_axis(left, 1), second_axis(right, 3)
     right1, left3 = second_axis(right, 1), second_axis(left, 3)
     left2, right2 = second_axis(left1, 1), second_axis(right3, 3)
-    right2, picked = lax.optimization_barrier((right2, picked))
+    right2, left2, picked = lax.optimization_barrier((right2, left2, picked))
     own = [line, left1, right3, right1, left3, left2, right2]
     oth = [swap_cores(v) for v in own]
 

time: 163 us -> 162 us (level)
  starting transfers between devices: 49.5 us -> 47 us
    ppermute x27, starting transfers between devices: 32.8 us -> 30.3 us  [permute(): return lax.ppermute(v, AXES, pairs)]
    unnamed x16 -> x20, local copies, waits for them, and re-layouts: 6.49 us -> 7.59 us
  transfers between devices with their start and end apart: 29 -> 29, of which waited for: 12 -> 13; matrix products, arithmetic and copies ran while one was open for 5% -> 5% of each run, Pallas kernels for 8% -> 8%
where the time goes in v5:
time: 162 us; the launch traced here: 161 us
  waiting for transfers between devices  54.8 us (34%)
  starting transfers between devices  47 us (29%)
  blocking collectives  24.4 us (15%)
  Pallas kernels  20.8 us (13%)
  local copies, waits for them, and re-layouts  8.42 us (5%)
  other arithmetic  3.38 us (2%)
    ppermute x27, waiting for transfers between devices, permute(): return lax.ppermute(v, AXES, pairs)  46.7 us
    ppermute x27, starting transfers between devices, permute(): return lax.ppermute(v, AXES, pairs)  30.3 us
    all_to_all x1, blocking collectives, per_device(): lax.all_to_all(jnp.concatenate([mine[:224].reshape(16, 14, HH), mine[224:...  24.4 us
    all_to_all x1, starting transfers between devices, per_device(): lax.all_to_all(fan_out(proj_in, proj_out), ('zh', 'zl', 'c'), split_axis=...  9.98 us
    pallas_call x1, Pallas kernels, head(): pl.pallas_call(head_kernel, in_specs=[pl.BlockSpec(memory_space=pltpu.SME...  8.24 us
    all_to_all x1, waiting for transfers between devices, per_device(): lax.all_to_all(fan_out(proj_in, proj_out), ('zh', 'zl', 'c'), split_axis=...  8.14 us
    unnamed x20, local copies, waits for them, and re-layouts  7.59 us
    all_to_all x1, starting transfers between devices, per_device(): lax.all_to_all(sent, ('zh', 'x', 'y'), split_axis=0, concat_axis=0, tiled...  6.73 us
  transfers between devices with their start and end apart: 29, of which 13 were waited for; matrix products, arithmetic and copies ran while one was open for 5% of the time, Pallas kernels for 8%

profile of v5, /device:TPU:1, one launch (start us, length us, event | category | flops | bytes accessed | tf_op | source)
XLA Modules:
  0.0 161.1 jit_solution(4981350890284042970)
XLA Ops:
  0.7 1.6 fan_out.1
  2.2 10.0 %all-to-all-start = ((bf16[16,20,512]{2,1,0:T(8,128)(2,1)}), bf16[16,20,512]{2,1,0:T(8,128)(2,1)S(1)}, u32[]{:S(2)}, u32[]{:S(2)}) async-start(bf16[16,20,512]{2,1,0:T(8,128)(2,1)} %fan_out.1), calls=%async_computation | async-start | bytes 786432 | tf_op jit(solution)/shard_map/all_to_all | solution.py:312
  12.2 0.8 sign_compare_fusion
  13.1 0.1 ne.39
  13.2 0.1 dynamic-slice_remainder_fusion
  13.3 0.1 rem.24
  13.4 0.1 div.14
  13.5 3.8 %copy.13 = bf16[1,256,3584]{1,2,0:T(8,128)(2,1)} copy(bf16[1,256,3584]{2,1,0:T(8,128)(2,1)} %param.5) | data formatting | bytes 3670016 | tf_op args[0]
  17.3 1.3 fusion
  18.6 8.1 %all-to-all-done = bf16[16,20,512]{2,1,0:T(8,128)(2,1)S(1)} async-done(((bf16[16,20,512]{2,1,0:T(8,128)(2,1)}), bf16[16,20,512]{2,1,0:T(8,128)(2,1)S(1)}, u32[]{:S(2)}, u32[]{:S(2)}) %all-to-all-start) | async-done | bytes 327712 | tf_op jit(solution)/shard_map/all_to_all | solution.py:312
  27.2 3.0 %collective-permute-start.3 = (bf16[320,512]{1,0:T(8,128)(2,1)S(1)}, bf16[320,512]{1,0:T(8,128)(2,1)S(1)}, u32[]{:S(2)}, u32[]{:S(2)}) collective-permute-start(bf16[320,512]{1,0:T(8,128)(2,1)S(1)} %pad_maximum_fusion.1), channel_id=1, source_target_pairs={{0,64},{1,17},{2,66},{3,19},{4,68},{5,21},{6,70},{7,23},{8,72},{9,... | collective-permute-start | bytes 983048 | tf_op jit(solution)/shard_map/ppermute | solution.py:30
  30.2 0.8 collective-permute-start.2
  30.9 0.7 collective-permute-start.1
  31.6 6.7 %all-to-all-start.1 = ((bf16[32,8,1536]{2,1,0:T(8,128)(2,1)}), bf16[32,8,1536]{2,1,0:T(8,128)(2,1)S(1)}, u32[]{:S(2)}, u32[]{:S(2)}) async-start(bf16[32,8,1536]{2,1,0:T(8,128)(2,1)} %fusion), calls=%async_computation.1 | async-start | bytes 1572864 | tf_op jit(solution)/shard_map/all_to_all | solution.py:339
  38.4 0.2 collective-permute-done.2
  38.6 0.7 copy-done.7
  39.3 1.1 pad_maximum_fusion.refs_0_
  40.4 0.1 fusion.12
  40.5 2.6 %collective-permute-start.4 = (bf16[4,320,256]{2,1,0:T(8,128)(2,1)S(1)}, bf16[4,320,256]{2,1,0:T(8,128)(2,1)S(1)}, u32[]{:S(2)}, u32[]{:S(2)}) collective-permute-start(bf16[4,320,256]{2,1,0:T(8,128)(2,1)S(1)} %get-tuple-element.29), channel_id=1, source_target_pairs={{0,24},{1,97},{2,26},{3,99},{4,28},{5,101},{6,30},{7,103},{8,0},{9... | collective-permute-start | bytes 1966088 | tf_op jit(solution)/shard_map/ppermute | solution.py:30
  43.1 0.2 collective-permute-start.8
  43.3 2.5 %collective-permute-start.9 = (bf16[4,320,256]{2,1,0:T(8,128)(2,1)S(1)}, bf16[4,320,256]{2,1,0:T(8,128)(2,1)}, u32[]{:S(2)}, u32[]{:S(2)}) collective-permute-start(bf16[4,320,256]{2,1,0:T(8,128)(2,1)S(1)} %get-tuple-element.30), channel_id=1, source_target_pairs={{0,24},{1,97},{2,26},{3,99},{4,28},{5,101},{6,30},{7,103},{8,0},{9... | collective-permute-start | bytes 1966088 | tf_op jit(solution)/shard_map/ppermute | solution.py:30
  45.8 10.7 %collective-permute-done.4.refs_2_ = bf16[4,320,256]{2,1,0:T(8,128)(2,1)S(1)} collective-permute-done((bf16[4,320,256]{2,1,0:T(8,128)(2,1)S(1)}, bf16[4,320,256]{2,1,0:T(8,128)(2,1)S(1)}, u32[]{:S(2)}, u32[]{:S(2)}) %collective-permute-start.4) | collective-permute-done | bytes 655392 | tf_op jit(solution)/shard_map/ppermute | solution.py:30
  56.5 2.4 %collective-permute-start.5 = (bf16[4,320,256]{2,1,0:T(8,128)(2,1)S(1)}, bf16[4,320,256]{2,1,0:T(8,128)(2,1)S(1)}, u32[]{:S(2)}, u32[]{:S(2)}) collective-permute-start(bf16[4,320,256]{2,1,0:T(8,128)(2,1)S(1)} %collective-permute-done.4.refs_2_), channel_id=1, source_target_pairs={{0,24},{1,97},{2,26},{3,99},{4,28},{5,101},{6,30},{7,103},{8,0},{9... | collective-permute-start | bytes 1966088 | tf_op jit(solution)/shard_map/ppermute | solution.py:30
  58.9 6.6 %collective-permute-done.8.refs_3_ = bf16[4,320,256]{2,1,0:T(8,128)(2,1)} collective-permute-done((bf16[4,320,256]{2,1,0:T(8,128)(2,1)S(1)}, bf16[4,320,256]{2,1,0:T(8,128)(2,1)}, u32[]{:S(2)}, u32[]{:S(2)}) %collective-permute-start.8) | collective-permute-done | bytes 655392 | tf_op jit(solution)/shard_map/ppermute | solution.py:30
  65.5 2.4 %collective-permute-start.13 = (bf16[4,320,256]{2,1,0:T(8,128)(2,1)}, bf16[4,320,256]{2,1,0:T(8,128)(2,1)}, u32[]{:S(2)}, u32[]{:S(2)}) collective-permute-start(bf16[4,320,256]{2,1,0:T(8,128)(2,1)} %collective-permute-done.8.refs_3_), channel_id=1, source_target_pairs={{0,1},{1,0},{2,3},{3,2},{4,5},{5,4},{6,7},{7,6},{8,9},{9,8},{10,11... | collective-permute-start | bytes 1966088 | tf_op jit(solution)/shard_map/ppermute | solution.py:30
  67.8 0.5 collective-permute-start.12
  68.3 2.1 %collective-permute-done.5.refs_6_ = bf16[4,320,256]{2,1,0:T(8,128)(2,1)S(1)} collective-permute-done((bf16[4,320,256]{2,1,0:T(8,128)(2,1)S(1)}, bf16[4,320,256]{2,1,0:T(8,128)(2,1)S(1)}, u32[]{:S(2)}, u32[]{:S(2)}) %collective-permute-start.5) | collective-permute-done | bytes 655392 | tf_op jit(solution)/shard_map/ppermute | solution.py:30
  70.4 1.7 %collective-permute-start.14 = (bf16[4,320,256]{2,1,0:T(8,128)(2,1)}, bf16[4,320,256]{2,1,0:T(8,128)(2,1)}, u32[]{:S(2)}, u32[]{:S(2)}) collective-permute-start(bf16[4,320,256]{2,1,0:T(8,128)(2,1)} %collective-permute-done.9.refs_4_), channel_id=1, source_target_pairs={{0,1},{1,0},{2,3},{3,2},{4,5},{5,4},{6,7},{7,6},{8,9},{9,8},{10,11... | collective-permute-start | bytes 1966088 | tf_op jit(solution)/shard_map/ppermute | solution.py:30
  72.2 0.2 collective-permute-done.7.refs_5_
  72.4 0.9 copy-done.5
  73.2 2.4 %collective-permute-start.11 = (bf16[4,320,256]{2,1,0:T(8,128)(2,1)}, bf16[4,320,256]{2,1,0:T(8,128)(2,1)}, u32[]{:S(2)}, u32[]{:S(2)}) collective-permute-start(bf16[4,320,256]{2,1,0:T(8,128)(2,1)} %collective-permute-done.6.refs_1_), channel_id=1, source_target_pairs={{0,1},{1,0},{2,3},{3,2},{4,5},{5,4},{6,7},{7,6},{8,9},{9,8},{10,11... | collective-permute-start | bytes 1966088 | tf_op jit(solution)/shard_map/ppermute | solution.py:30
  75.6 0.3 collective-permute-start.15
  75.9 0.2 collective-permute-start.16
  76.1 0.3 collective-permute-start
  76.5 1.2 collective-permute-done.11.refs_8_
  77.7 0.9 collective-permute-done.15.refs_12_
  78.6 0.9 collective-permute-done.16.refs_13_
  79.5 1.1 copy-done.4
  80.6 1.1 copy-done.6
  81.7 8.2 %head.1 = (bf16[256,1024]{1,0:T(8,128)(2,1)S(1)}, bf16[256,2304]{1,0:T(8,128)(2,1)S(1)}, bf16[256,2304]{1,0:T(8,128)(2,1)S(1)}, bf16[16,224,1024]{2,1,0:T(8,128)(2,1)}) custom-call(s32[3]{0:T(128)S(1)} %pad_add_fusion.place, bf16[256,3584]{1,0:T(8,128)(2,1)} %bitcast.52, bf16[256,1536]{1,0:T(8,128)(2,1)S(1)} %bitcast.50, ...), custom_call_target="tpu_custom_call" | custom-call | flops 5000000000 | bytes 30000000 | tf_op jit(solution)/shard_map/head/pallas_call | solution.py:161
  90.0 0.5 collective-permute-start.17
  90.4 2.5 %collective-permute-done.17.rcv = bf16[256,2304]{1,0:T(8,128)(2,1)S(1)} collective-permute-done((bf16[256,2304]{1,0:T(8,128)(2,1)S(1)}, bf16[256,2304]{1,0:T(8,128)(2,1)S(1)}, u32[]{:S(2)}, u32[]{:S(2)}) %collective-permute-start.17) | collective-permute-done | bytes 1179680 | tf_op jit(solution)/shard_map/ppermute | solution.py:30
  92.9 4.9 %tail.1 = (bf16[4,320,256]{2,1,0:T(8,128)(2,1)S(1)}, bf16[4,320,256]{2,1,0:T(8,128)(2,1)S(1)}, bf16[4,320,256]{2,1,0:T(8,128)(2,1)S(1)}, bf16[4,320,256]{2,1,0:T...) custom-call(s32[3]{0:T(128)S(1)} %pad_add_fusion.place, ...), custom_call_target="tpu_custom_call" | custom-call | flops 2700000000 | bytes 12000000 | tf_op jit(solution)/shard_map/tail/pallas_call | solution.py:221
  97.9 1.1 collective-permute-start.18
  99.0 1.6 %collective-permute-start.22 = (bf16[4,320,256]{2,1,0:T(8,128)(2,1)S(1)}, bf16[4,320,256]{2,1,0:T(8,128)(2,1)S(1)}, u32[]{:S(2)}, u32[]{:S(2)}) collective-permute-start(bf16[4,320,256]{2,1,0:T(8,128)(2,1)S(1)} %get-tuple-element.48), channel_id=1, source_target_pairs={{0,24},{1,97},{2,26},{3,99},{4,28},{5,101},{6,30},{7,103},{8,0},{9... | collective-permute-start | bytes 1966088 | tf_op jit(solution)/shard_map/ppermute | solution.py:30
  100.6 0.7 collective-permute-start.20
  101.4 0.7 collective-permute-start.21
  102.1 6.8 %collective-permute-done.18 = bf16[4,320,256]{2,1,0:T(8,128)(2,1)S(1)} collective-permute-done((bf16[4,320,256]{2,1,0:T(8,128)(2,1)S(1)}, bf16[4,320,256]{2,1,0:T(8,128)(2,1)S(1)}, u32[]{:S(2)}, u32[]{:S(2)}) %collective-permute-start.18) | collective-permute-done | bytes 655392 | tf_op jit(solution)/shard_map/ppermute | solution.py:30
  108.9 0.2 add_convert_fusion.1
  109.1 0.1 collective-permute-start.19
  109.2 0.2 add_convert_fusion
  109.3 2.7 %collective-permute-start.23 = (bf16[4,320,256]{2,1,0:T(8,128)(2,1)S(1)}, bf16[4,320,256]{2,1,0:T(8,128)(2,1)S(1)}, u32[]{:S(2)}, u32[]{:S(2)}) collective-permute-start(bf16[4,320,256]{2,1,0:T(8,128)(2,1)S(1)} %add_convert_fusion), channel_id=1, source_target_pairs={{0,24},{1,97},{2,26},{3,99},{4,28},{5,101},{6,30},{7,103},{8,0},{9... | collective-permute-start | bytes 1966088 | tf_op jit(solution)/shard_map/ppermute | solution.py:30
  112.1 4.3 %back.1 = bf16[256,3584]{1,0:T(8,128)(2,1)} custom-call(bf16[256,1024]{1,0:T(8,128)(2,1)S(1)} %get-tuple-element.39.grad_pre, bf16[16,224,1024]{2,1,0:T(8,128)(2,1)S(1)} %copy-done.1), custom_call_target="tpu_custom_call" | custom-call | flops 1900000000 | bytes 10000000 | tf_op jit(solution)/shard_map/back/pallas_call | solution.py:242
  116.4 6.5 %collective-permute-done.19 = bf16[4,320,256]{2,1,0:T(8,128)(2,1)S(1)} collective-permute-done((bf16[4,320,256]{2,1,0:T(8,128)(2,1)S(1)}, bf16[4,320,256]{2,1,0:T(8,128)(2,1)S(1)}, u32[]{:S(2)}, u32[]{:S(2)}) %collective-permute-start.19) | collective-permute-done | bytes 655392 | tf_op jit(solution)/shard_map/ppermute | solution.py:30
  122.9 0.2 fusion.1
  123.2 0.2 fusion.2
  123.5 0.1 collective-permute-start.24
  123.6 2.7 %collective-permute-start.25 = (bf16[320,512]{1,0:T(8,128)(2,1)S(1)}, bf16[320,512]{1,0:T(8,128)(2,1)S(1)}, u32[]{:S(2)}, u32[]{:S(2)}) collective-permute-start(bf16[320,512]{1,0:T(8,128)(2,1)S(1)} %pad_maximum_fusion.3), channel_id=1, source_target_pairs={{0,96},{1,25},{2,98},{3,27},{4,100},{5,29},{6,102},{7,31},{8,104},... | collective-permute-start | bytes 983048 | tf_op jit(solution)/shard_map/ppermute | solution.py:30
  126.4 0.1 collective-permute-start.26
  126.5 8.0 %collective-permute-done.24 = bf16[320,512]{1,0:T(8,128)(2,1)S(1)} collective-permute-done((bf16[320,512]{1,0:T(8,128)(2,1)S(1)}, bf16[320,512]{1,0:T(8,128)(2,1)S(1)}, u32[]{:S(2)}, u32[]{:S(2)}) %collective-permute-start.24) | collective-permute-done | bytes 327712 | tf_op jit(solution)/shard_map/ppermute | solution.py:30
  134.5 0.2 add_convert_fusion.2
  134.9 0.1 maximum_maximum_fusion
  135.0 24.4 %all_to_all.15.last = bf16[16,20,512]{2,1,0:T(8,128)(2,1)} all-to-all(bf16[16,20,512]{2,1,0:T(8,128)(2,1)S(1)} %maximum_maximum_fusion), channel_id=1, replica_groups=mesh['zh'=2,'x'=4,'y'=4,'zl'=4,'c'=2] {'zh','zl','c'}, dimensions={0} | all-to-all | bytes 655360 | tf_op jit(solution)/shard_map/all_to_all | solution.py:376
  159.4 1.7 %fan_in.1 = (f32[14,1024]{1,0:T(8,128)}, f32[4,1536]{1,0:T(4,128)}) custom-call(bf16[16,20,512]{2,1,0:T(8,128)(2,1)} %all_to_all.15.last), custom_call_target="tpu_custom_call" | custom-call | tf_op jit(solution)/shard_map/fan_in/pallas_call | solution.py:298
  (56 shorter events, 0.7 us)
Async XLA Ops:
  0.6 16.7 %copy-start = (bf16[1,48,3,1536]{3,1,2,0:T(8,128)(2,1)S(1)}, bf16[1,48,3,1536]{3,1,2,0:T(8,128)(2,1)}, u32[]{:S(2)}) copy-start(bf16[1,48,3,1536]{3,1,2,0:T(8,128)(2,1)} %param.6) | copy-start | bytes 1327108
  0.6 12.5 %copy-start.8 = (s32[1,64,128]{2,1,0:T(8,128)S(1)}, s32[1,64,128]{2,1,0:T(8,128)}, u32[]{:S(2)}) copy-start(s32[1,64,128]{2,1,0:T(8,128)} %param.7) | copy-start | bytes 98308
  2.2 24.5 %all-to-all-start = ((bf16[16,20,512]{2,1,0:T(8,128)(2,1)}), bf16[16,20,512]{2,1,0:T(8,128)(2,1)S(1)}, u32[]{:S(2)}, u32[]{:S(2)}) async-start(bf16[16,20,512]{2,1,0:T(8,128)(2,1)} %fan_out.1), calls=%async_computation | async-start | bytes 786432 | tf_op jit(solution)/shard_map/all_to_all | solution.py:312
  27.2 11.2 %collective-permute-start.3 = (bf16[320,512]{1,0:T(8,128)(2,1)S(1)}, bf16[320,512]{1,0:T(8,128)(2,1)S(1)}, u32[]{:S(2)}, u32[]{:S(2)}) collective-permute-start(bf16[320,512]{1,0:T(8,128)(2,1)S(1)} %pad_maximum_fusion.1), channel_id=1, source_target_pairs={{0,64},{1,17},{2,66},{3,19},{4,68},{5,21},{6,70},{7,23},{8,72},{9,... | collective-permute-start | bytes 983048 | tf_op jit(solution)/shard_map/ppermute | solution.py:30
  30.2 8.4 %collective-permute-start.2 = (bf16[320,512]{1,0:T(8,128)(2,1)S(1)}, bf16[320,512]{1,0:T(8,128)(2,1)S(1)}, u32[]{:S(2)}, u32[]{:S(2)}) collective-permute-start(bf16[320,512]{1,0:T(8,128)(2,1)S(1)} %pad_maximum_fusion.1), channel_id=1, source_target_pairs={{0,96},{1,25},{2,98},{3,27},{4,100},{5,29},{6,102},{7,31},{8,104},... | collective-permute-start | bytes 983048 | tf_op jit(solution)/shard_map/ppermute | solution.py:30
  30.9 7.6 %collective-permute-start.1 = (bf16[320,512]{1,0:T(8,128)(2,1)S(1)}, bf16[320,512]{1,0:T(8,128)(2,1)S(1)}, u32[]{:S(2)}, u32[]{:S(2)}) collective-permute-start(bf16[320,512]{1,0:T(8,128)(2,1)S(1)} %pad_maximum_fusion.1), channel_id=1, source_target_pairs={{0,32},{1,9},{2,34},{3,11},{4,36},{5,13},{6,38},{7,15},{8,40},{9,1... | collective-permute-start | bytes 983048 | tf_op jit(solution)/shard_map/ppermute | solution.py:30
  31.6 44.0 %all-to-all-start.1 = ((bf16[32,8,1536]{2,1,0:T(8,128)(2,1)}), bf16[32,8,1536]{2,1,0:T(8,128)(2,1)S(1)}, u32[]{:S(2)}, u32[]{:S(2)}) async-start(bf16[32,8,1536]{2,1,0:T(8,128)(2,1)} %fusion), calls=%async_computation.1 | async-start | bytes 1572864 | tf_op jit(solution)/shard_map/all_to_all | solution.py:339
  38.6 0.7 copy-start.7
  40.5 16.0 %collective-permute-start.4 = (bf16[4,320,256]{2,1,0:T(8,128)(2,1)S(1)}, bf16[4,320,256]{2,1,0:T(8,128)(2,1)S(1)}, u32[]{:S(2)}, u32[]{:S(2)}) collective-permute-start(bf16[4,320,256]{2,1,0:T(8,128)(2,1)S(1)} %get-tuple-element.29), channel_id=1, source_target_pairs={{0,24},{1,97},{2,26},{3,99},{4,28},{5,101},{6,30},{7,103},{8,0},{9... | collective-permute-start | bytes 1966088 | tf_op jit(solution)/shard_map/ppermute | solution.py:30
  43.1 15.8 %collective-permute-start.6 = (bf16[4,320,256]{2,1,0:T(8,128)(2,1)S(1)}, bf16[4,320,256]{2,1,0:T(8,128)(2,1)}, u32[]{:S(2)}, u32[]{:S(2)}) collective-permute-start(bf16[4,320,256]{2,1,0:T(8,128)(2,1)S(1)} %get-tuple-element.30), channel_id=1, source_target_pairs={{0,8},{1,33},{2,10},{3,35},{4,12},{5,37},{6,14},{7,39},{8,16},{9,4... | collective-permute-start | bytes 1966088 | tf_op jit(solution)/shard_map/ppermute | solution.py:30
  43.1 22.4 %collective-permute-start.8 = (bf16[4,320,256]{2,1,0:T(8,128)(2,1)S(1)}, bf16[4,320,256]{2,1,0:T(8,128)(2,1)}, u32[]{:S(2)}, u32[]{:S(2)}) collective-permute-start(bf16[4,320,256]{2,1,0:T(8,128)(2,1)S(1)} %get-tuple-element.29), channel_id=1, source_target_pairs={{0,8},{1,33},{2,10},{3,35},{4,12},{5,37},{6,14},{7,39},{8,16},{9,4... | collective-permute-start | bytes 1966088 | tf_op jit(solution)/shard_map/ppermute | solution.py:30
  43.3 24.5 %collective-permute-start.9 = (bf16[4,320,256]{2,1,0:T(8,128)(2,1)S(1)}, bf16[4,320,256]{2,1,0:T(8,128)(2,1)}, u32[]{:S(2)}, u32[]{:S(2)}) collective-permute-start(bf16[4,320,256]{2,1,0:T(8,128)(2,1)S(1)} %get-tuple-element.30), channel_id=1, source_target_pairs={{0,24},{1,97},{2,26},{3,99},{4,28},{5,101},{6,30},{7,103},{8,0},{9... | collective-permute-start | bytes 1966088 | tf_op jit(solution)/shard_map/ppermute | solution.py:30
  56.5 13.9 %collective-permute-start.5 = (bf16[4,320,256]{2,1,0:T(8,128)(2,1)S(1)}, bf16[4,320,256]{2,1,0:T(8,128)(2,1)S(1)}, u32[]{:S(2)}, u32[]{:S(2)}) collective-permute-start(bf16[4,320,256]{2,1,0:T(8,128)(2,1)S(1)} %collective-permute-done.4.refs_2_), channel_id=1, source_target_pairs={{0,24},{1,97},{2,26},{3,99},{4,28},{5,101},{6,30},{7,103},{8,0},{9... | collective-permute-start | bytes 1966088 | tf_op jit(solution)/shard_map/ppermute | solution.py:30
  58.9 13.5 %collective-permute-start.7 = (bf16[4,320,256]{2,1,0:T(8,128)(2,1)}, bf16[4,320,256]{2,1,0:T(8,128)(2,1)S(1)}, u32[]{:S(2)}, u32[]{:S(2)}) collective-permute-start(bf16[4,320,256]{2,1,0:T(8,128)(2,1)} %collective-permute-done.6.refs_1_), channel_id=1, source_target_pairs={{0,8},{1,33},{2,10},{3,35},{4,12},{5,37},{6,14},{7,39},{8,16},{9,4... | collective-permute-start | bytes 1966088 | tf_op jit(solution)/shard_map/ppermute | solution.py:30
  65.5 10.1 %collective-permute-start.13 = (bf16[4,320,256]{2,1,0:T(8,128)(2,1)}, bf16[4,320,256]{2,1,0:T(8,128)(2,1)}, u32[]{:S(2)}, u32[]{:S(2)}) collective-permute-start(bf16[4,320,256]{2,1,0:T(8,128)(2,1)} %collective-permute-done.8.refs_3_), channel_id=1, source_target_pairs={{0,1},{1,0},{2,3},{3,2},{4,5},{5,4},{6,7},{7,6},{8,9},{9,8},{10,11... | collective-permute-start | bytes 1966088 | tf_op jit(solution)/shard_map/ppermute | solution.py:30
  67.8 9.9 %collective-permute-start.10 = (bf16[4,320,512]{2,1,0:T(8,128)(2,1)S(1)}, bf16[4,320,512]{2,1,0:T(8,128)(2,1)}, u32[]{:S(2)}, u32[]{:S(2)}) collective-permute-start(bf16[4,320,512]{2,1,0:T(8,128)(2,1)S(1)} %pad_maximum_fusion.refs_0_), channel_id=1, source_target_pairs={{0,1},{1,0},{2,3},{3,2},{4,5},{5,4},{6,7},{7,6},{8,9},{9,8},{10,11... | collective-permute-start | bytes 3932168 | tf_op jit(solution)/shard_map/ppermute | solution.py:30
  67.8 8.1 %collective-permute-start.12 = (bf16[4,320,256]{2,1,0:T(8,128)(2,1)S(1)}, bf16[4,320,256]{2,1,0:T(8,128)(2,1)}, u32[]{:S(2)}, u32[]{:S(2)}) collective-permute-start(bf16[4,320,256]{2,1,0:T(8,128)(2,1)S(1)} %collective-permute-done.4.refs_2_), channel_id=1, source_target_pairs={{0,1},{1,0},{2,3},{3,2},{4,5},{5,4},{6,7},{7,6},{8,9},{9,8},{10,11... | collective-permute-start | bytes 1966088 | tf_op jit(solution)/shard_map/ppermute | solution.py:30
  70.4 1.9 %copy-start.3 = (bf16[4,320,256]{2,1,0:T(8,128)(2,1)}, bf16[4,320,256]{2,1,0:T(8,128)(2,1)S(1)}, u32[]{:S(2)}) copy-start(bf16[4,320,256]{2,1,0:T(8,128)(2,1)S(1)} %collective-permute-done.5.refs_6_) | copy-start | bytes 1966084
  70.4 5.7 %collective-permute-start.14 = (bf16[4,320,256]{2,1,0:T(8,128)(2,1)}, bf16[4,320,256]{2,1,0:T(8,128)(2,1)}, u32[]{:S(2)}, u32[]{:S(2)}) collective-permute-start(bf16[4,320,256]{2,1,0:T(8,128)(2,1)} %collective-permute-done.9.refs_4_), channel_id=1, source_target_pairs={{0,1},{1,0},{2,3},{3,2},{4,5},{5,4},{6,7},{7,6},{8,9},{9,8},{10,11... | collective-permute-start | bytes 1966088 | tf_op jit(solution)/shard_map/ppermute | solution.py:30
  72.4 0.9 copy-start.5
  73.2 4.4 %collective-permute-start.11 = (bf16[4,320,256]{2,1,0:T(8,128)(2,1)}, bf16[4,320,256]{2,1,0:T(8,128)(2,1)}, u32[]{:S(2)}, u32[]{:S(2)}) collective-permute-start(bf16[4,320,256]{2,1,0:T(8,128)(2,1)} %collective-permute-done.6.refs_1_), channel_id=1, source_target_pairs={{0,1},{1,0},{2,3},{3,2},{4,5},{5,4},{6,7},{7,6},{8,9},{9,8},{10,11... | collective-permute-start | bytes 1966088 | tf_op jit(solution)/shard_map/ppermute | solution.py:30
  75.6 3.0 %collective-permute-start.15 = (bf16[4,320,256]{2,1,0:T(8,128)(2,1)}, bf16[4,320,256]{2,1,0:T(8,128)(2,1)}, u32[]{:S(2)}, u32[]{:S(2)}) collective-permute-start(bf16[4,320,256]{2,1,0:T(8,128)(2,1)} %copy-done.5), channel_id=1, source_target_pairs={{0,1},{1,0},{2,3},{3,2},{4,5},{5,4},{6,7},{7,6},{8,9},{9,8},{10,11... | collective-permute-start | bytes 1966088 | tf_op jit(solution)/shard_map/ppermute | solution.py:30
  75.9 3.7 %collective-permute-start.16 = (bf16[4,320,256]{2,1,0:T(8,128)(2,1)}, bf16[4,320,256]{2,1,0:T(8,128)(2,1)}, u32[]{:S(2)}, u32[]{:S(2)}) collective-permute-start(bf16[4,320,256]{2,1,0:T(8,128)(2,1)} %copy-done.3), channel_id=1, source_target_pairs={{0,1},{1,0},{2,3},{3,2},{4,5},{5,4},{6,7},{7,6},{8,9},{9,8},{10,11... | collective-permute-start | bytes 1966088 | tf_op jit(solution)/shard_map/ppermute | solution.py:30
  76.1 14.3 %collective-permute-start = (bf16[3584,256]{1,0:T(8,128)(2,1)}, bf16[3584,256]{1,0:T(8,128)(2,1)}, u32[]{:S(2)}, u32[]{:S(2)}) collective-permute-start(bf16[3584,256]{1,0:T(8,128)(2,1)} %bitcast.48), channel_id=1, source_target_pairs={{0,1},{1,0},{2,3},{3,2},{4,5},{5,4},{6,7},{7,6},{8,9},{9,8},{10,11... | collective-permute-start | bytes 5505032 | tf_op jit(solution)/shard_map/ppermute | solution.py:30
  79.5 1.1 copy-start.4
  80.6 1.1 copy-start.6
  81.7 11.2 %copy-start.2 = (bf16[1,256,3584]{1,2,0:T(8,128)(2,1)S(1)}, bf16[1,256,3584]{1,2,0:T(8,128)(2,1)}, u32[]{:S(2)}) copy-start(bf16[1,256,3584]{1,2,0:T(8,128)(2,1)} %copy.13) | copy-start | bytes 5505028
  90.0 3.0 %collective-permute-start.17 = (bf16[256,2304]{1,0:T(8,128)(2,1)S(1)}, bf16[256,2304]{1,0:T(8,128)(2,1)S(1)}, u32[]{:S(2)}, u32[]{:S(2)}) collective-permute-start(bf16[256,2304]{1,0:T(8,128)(2,1)S(1)} %get-tuple-element.36), channel_id=1, source_target_pairs={{0,1},{1,0},{2,3},{3,2},{4,5},{5,4},{6,7},{7,6},{8,9},{9,8},{10,11... | collective-permute-start | bytes 3538952 | tf_op jit(solution)/shard_map/ppermute | solution.py:30
  92.9 19.1 %copy-start.1 = (bf16[16,224,1024]{2,1,0:T(8,128)(2,1)S(1)}, bf16[16,224,1024]{2,1,0:T(8,128)(2,1)}, u32[]{:S(2)}) copy-start(bf16[16,224,1024]{2,1,0:T(8,128)(2,1)} %get-tuple-element.40.w_in) | copy-start | bytes 22020100
  97.9 11.0 %collective-permute-start.18 = (bf16[4,320,256]{2,1,0:T(8,128)(2,1)S(1)}, bf16[4,320,256]{2,1,0:T(8,128)(2,1)S(1)}, u32[]{:S(2)}, u32[]{:S(2)}) collective-permute-start(bf16[4,320,256]{2,1,0:T(8,128)(2,1)S(1)} %get-tuple-element.38), channel_id=1, source_target_pairs={{0,8},{1,33},{2,10},{3,35},{4,12},{5,37},{6,14},{7,39},{8,16},{9,4... | collective-permute-start | bytes 1966088 | tf_op jit(solution)/shard_map/ppermute | solution.py:30
  99.0 10.2 %collective-permute-start.22 = (bf16[4,320,256]{2,1,0:T(8,128)(2,1)S(1)}, bf16[4,320,256]{2,1,0:T(8,128)(2,1)S(1)}, u32[]{:S(2)}, u32[]{:S(2)}) collective-permute-start(bf16[4,320,256]{2,1,0:T(8,128)(2,1)S(1)} %get-tuple-element.48), channel_id=1, source_target_pairs={{0,24},{1,97},{2,26},{3,99},{4,28},{5,101},{6,30},{7,103},{8,0},{9... | collective-permute-start | bytes 1966088 | tf_op jit(solution)/shard_map/ppermute | solution.py:30
  100.6 22.3 %collective-permute-start.20 = (bf16[4,320,256]{2,1,0:T(8,128)(2,1)S(1)}, bf16[4,320,256]{2,1,0:T(8,128)(2,1)S(1)}, u32[]{:S(2)}, u32[]{:S(2)}) collective-permute-start(bf16[4,320,256]{2,1,0:T(8,128)(2,1)S(1)} %get-tuple-element.44), channel_id=1, source_target_pairs={{0,24},{1,97},{2,26},{3,99},{4,28},{5,101},{6,30},{7,103},{8,0},{9... | collective-permute-start | bytes 1966088 | tf_op jit(solution)/shard_map/ppermute | solution.py:30
  101.4 21.8 %collective-permute-start.21 = (bf16[4,320,256]{2,1,0:T(8,128)(2,1)S(1)}, bf16[4,320,256]{2,1,0:T(8,128)(2,1)S(1)}, u32[]{:S(2)}, u32[]{:S(2)}) collective-permute-start(bf16[4,320,256]{2,1,0:T(8,128)(2,1)S(1)} %get-tuple-element.46), channel_id=1, source_target_pairs={{0,8},{1,33},{2,10},{3,35},{4,12},{5,37},{6,14},{7,39},{8,16},{9,4... | collective-permute-start | bytes 1966088 | tf_op jit(solution)/shard_map/ppermute | solution.py:30
  109.1 13.9 %collective-permute-start.19 = (bf16[4,320,256]{2,1,0:T(8,128)(2,1)S(1)}, bf16[4,320,256]{2,1,0:T(8,128)(2,1)S(1)}, u32[]{:S(2)}, u32[]{:S(2)}) collective-permute-start(bf16[4,320,256]{2,1,0:T(8,128)(2,1)S(1)} %add_convert_fusion.1), channel_id=1, source_target_pairs={{0,8},{1,33},{2,10},{3,35},{4,12},{5,37},{6,14},{7,39},{8,16},{9,4... | collective-permute-start | bytes 1966088 | tf_op jit(solution)/shard_map/ppermute | solution.py:30
  109.3 13.9 %collective-permute-start.23 = (bf16[4,320,256]{2,1,0:T(8,128)(2,1)S(1)}, bf16[4,320,256]{2,1,0:T(8,128)(2,1)S(1)}, u32[]{:S(2)}, u32[]{:S(2)}) collective-permute-start(bf16[4,320,256]{2,1,0:T(8,128)(2,1)S(1)} %add_convert_fusion), channel_id=1, source_target_pairs={{0,24},{1,97},{2,26},{3,99},{4,28},{5,101},{6,30},{7,103},{8,0},{9... | collective-permute-start | bytes 1966088 | tf_op jit(solution)/shard_map/ppermute | solution.py:30
  123.5 11.0 %collective-permute-start.24 = (bf16[320,512]{1,0:T(8,128)(2,1)S(1)}, bf16[320,512]{1,0:T(8,128)(2,1)S(1)}, u32[]{:S(2)}, u32[]{:S(2)}) collective-permute-start(bf16[320,512]{1,0:T(8,128)(2,1)S(1)} %pad_maximum_fusion.2), channel_id=1, source_target_pairs={{0,32},{1,9},{2,34},{3,11},{4,36},{5,13},{6,38},{7,15},{8,40},{9,1... | collective-permute-start | bytes 983048 | tf_op jit(solution)/shard_map/ppermute | solution.py:30
  123.6 10.9 %collective-permute-start.25 = (bf16[320,512]{1,0:T(8,128)(2,1)S(1)}, bf16[320,512]{1,0:T(8,128)(2,1)S(1)}, u32[]{:S(2)}, u32[]{:S(2)}) collective-permute-start(bf16[320,512]{1,0:T(8,128)(2,1)S(1)} %pad_maximum_fusion.3), channel_id=1, source_target_pairs={{0,96},{1,25},{2,98},{3,27},{4,100},{5,29},{6,102},{7,31},{8,104},... | collective-permute-start | bytes 983048 | tf_op jit(solution)/shard_map/ppermute | solution.py:30
  126.4 8.1 %collective-permute-start.26 = (bf16[320,512]{1,0:T(8,128)(2,1)S(1)}, bf16[320,512]{1,0:T(8,128)(2,1)S(1)}, u32[]{:S(2)}, u32[]{:S(2)}) collective-permute-start(bf16[320,512]{1,0:T(8,128)(2,1)S(1)} %pad_maximum_fusion.4), channel_id=1, source_target_pairs={{0,64},{1,17},{2,66},{3,19},{4,68},{5,21},{6,70},{7,23},{8,72},{9,... | collective-permute-start | bytes 983048 | tf_op jit(solution)/shard_map/ppermute | solution.py:30

commit v6 on v5

--- a/solution.py
+++ b/solution.py
@@ -176,7 +176,7 @@
             pltpu.VMEM((TOK, DT), bf16),
             pltpu.SemaphoreType.DMA((4,)),
         ],
-        compiler_params=pltpu.CompilerParams(vmem_limit_bytes=40 * 2**20),
+        compiler_params=pltpu.CompilerParams(vmem_limit_bytes=48 * 2**20),
         cost_estimate=pl.CostEstimate(
             flops=5_000_000_000, bytes_accessed=30_000_000, transcendentals=600_000
         ),

time: 162 us -> 167 us (1.031)
  Pallas kernels: 20.8 us -> 22.7 us
    pallas_call x1, Pallas kernels: 8.24 us -> 10.1 us  [head(): pl.pallas_call(head_kernel, in_specs=[pl.BlockSpec(memory_space=pltpu.SME...]
    unnamed x20 -> x14, local copies, waits for them, and re-layouts: 7.59 us -> 6.13 us
  transfers between devices with their start and end apart: 29 -> 29, of which waited for: 13 -> 12; matrix products, arithmetic and copies ran while one was open for 5% -> 6% of each run, Pallas kernels for 8% -> 9%
where the time goes in v6:
time: 167 us; the launch traced here: 166 us
  waiting for transfers between devices  55.4 us (33%)
  starting transfers between devices  48 us (29%)
  blocking collectives  25.1 us (15%)
  Pallas kernels  22.7 us (14%)
  local copies, waits for them, and re-layouts  8.23 us (5%)
  other arithmetic  4.44 us (3%)
    ppermute x27, waiting for transfers between devices, permute(): return lax.ppermute(v, AXES, pairs)  46.3 us
    ppermute x27, starting transfers between devices, permute(): return lax.ppermute(v, AXES, pairs)  31.2 us
    all_to_all x1, blocking collectives, per_device(): lax.all_to_all(jnp.concatenate([mine[:224].reshape(16, 14, HH), mine[224:...  25.1 us
    pallas_call x1, Pallas kernels, head(): pl.pallas_call(head_kernel, in_specs=[pl.BlockSpec(memory_space=pltpu.SME...  10.1 us
    all_to_all x1, starting transfers between devices, per_device(): lax.all_to_all(fan_out(proj_in, proj_out), ('zh', 'zl', 'c'), split_axis=...  9.98 us
    all_to_all x1, waiting for transfers between devices, per_device(): lax.all_to_all(fan_out(proj_in, proj_out), ('zh', 'zl', 'c'), split_axis=...  9.07 us
    all_to_all x1, starting transfers between devices, per_device(): lax.all_to_all(sent, ('zh', 'x', 'y'), split_axis=0, concat_axis=0, tiled...  6.84 us
    unnamed x14, local copies, waits for them, and re-layouts  6.13 us
  transfers between devices with their start and end apart: 29, of which 12 were waited for; matrix products, arithmetic and copies ran while one was open for 6% of the time, Pallas kernels for 9%

profile of v6, /device:TPU:1, one launch (start us, length us, event | category | flops | bytes accessed | tf_op | source)
XLA Modules:
  0.0 166.1 jit_solution(18104568180107633836)
XLA Ops:
  0.7 1.6 fan_out.1
  2.3 10.0 %all-to-all-start = ((bf16[16,20,512]{2,1,0:T(8,128)(2,1)}), bf16[16,20,512]{2,1,0:T(8,128)(2,1)S(1)}, u32[]{:S(2)}, u32[]{:S(2)}) async-start(bf16[16,20,512]{2,1,0:T(8,128)(2,1)} %fan_out.1), calls=%async_computation | async-start | bytes 786432 | tf_op jit(solution)/shard_map/all_to_all | solution.py:312
  12.2 0.8 sign_compare_fusion
  13.1 0.1 ne.39
  13.2 0.1 dynamic-slice_remainder_fusion
  13.3 0.1 rem.24
  13.4 0.1 div.14
  13.5 2.9 %copy.13 = bf16[1,256,3584]{1,2,0:T(8,128)(2,1)S(1)} copy(bf16[1,256,3584]{2,1,0:T(8,128)(2,1)} %param.5) | data formatting | bytes 3670016 | tf_op args[0]
  16.4 1.3 fusion
  17.7 9.1 %all-to-all-done = bf16[16,20,512]{2,1,0:T(8,128)(2,1)S(1)} async-done(((bf16[16,20,512]{2,1,0:T(8,128)(2,1)}), bf16[16,20,512]{2,1,0:T(8,128)(2,1)S(1)}, u32[]{:S(2)}, u32[]{:S(2)}) %all-to-all-start) | async-done | bytes 327712 | tf_op jit(solution)/shard_map/all_to_all | solution.py:312
  27.0 0.1 reshape.120
  27.2 3.0 %collective-permute-start.3 = (bf16[320,512]{1,0:T(8,128)(2,1)S(1)}, bf16[320,512]{1,0:T(8,128)(2,1)S(1)}, u32[]{:S(2)}, u32[]{:S(2)}) collective-permute-start(bf16[320,512]{1,0:T(8,128)(2,1)S(1)} %pad_maximum_fusion.1), channel_id=1, source_target_pairs={{0,64},{1,17},{2,66},{3,19},{4,68},{5,21},{6,70},{7,23},{8,72},{9,... | collective-permute-start | bytes 983048 | tf_op jit(solution)/shard_map/ppermute | solution.py:30
  30.2 0.8 collective-permute-start.2
  30.9 0.7 collective-permute-start.1
  31.6 6.8 %all-to-all-start.1 = ((bf16[32,8,1536]{2,1,0:T(8,128)(2,1)}), bf16[32,8,1536]{2,1,0:T(8,128)(2,1)}, u32[]{:S(2)}, u32[]{:S(2)}) async-start(bf16[32,8,1536]{2,1,0:T(8,128)(2,1)} %fusion), calls=%async_computation.1 | async-start | bytes 1572864 | tf_op jit(solution)/shard_map/all_to_all | solution.py:339
  38.5 0.2 collective-permute-done.2
  38.7 2.2 %pad_maximum_fusion.refs_0_ = bf16[4,320,512]{2,1,0:T(8,128)(2,1)} fusion(bf16[1,320,512]{2,1,0:T(8,128)(2,1)S(1)} %bitcast.53, bf16[1,320,512]{2,1,0:T(8,128)(2,1)S(1)} %bitcast.54, bf16[1,320,512]{2,1,0:T(8,128)(2,1)} %bitcast.12, bf16[1,320,512]{2,1,0:T(8,128)(2,1)S(1)} %bitcast.52), kind=kLoop, calls=%fused_computation.2 | loop fusion | flops 1966080 | bytes 2621440 | tf_op jit(solution)/shard_map/stack | solution.py:343
  40.8 1.4 fusion.12
  42.2 2.5 %collective-permute-start.4 = (bf16[4,320,256]{2,1,0:T(8,128)(2,1)S(1)}, bf16[4,320,256]{2,1,0:T(8,128)(2,1)S(1)}, u32[]{:S(2)}, u32[]{:S(2)}) collective-permute-start(bf16[4,320,256]{2,1,0:T(8,128)(2,1)S(1)} %get-tuple-element.29), channel_id=1, source_target_pairs={{0,24},{1,97},{2,26},{3,99},{4,28},{5,101},{6,30},{7,103},{8,0},{9... | collective-permute-start | bytes 1966088 | tf_op jit(solution)/shard_map/ppermute | solution.py:30
  44.7 0.2 collective-permute-start.8
  44.9 2.5 %collective-permute-start.9 = (bf16[4,320,256]{2,1,0:T(8,128)(2,1)S(1)}, bf16[4,320,256]{2,1,0:T(8,128)(2,1)}, u32[]{:S(2)}, u32[]{:S(2)}) collective-permute-start(bf16[4,320,256]{2,1,0:T(8,128)(2,1)S(1)} %get-tuple-element.30), channel_id=1, source_target_pairs={{0,24},{1,97},{2,26},{3,99},{4,28},{5,101},{6,30},{7,103},{8,0},{9... | collective-permute-start | bytes 1966088 | tf_op jit(solution)/shard_map/ppermute | solution.py:30
  47.4 9.1 %collective-permute-done.4.refs_2_ = bf16[4,320,256]{2,1,0:T(8,128)(2,1)S(1)} collective-permute-done((bf16[4,320,256]{2,1,0:T(8,128)(2,1)S(1)}, bf16[4,320,256]{2,1,0:T(8,128)(2,1)S(1)}, u32[]{:S(2)}, u32[]{:S(2)}) %collective-permute-start.4) | collective-permute-done | bytes 655392 | tf_op jit(solution)/shard_map/ppermute | solution.py:30
  56.5 3.0 %collective-permute-start.5 = (bf16[4,320,256]{2,1,0:T(8,128)(2,1)S(1)}, bf16[4,320,256]{2,1,0:T(8,128)(2,1)S(1)}, u32[]{:S(2)}, u32[]{:S(2)}) collective-permute-start(bf16[4,320,256]{2,1,0:T(8,128)(2,1)S(1)} %collective-permute-done.4.refs_2_), channel_id=1, source_target_pairs={{0,24},{1,97},{2,26},{3,99},{4,28},{5,101},{6,30},{7,103},{8,0},{9... | collective-permute-start | bytes 1966088 | tf_op jit(solution)/shard_map/ppermute | solution.py:30
  59.5 6.7 %collective-permute-done.8.refs_3_ = bf16[4,320,256]{2,1,0:T(8,128)(2,1)} collective-permute-done((bf16[4,320,256]{2,1,0:T(8,128)(2,1)S(1)}, bf16[4,320,256]{2,1,0:T(8,128)(2,1)}, u32[]{:S(2)}, u32[]{:S(2)}) %collective-permute-start.8) | collective-permute-done | bytes 655392 | tf_op jit(solution)/shard_map/ppermute | solution.py:30
  66.2 2.5 %collective-permute-start.13 = (bf16[4,320,256]{2,1,0:T(8,128)(2,1)}, bf16[4,320,256]{2,1,0:T(8,128)(2,1)}, u32[]{:S(2)}, u32[]{:S(2)}) collective-permute-start(bf16[4,320,256]{2,1,0:T(8,128)(2,1)} %collective-permute-done.8.refs_3_), channel_id=1, source_target_pairs={{0,1},{1,0},{2,3},{3,2},{4,5},{5,4},{6,7},{7,6},{8,9},{9,8},{10,11... | collective-permute-start | bytes 1966088 | tf_op jit(solution)/shard_map/ppermute | solution.py:30
  68.7 0.5 collective-permute-start.12
  69.2 1.3 collective-permute-done.5.refs_6_
  70.5 0.9 copy-done.2
  71.4 2.3 %collective-permute-start.14 = (bf16[4,320,256]{2,1,0:T(8,128)(2,1)}, bf16[4,320,256]{2,1,0:T(8,128)(2,1)}, u32[]{:S(2)}, u32[]{:S(2)}) collective-permute-start(bf16[4,320,256]{2,1,0:T(8,128)(2,1)} %collective-permute-done.9.refs_4_), channel_id=1, source_target_pairs={{0,1},{1,0},{2,3},{3,2},{4,5},{5,4},{6,7},{7,6},{8,9},{9,8},{10,11... | collective-permute-start | bytes 1966088 | tf_op jit(solution)/shard_map/ppermute | solution.py:30
  73.7 2.1 %collective-permute-start.11 = (bf16[4,320,256]{2,1,0:T(8,128)(2,1)}, bf16[4,320,256]{2,1,0:T(8,128)(2,1)}, u32[]{:S(2)}, u32[]{:S(2)}) collective-permute-start(bf16[4,320,256]{2,1,0:T(8,128)(2,1)} %collective-permute-done.6.refs_1_), channel_id=1, source_target_pairs={{0,1},{1,0},{2,3},{3,2},{4,5},{5,4},{6,7},{7,6},{8,9},{9,8},{10,11... | collective-permute-start | bytes 1966088 | tf_op jit(solution)/shard_map/ppermute | solution.py:30
  75.8 0.3 collective-permute-start.15
  76.0 0.2 collective-permute-start.16
  76.3 0.3 collective-permute-start
  76.6 0.1 pad_add_fusion.place
  76.6 1.2 collective-permute-done.11.refs_8_
  77.8 1.9 %collective-permute-done.15.refs_12_ = bf16[4,320,256]{2,1,0:T(8,128)(2,1)} collective-permute-done((bf16[4,320,256]{2,1,0:T(8,128)(2,1)}, bf16[4,320,256]{2,1,0:T(8,128)(2,1)}, u32[]{:S(2)}, u32[]{:S(2)}) %collective-permute-start.15) | collective-permute-done | bytes 655392 | tf_op jit(solution)/shard_map/ppermute | solution.py:30
  79.7 1.9 %collective-permute-done.16.refs_13_ = bf16[4,320,256]{2,1,0:T(8,128)(2,1)} collective-permute-done((bf16[4,320,256]{2,1,0:T(8,128)(2,1)}, bf16[4,320,256]{2,1,0:T(8,128)(2,1)}, u32[]{:S(2)}, u32[]{:S(2)}) %collective-permute-start.16) | collective-permute-done | bytes 655392 | tf_op jit(solution)/shard_map/ppermute | solution.py:30
  81.6 1.1 copy-done.3
  82.7 10.1 %head.1 = (bf16[256,1024]{1,0:T(8,128)(2,1)S(1)}, bf16[256,2304]{1,0:T(8,128)(2,1)}, bf16[256,2304]{1,0:T(8,128)(2,1)}, bf16[16,224,1024]{2,1,0:T(8,128)(2,1)}) custom-call(s32[3]{0:T(128)S(1)} %pad_add_fusion.place, bf16[256,3584]{1,0:T(8,128)(2,1)} %bitcast.51, bf16[256,1536]{1,0:T(8,128)(2,1)} %bitcast.15.picked, ...), custom_call_target="tpu_custom_call" | custom-call | flops 5000000000 | bytes 30000000 | tf_op jit(solution)/shard_map/head/pallas_call | solution.py:161
  92.8 0.5 collective-permute-start.17
  93.2 2.7 %collective-permute-done.17.rcv = bf16[256,2304]{1,0:T(8,128)(2,1)S(1)} collective-permute-done((bf16[256,2304]{1,0:T(8,128)(2,1)}, bf16[256,2304]{1,0:T(8,128)(2,1)S(1)}, u32[]{:S(2)}, u32[]{:S(2)}) %collective-permute-start.17) | collective-permute-done | bytes 1179680 | tf_op jit(solution)/shard_map/ppermute | solution.py:30
  95.9 1.3 copy-done.4
  97.2 4.9 %tail.1 = (bf16[4,320,256]{2,1,0:T(8,128)(2,1)S(1)}, bf16[4,320,256]{2,1,0:T(8,128)(2,1)S(1)}, bf16[4,320,256]{2,1,0:T(8,128)(2,1)S(1)}, bf16[4,320,256]{2,1,0:T...) custom-call(s32[3]{0:T(128)S(1)} %pad_add_fusion.place, ...), custom_call_target="tpu_custom_call" | custom-call | flops 2700000000 | bytes 12000000 | tf_op jit(solution)/shard_map/tail/pallas_call | solution.py:221
  102.2 1.3 collective-permute-start.18
  103.5 1.4 collective-permute-start.22
  104.9 1.0 collective-permute-start.20
  105.9 0.5 collective-permute-start.21
  106.4 6.8 %collective-permute-done.18 = bf16[4,320,256]{2,1,0:T(8,128)(2,1)S(1)} collective-permute-done((bf16[4,320,256]{2,1,0:T(8,128)(2,1)S(1)}, bf16[4,320,256]{2,1,0:T(8,128)(2,1)S(1)}, u32[]{:S(2)}, u32[]{:S(2)}) %collective-permute-start.18) | collective-permute-done | bytes 655392 | tf_op jit(solution)/shard_map/ppermute | solution.py:30
  113.2 0.2 add_convert_fusion.1
  113.4 0.1 collective-permute-start.19
  113.5 0.2 add_convert_fusion
  113.6 2.7 %collective-permute-start.23 = (bf16[4,320,256]{2,1,0:T(8,128)(2,1)S(1)}, bf16[4,320,256]{2,1,0:T(8,128)(2,1)S(1)}, u32[]{:S(2)}, u32[]{:S(2)}) collective-permute-start(bf16[4,320,256]{2,1,0:T(8,128)(2,1)S(1)} %add_convert_fusion), channel_id=1, source_target_pairs={{0,24},{1,97},{2,26},{3,99},{4,28},{5,101},{6,30},{7,103},{8,0},{9... | collective-permute-start | bytes 1966088 | tf_op jit(solution)/shard_map/ppermute | solution.py:30
  116.4 4.3 %back.1 = bf16[256,3584]{1,0:T(8,128)(2,1)} custom-call(bf16[256,1024]{1,0:T(8,128)(2,1)S(1)} %get-tuple-element.39.grad_pre, bf16[16,224,1024]{2,1,0:T(8,128)(2,1)S(1)} %copy-done.1), custom_call_target="tpu_custom_call" | custom-call | flops 1900000000 | bytes 10000000 | tf_op jit(solution)/shard_map/back/pallas_call | solution.py:242
  120.7 6.5 %collective-permute-done.19 = bf16[4,320,256]{2,1,0:T(8,128)(2,1)S(1)} collective-permute-done((bf16[4,320,256]{2,1,0:T(8,128)(2,1)S(1)}, bf16[4,320,256]{2,1,0:T(8,128)(2,1)S(1)}, u32[]{:S(2)}, u32[]{:S(2)}) %collective-permute-start.19) | collective-permute-done | bytes 655392 | tf_op jit(solution)/shard_map/ppermute | solution.py:30
  127.2 0.2 fusion.1
  127.5 0.2 fusion.2
  127.8 0.1 collective-permute-start.24
  127.9 2.7 %collective-permute-start.25 = (bf16[320,512]{1,0:T(8,128)(2,1)S(1)}, bf16[320,512]{1,0:T(8,128)(2,1)S(1)}, u32[]{:S(2)}, u32[]{:S(2)}) collective-permute-start(bf16[320,512]{1,0:T(8,128)(2,1)S(1)} %pad_maximum_fusion.3), channel_id=1, source_target_pairs={{0,96},{1,25},{2,98},{3,27},{4,100},{5,29},{6,102},{7,31},{8,104},... | collective-permute-start | bytes 983048 | tf_op jit(solution)/shard_map/ppermute | solution.py:30
  130.7 0.1 collective-permute-start.26
  130.8 8.0 %collective-permute-done.24 = bf16[320,512]{1,0:T(8,128)(2,1)S(1)} collective-permute-done((bf16[320,512]{1,0:T(8,128)(2,1)S(1)}, bf16[320,512]{1,0:T(8,128)(2,1)S(1)}, u32[]{:S(2)}, u32[]{:S(2)}) %collective-permute-start.24) | collective-permute-done | bytes 327712 | tf_op jit(solution)/shard_map/ppermute | solution.py:30
  138.8 0.2 add_convert_fusion.2
  139.2 0.1 maximum_maximum_fusion
  139.3 25.1 %all_to_all.15.last = bf16[16,20,512]{2,1,0:T(8,128)(2,1)} all-to-all(bf16[16,20,512]{2,1,0:T(8,128)(2,1)S(1)} %maximum_maximum_fusion), channel_id=1, replica_groups=mesh['zh'=2,'x'=4,'y'=4,'zl'=4,'c'=2] {'zh','zl','c'}, dimensions={0} | all-to-all | bytes 655360 | tf_op jit(solution)/shard_map/all_to_all | solution.py:376
  164.5 1.7 %fan_in.1 = (f32[14,1024]{1,0:T(8,128)}, f32[4,1536]{1,0:T(4,128)}) custom-call(bf16[16,20,512]{2,1,0:T(8,128)(2,1)} %all_to_all.15.last), custom_call_target="tpu_custom_call" | custom-call | tf_op jit(solution)/shard_map/fan_in/pallas_call | solution.py:298
  (50 shorter events, 0.6 us)
Async XLA Ops:
  0.6 15.8 %copy-start = (bf16[1,48,3,1536]{3,1,2,0:T(8,128)(2,1)S(1)}, bf16[1,48,3,1536]{3,1,2,0:T(8,128)(2,1)}, u32[]{:S(2)}) copy-start(bf16[1,48,3,1536]{3,1,2,0:T(8,128)(2,1)} %param.6) | copy-start | bytes 1327108
  0.6 12.5 %copy-start.5 = (s32[1,64,128]{2,1,0:T(8,128)S(1)}, s32[1,64,128]{2,1,0:T(8,128)}, u32[]{:S(2)}) copy-start(s32[1,64,128]{2,1,0:T(8,128)} %param.7) | copy-start | bytes 98308
  2.3 24.5 %all-to-all-start = ((bf16[16,20,512]{2,1,0:T(8,128)(2,1)}), bf16[16,20,512]{2,1,0:T(8,128)(2,1)S(1)}, u32[]{:S(2)}, u32[]{:S(2)}) async-start(bf16[16,20,512]{2,1,0:T(8,128)(2,1)} %fan_out.1), calls=%async_computation | async-start | bytes 786432 | tf_op jit(solution)/shard_map/all_to_all | solution.py:312
  27.2 11.3 %collective-permute-start.3 = (bf16[320,512]{1,0:T(8,128)(2,1)S(1)}, bf16[320,512]{1,0:T(8,128)(2,1)S(1)}, u32[]{:S(2)}, u32[]{:S(2)}) collective-permute-start(bf16[320,512]{1,0:T(8,128)(2,1)S(1)} %pad_maximum_fusion.1), channel_id=1, source_target_pairs={{0,64},{1,17},{2,66},{3,19},{4,68},{5,21},{6,70},{7,23},{8,72},{9,... | collective-permute-start | bytes 983048 | tf_op jit(solution)/shard_map/ppermute | solution.py:30
  30.2 8.5 %collective-permute-start.2 = (bf16[320,512]{1,0:T(8,128)(2,1)S(1)}, bf16[320,512]{1,0:T(8,128)(2,1)S(1)}, u32[]{:S(2)}, u32[]{:S(2)}) collective-permute-start(bf16[320,512]{1,0:T(8,128)(2,1)S(1)} %pad_maximum_fusion.1), channel_id=1, source_target_pairs={{0,96},{1,25},{2,98},{3,27},{4,100},{5,29},{6,102},{7,31},{8,104},... | collective-permute-start | bytes 983048 | tf_op jit(solution)/shard_map/ppermute | solution.py:30
  30.9 7.7 %collective-permute-start.1 = (bf16[320,512]{1,0:T(8,128)(2,1)S(1)}, bf16[320,512]{1,0:T(8,128)(2,1)}, u32[]{:S(2)}, u32[]{:S(2)}) collective-permute-start(bf16[320,512]{1,0:T(8,128)(2,1)S(1)} %pad_maximum_fusion.1), channel_id=1, source_target_pairs={{0,32},{1,9},{2,34},{3,11},{4,36},{5,13},{6,38},{7,15},{8,40},{9,1... | collective-permute-start | bytes 983048 | tf_op jit(solution)/shard_map/ppermute | solution.py:30
  31.6 44.1 %all-to-all-start.1 = ((bf16[32,8,1536]{2,1,0:T(8,128)(2,1)}), bf16[32,8,1536]{2,1,0:T(8,128)(2,1)}, u32[]{:S(2)}, u32[]{:S(2)}) async-start(bf16[32,8,1536]{2,1,0:T(8,128)(2,1)} %fusion), calls=%async_computation.1 | async-start | bytes 1572864 | tf_op jit(solution)/shard_map/all_to_all | solution.py:339
  42.2 14.3 %collective-permute-start.4 = (bf16[4,320,256]{2,1,0:T(8,128)(2,1)S(1)}, bf16[4,320,256]{2,1,0:T(8,128)(2,1)S(1)}, u32[]{:S(2)}, u32[]{:S(2)}) collective-permute-start(bf16[4,320,256]{2,1,0:T(8,128)(2,1)S(1)} %get-tuple-element.29), channel_id=1, source_target_pairs={{0,24},{1,97},{2,26},{3,99},{4,28},{5,101},{6,30},{7,103},{8,0},{9... | collective-permute-start | bytes 1966088 | tf_op jit(solution)/shard_map/ppermute | solution.py:30
  44.7 14.8 %collective-permute-start.6 = (bf16[4,320,256]{2,1,0:T(8,128)(2,1)S(1)}, bf16[4,320,256]{2,1,0:T(8,128)(2,1)}, u32[]{:S(2)}, u32[]{:S(2)}) collective-permute-start(bf16[4,320,256]{2,1,0:T(8,128)(2,1)S(1)} %get-tuple-element.30), channel_id=1, source_target_pairs={{0,8},{1,33},{2,10},{3,35},{4,12},{5,37},{6,14},{7,39},{8,16},{9,4... | collective-permute-start | bytes 1966088 | tf_op jit(solution)/shard_map/ppermute | solution.py:30
  44.7 21.5 %collective-permute-start.8 = (bf16[4,320,256]{2,1,0:T(8,128)(2,1)S(1)}, bf16[4,320,256]{2,1,0:T(8,128)(2,1)}, u32[]{:S(2)}, u32[]{:S(2)}) collective-permute-start(bf16[4,320,256]{2,1,0:T(8,128)(2,1)S(1)} %get-tuple-element.29), channel_id=1, source_target_pairs={{0,8},{1,33},{2,10},{3,35},{4,12},{5,37},{6,14},{7,39},{8,16},{9,4... | collective-permute-start | bytes 1966088 | tf_op jit(solution)/shard_map/ppermute | solution.py:30
  44.9 23.8 %collective-permute-start.9 = (bf16[4,320,256]{2,1,0:T(8,128)(2,1)S(1)}, bf16[4,320,256]{2,1,0:T(8,128)(2,1)}, u32[]{:S(2)}, u32[]{:S(2)}) collective-permute-start(bf16[4,320,256]{2,1,0:T(8,128)(2,1)S(1)} %get-tuple-element.30), channel_id=1, source_target_pairs={{0,24},{1,97},{2,26},{3,99},{4,28},{5,101},{6,30},{7,103},{8,0},{9... | collective-permute-start | bytes 1966088 | tf_op jit(solution)/shard_map/ppermute | solution.py:30
  56.5 14.0 %collective-permute-start.5 = (bf16[4,320,256]{2,1,0:T(8,128)(2,1)S(1)}, bf16[4,320,256]{2,1,0:T(8,128)(2,1)S(1)}, u32[]{:S(2)}, u32[]{:S(2)}) collective-permute-start(bf16[4,320,256]{2,1,0:T(8,128)(2,1)S(1)} %collective-permute-done.4.refs_2_), channel_id=1, source_target_pairs={{0,24},{1,97},{2,26},{3,99},{4,28},{5,101},{6,30},{7,103},{8,0},{9... | collective-permute-start | bytes 1966088 | tf_op jit(solution)/shard_map/ppermute | solution.py:30
  59.5 14.2 %collective-permute-start.7 = (bf16[4,320,256]{2,1,0:T(8,128)(2,1)}, bf16[4,320,256]{2,1,0:T(8,128)(2,1)}, u32[]{:S(2)}, u32[]{:S(2)}) collective-permute-start(bf16[4,320,256]{2,1,0:T(8,128)(2,1)} %collective-permute-done.6.refs_1_), channel_id=1, source_target_pairs={{0,8},{1,33},{2,10},{3,35},{4,12},{5,37},{6,14},{7,39},{8,16},{9,4... | collective-permute-start | bytes 1966088 | tf_op jit(solution)/shard_map/ppermute | solution.py:30
  66.2 9.6 %collective-permute-start.13 = (bf16[4,320,256]{2,1,0:T(8,128)(2,1)}, bf16[4,320,256]{2,1,0:T(8,128)(2,1)}, u32[]{:S(2)}, u32[]{:S(2)}) collective-permute-start(bf16[4,320,256]{2,1,0:T(8,128)(2,1)} %collective-permute-done.8.refs_3_), channel_id=1, source_target_pairs={{0,1},{1,0},{2,3},{3,2},{4,5},{5,4},{6,7},{7,6},{8,9},{9,8},{10,11... | collective-permute-start | bytes 1966088 | tf_op jit(solution)/shard_map/ppermute | solution.py:30
  68.7 9.1 %collective-permute-start.10 = (bf16[4,320,512]{2,1,0:T(8,128)(2,1)}, bf16[4,320,512]{2,1,0:T(8,128)(2,1)}, u32[]{:S(2)}, u32[]{:S(2)}) collective-permute-start(bf16[4,320,512]{2,1,0:T(8,128)(2,1)} %pad_maximum_fusion.refs_0_), channel_id=1, source_target_pairs={{0,1},{1,0},{2,3},{3,2},{4,5},{5,4},{6,7},{7,6},{8,9},{9,8},{10,11... | collective-permute-start | bytes 3932168 | tf_op jit(solution)/shard_map/ppermute | solution.py:30
  68.7 7.3 %collective-permute-start.12 = (bf16[4,320,256]{2,1,0:T(8,128)(2,1)S(1)}, bf16[4,320,256]{2,1,0:T(8,128)(2,1)}, u32[]{:S(2)}, u32[]{:S(2)}) collective-permute-start(bf16[4,320,256]{2,1,0:T(8,128)(2,1)S(1)} %collective-permute-done.4.refs_2_), channel_id=1, source_target_pairs={{0,1},{1,0},{2,3},{3,2},{4,5},{5,4},{6,7},{7,6},{8,9},{9,8},{10,11... | collective-permute-start | bytes 1966088 | tf_op jit(solution)/shard_map/ppermute | solution.py:30
  70.5 0.9 copy-start.2
  71.4 4.9 %collective-permute-start.14 = (bf16[4,320,256]{2,1,0:T(8,128)(2,1)}, bf16[4,320,256]{2,1,0:T(8,128)(2,1)}, u32[]{:S(2)}, u32[]{:S(2)}) collective-permute-start(bf16[4,320,256]{2,1,0:T(8,128)(2,1)} %collective-permute-done.9.refs_4_), channel_id=1, source_target_pairs={{0,1},{1,0},{2,3},{3,2},{4,5},{5,4},{6,7},{7,6},{8,9},{9,8},{10,11... | collective-permute-start | bytes 1966088 | tf_op jit(solution)/shard_map/ppermute | solution.py:30
  73.7 4.2 %collective-permute-start.11 = (bf16[4,320,256]{2,1,0:T(8,128)(2,1)}, bf16[4,320,256]{2,1,0:T(8,128)(2,1)}, u32[]{:S(2)}, u32[]{:S(2)}) collective-permute-start(bf16[4,320,256]{2,1,0:T(8,128)(2,1)} %collective-permute-done.6.refs_1_), channel_id=1, source_target_pairs={{0,1},{1,0},{2,3},{3,2},{4,5},{5,4},{6,7},{7,6},{8,9},{9,8},{10,11... | collective-permute-start | bytes 1966088 | tf_op jit(solution)/shard_map/ppermute | solution.py:30
  75.8 3.9 %collective-permute-start.15 = (bf16[4,320,256]{2,1,0:T(8,128)(2,1)}, bf16[4,320,256]{2,1,0:T(8,128)(2,1)}, u32[]{:S(2)}, u32[]{:S(2)}) collective-permute-start(bf16[4,320,256]{2,1,0:T(8,128)(2,1)} %collective-permute-done.7.refs_5_), channel_id=1, source_target_pairs={{0,1},{1,0},{2,3},{3,2},{4,5},{5,4},{6,7},{7,6},{8,9},{9,8},{10,11... | collective-permute-start | bytes 1966088 | tf_op jit(solution)/shard_map/ppermute | solution.py:30
  76.0 5.5 %collective-permute-start.16 = (bf16[4,320,256]{2,1,0:T(8,128)(2,1)}, bf16[4,320,256]{2,1,0:T(8,128)(2,1)}, u32[]{:S(2)}, u32[]{:S(2)}) collective-permute-start(bf16[4,320,256]{2,1,0:T(8,128)(2,1)} %copy-done.2), channel_id=1, source_target_pairs={{0,1},{1,0},{2,3},{3,2},{4,5},{5,4},{6,7},{7,6},{8,9},{9,8},{10,11... | collective-permute-start | bytes 1966088 | tf_op jit(solution)/shard_map/ppermute | solution.py:30
  76.3 17.0 %collective-permute-start = (bf16[3584,256]{1,0:T(8,128)(2,1)S(1)}, bf16[3584,256]{1,0:T(8,128)(2,1)}, u32[]{:S(2)}, u32[]{:S(2)}) collective-permute-start(bf16[3584,256]{1,0:T(8,128)(2,1)S(1)} %bitcast.48), channel_id=1, source_target_pairs={{0,1},{1,0},{2,3},{3,2},{4,5},{5,4},{6,7},{7,6},{8,9},{9,8},{10,11... | collective-permute-start | bytes 5505032 | tf_op jit(solution)/shard_map/ppermute | solution.py:30
  81.6 1.1 copy-start.3
  92.8 3.1 %collective-permute-start.17 = (bf16[256,2304]{1,0:T(8,128)(2,1)}, bf16[256,2304]{1,0:T(8,128)(2,1)S(1)}, u32[]{:S(2)}, u32[]{:S(2)}) collective-permute-start(bf16[256,2304]{1,0:T(8,128)(2,1)} %get-tuple-element.36), channel_id=1, source_target_pairs={{0,1},{1,0},{2,3},{3,2},{4,5},{5,4},{6,7},{7,6},{8,9},{9,8},{10,11... | collective-permute-start | bytes 3538952 | tf_op jit(solution)/shard_map/ppermute | solution.py:30
  95.9 1.3 copy-start.4
  97.2 19.1 %copy-start.1 = (bf16[16,224,1024]{2,1,0:T(8,128)(2,1)S(1)}, bf16[16,224,1024]{2,1,0:T(8,128)(2,1)}, u32[]{:S(2)}) copy-start(bf16[16,224,1024]{2,1,0:T(8,128)(2,1)} %get-tuple-element.40.w_in) | copy-start | bytes 22020100
  102.2 11.0 %collective-permute-start.18 = (bf16[4,320,256]{2,1,0:T(8,128)(2,1)S(1)}, bf16[4,320,256]{2,1,0:T(8,128)(2,1)S(1)}, u32[]{:S(2)}, u32[]{:S(2)}) collective-permute-start(bf16[4,320,256]{2,1,0:T(8,128)(2,1)S(1)} %get-tuple-element.38), channel_id=1, source_target_pairs={{0,8},{1,33},{2,10},{3,35},{4,12},{5,37},{6,14},{7,39},{8,16},{9,4... | collective-permute-start | bytes 1966088 | tf_op jit(solution)/shard_map/ppermute | solution.py:30
  103.5 10.0 %collective-permute-start.22 = (bf16[4,320,256]{2,1,0:T(8,128)(2,1)S(1)}, bf16[4,320,256]{2,1,0:T(8,128)(2,1)S(1)}, u32[]{:S(2)}, u32[]{:S(2)}) collective-permute-start(bf16[4,320,256]{2,1,0:T(8,128)(2,1)S(1)} %get-tuple-element.48), channel_id=1, source_target_pairs={{0,24},{1,97},{2,26},{3,99},{4,28},{5,101},{6,30},{7,103},{8,0},{9... | collective-permute-start | bytes 1966088 | tf_op jit(solution)/shard_map/ppermute | solution.py:30
  104.9 22.3 %collective-permute-start.20 = (bf16[4,320,256]{2,1,0:T(8,128)(2,1)S(1)}, bf16[4,320,256]{2,1,0:T(8,128)(2,1)S(1)}, u32[]{:S(2)}, u32[]{:S(2)}) collective-permute-start(bf16[4,320,256]{2,1,0:T(8,128)(2,1)S(1)} %get-tuple-element.44), channel_id=1, source_target_pairs={{0,24},{1,97},{2,26},{3,99},{4,28},{5,101},{6,30},{7,103},{8,0},{9... | collective-permute-start | bytes 1966088 | tf_op jit(solution)/shard_map/ppermute | solution.py:30
  105.9 21.5 %collective-permute-start.21 = (bf16[4,320,256]{2,1,0:T(8,128)(2,1)S(1)}, bf16[4,320,256]{2,1,0:T(8,128)(2,1)S(1)}, u32[]{:S(2)}, u32[]{:S(2)}) collective-permute-start(bf16[4,320,256]{2,1,0:T(8,128)(2,1)S(1)} %get-tuple-element.46), channel_id=1, source_target_pairs={{0,8},{1,33},{2,10},{3,35},{4,12},{5,37},{6,14},{7,39},{8,16},{9,4... | collective-permute-start | bytes 1966088 | tf_op jit(solution)/shard_map/ppermute | solution.py:30
  113.4 13.9 %collective-permute-start.19 = (bf16[4,320,256]{2,1,0:T(8,128)(2,1)S(1)}, bf16[4,320,256]{2,1,0:T(8,128)(2,1)S(1)}, u32[]{:S(2)}, u32[]{:S(2)}) collective-permute-start(bf16[4,320,256]{2,1,0:T(8,128)(2,1)S(1)} %add_convert_fusion.1), channel_id=1, source_target_pairs={{0,8},{1,33},{2,10},{3,35},{4,12},{5,37},{6,14},{7,39},{8,16},{9,4... | collective-permute-start | bytes 1966088 | tf_op jit(solution)/shard_map/ppermute | solution.py:30
  113.6 13.9 %collective-permute-start.23 = (bf16[4,320,256]{2,1,0:T(8,128)(2,1)S(1)}, bf16[4,320,256]{2,1,0:T(8,128)(2,1)S(1)}, u32[]{:S(2)}, u32[]{:S(2)}) collective-permute-start(bf16[4,320,256]{2,1,0:T(8,128)(2,1)S(1)} %add_convert_fusion), channel_id=1, source_target_pairs={{0,24},{1,97},{2,26},{3,99},{4,28},{5,101},{6,30},{7,103},{8,0},{9... | collective-permute-start | bytes 1966088 | tf_op jit(solution)/shard_map/ppermute | solution.py:30
  127.8 11.0 %collective-permute-start.24 = (bf16[320,512]{1,0:T(8,128)(2,1)S(1)}, bf16[320,512]{1,0:T(8,128)(2,1)S(1)}, u32[]{:S(2)}, u32[]{:S(2)}) collective-permute-start(bf16[320,512]{1,0:T(8,128)(2,1)S(1)} %pad_maximum_fusion.2), channel_id=1, source_target_pairs={{0,32},{1,9},{2,34},{3,11},{4,36},{5,13},{6,38},{7,15},{8,40},{9,1... | collective-permute-start | bytes 983048 | tf_op jit(solution)/shard_map/ppermute | solution.py:30
  127.9 10.9 %collective-permute-start.25 = (bf16[320,512]{1,0:T(8,128)(2,1)S(1)}, bf16[320,512]{1,0:T(8,128)(2,1)S(1)}, u32[]{:S(2)}, u32[]{:S(2)}) collective-permute-start(bf16[320,512]{1,0:T(8,128)(2,1)S(1)} %pad_maximum_fusion.3), channel_id=1, source_target_pairs={{0,96},{1,25},{2,98},{3,27},{4,100},{5,29},{6,102},{7,31},{8,104},... | collective-permute-start | bytes 983048 | tf_op jit(solution)/shard_map/ppermute | solution.py:30
  130.7 8.1 %collective-permute-start.26 = (bf16[320,512]{1,0:T(8,128)(2,1)S(1)}, bf16[320,512]{1,0:T(8,128)(2,1)S(1)}, u32[]{:S(2)}, u32[]{:S(2)}) collective-permute-start(bf16[320,512]{1,0:T(8,128)(2,1)S(1)} %pad_maximum_fusion.4), channel_id=1, source_target_pairs={{0,64},{1,17},{2,66},{3,19},{4,68},{5,21},{6,70},{7,23},{8,72},{9,... | collective-permute-start | bytes 983048 | tf_op jit(solution)/shard_map/ppermute | solution.py:30
